TPU v7x, 32 devices: a whole 2x2x4 slice. The times are simulated.
32 devices in a mesh: slab: 8 (over z, y), rock: 4 (over x, core).
Axes of the slice: x: 2, y: 2, z: 4, core: 2. Of those that a mesh axis runs over, the one named last changes fastest.
Arguments:
- strain: float32 [1024, 6, 2048], P('slab', None, 'rock'), may hold values from -6 to 6
- dest: int32 [2, 1024, 1], P(None, 'slab'), may hold values from 0 to 7; in each aligned block of 128 rows (0 to 127, 128 to 255, ..., all dimensions but the last counted through in order) at most 32 rows name the same one
- det_row: int32 [2, 1024], P(None, 'slab'), may hold values from 0 to 7
- dirs: float32 [2, 4, 6], replicated, may hold values from -2.5 to 2.5
- rock_angles: float32 [16], replicated, may hold values from -2 to 2
- resolution: bfloat16 [2048, 2048], P(None, 'rock'), may hold values from -0.125 to 0.125
Outputs:
- detector: float32 [2, 64, 16, 2048], P(None, 'slab', None, 'rock')
Inputs may be any that keep to these rules, and one draw needn't show every extreme that they name: `dest`: within the 128 tiles of one index of slab, at one angle, at most 32 tiles name the same owner, a bound that some block reaches.
All inputs are finite; a program needn't handle non-finite values.
Results may differ from a plain program's by a relative error of at most 0.0003.
Values sent between devices are 32-bit elements; how exact they have to be, the bound alone decides.
No kernel may reach another device: no remote copies, remote signals or barrier semaphores. Data moves between devices by JAX's collectives and lax.ppermute only.
A program may use at most 128 MiB of HBM per device.

v0:
```python
import jax
import jax.numpy as jnp
from jax import lax
from jax.sharding import PartitionSpec as P

TILES_DEV = 128
DEPTH = 1
QDIR = 4
ROWS = 8
ANGLES = 2


def local(strain, dest, det_row, dirs, rock_angles, resolution):
    slabs = lax.axis_size("slab")
    tiles_here = strain.shape[0]
    vox_here = strain.shape[2]
    pix_here = resolution.shape[1]
    depth = vox_here // pix_here
    capacity = 2 * tiles_here // slabs
    slots = slabs * capacity
    block_size = 64
    rocks = rock_angles.shape[0]
    qcount = dirs.shape[1]
    norm = ROWS / (QDIR * DEPTH * TILES_DEV)
    row_ids = jnp.arange(ROWS, dtype=jnp.float32)
    lower = lax.broadcasted_iota(jnp.int32, (tiles_here, tiles_here), 1) < lax.broadcasted_iota(
        jnp.int32, (tiles_here, tiles_here), 0
    )

    def add_block(total, item):
        proj_block, row_block = item
        inten = jnp.sum(
            jnp.exp(-0.5 * (proj_block[:, :, None, :] - rock_angles[None, None, :, None]) ** 2),
            axis=1,
        )
        summed = inten.reshape(block_size, rocks, pix_here, depth).sum(axis=3)
        onehot = (row_ids[:, None] == row_block[None, :]).astype(jnp.float32)
        added = jnp.dot(
            onehot, summed.reshape(block_size, rocks * pix_here), precision=lax.Precision.HIGHEST
        )
        return (total + added, None)

    images = []
    for angle in range(ANGLES):
        owner = dest[angle, :, 0]
        same = (owner[:, None] == owner[None, :]) & lower
        rank = jnp.sum(same.astype(jnp.int32), axis=1)
        slot = owner * capacity + rank
        row_send = (
            jnp.full((slots,), -1.0, jnp.float32).at[slot].set(det_row[angle].astype(jnp.float32))
        )
        row_send = row_send.reshape(slabs, capacity)
        weights = dirs[angle]
        local_proj = jnp.einsum("qc,tcv->tqv", weights, strain, precision=lax.Precision.HIGHEST)
        outgoing = jnp.zeros((slots, qcount, vox_here), jnp.float32).at[slot].set(local_proj)
        outgoing = outgoing.reshape(slabs, capacity, qcount, vox_here)
        arrived, arrived_rows = (
            lax.all_to_all(outgoing, "slab", split_axis=0, concat_axis=0, tiled=True),
            lax.all_to_all(row_send, "slab", split_axis=0, concat_axis=0, tiled=True),
        )
        proj = arrived.reshape(slots, qcount, vox_here)
        proj_blocks = proj.reshape(slots // block_size, block_size, qcount, vox_here)
        row_blocks = arrived_rows.reshape(slots // block_size, block_size)
        image, unused = lax.scan(
            add_block, jnp.zeros((ROWS, rocks * pix_here), jnp.float32), (proj_blocks, row_blocks)
        )
        images.append(image.reshape(ROWS, rocks, pix_here) * norm)
    stacked = jnp.stack(images, axis=0)
    columns = resolution.astype(jnp.float32)
    return jnp.einsum(
        "agrp,pk->agrk",
        lax.all_gather(stacked, "rock", axis=3, tiled=True),
        columns,
        precision=lax.Precision.HIGHEST,
    )


def solution(mesh):
    placed = (
        P("slab", None, "rock"),
        P(None, "slab", None),
        P(None, "slab"),
        P(),
        P(),
        P(None, "rock"),
    )
    return jax.shard_map(
        local, mesh=mesh, in_specs=placed, out_specs=P(None, "slab", None, "rock"), check_vma=False
    )
```

profile of v0, /device:TPU:0, one launch (start us, length us, event | category | flops | bytes accessed | tf_op | source)
XLA Modules:
  0.0 218.6 jit_solution(8878018171080427440)
XLA Ops:
  10.6 7.3 %all-to-all-start = ((f32[8,1,32]{2,1,0:T(1,128)}), f32[8,1,32]{2,1,0:T(1,128)S(1)}, u32[]{:S(2)}, u32[]{:S(2)}) async-start(f32[8,1,32]{2,1,0:T(1,128)} %all_to_all.18), calls=%async_computation | async-start | bytes 8192 | tf_op jit(solution)/shard_map/all_to_all | solution.py:59
  19.6 4.8 %all-to-all-done = f32[8,1,32]{2,1,0:T(1,128)S(1)} async-done(((f32[8,1,32]{2,1,0:T(1,128)}), f32[8,1,32]{2,1,0:T(1,128)S(1)}, u32[]{:S(2)}, u32[]{:S(2)}) %all-to-all-start) | async-done | bytes 1056 | tf_op jit(solution)/shard_map/all_to_all | solution.py:59
  24.4 3.3 %all-to-all-start.2 = ((f32[8,1,32]{2,1,0:T(1,128)}), f32[8,1,32]{2,1,0:T(1,128)S(1)}, u32[]{:S(2)}, u32[]{:S(2)}) async-start(f32[8,1,32]{2,1,0:T(1,128)} %all_to_all.21), calls=%async_computation.2 | async-start | bytes 8192 | tf_op jit(solution)/shard_map/all_to_all | solution.py:59
  27.7 4.2 %fusion.12 = f32[128,4,512]{2,1,0:T(4,128)S(1)} fusion(f32[128,6,512]{2,0,1:T(8,128)} %param.10, f32[2,4,6]{2,1,0:T(4,128)} %param.13), kind=kOutput, calls=%fused_computation.24 | convolution fusion | flops 18874368 | bytes 2623488 | tf_op jit(solution)/shard_map/qc,tcv->tqv/dot_general | solution.py:54
  33.5 13.7 %scatter_fusion = f32[256,4,512]{2,1,0:T(4,128)} fusion(f32[256,4,512]{2,1,0:T(4,128)} %broadcast.98.clone.1, s32[128]{0:T(128)S(1)} %get-tuple-element.133, f32[128,4,512]{2,1,0:T(4,128)S(1)} %fusion.12), kind=kCustom, calls=%fused_computation.1 | custom fusion | bytes 3146240 | tf_op jit(solution)/shard_map/scatter | solution.py:55
  47.2 6.1 %all-to-all-start.1 = ((f32[8,32,4,512]{3,2,1,0:T(4,128)}), f32[8,32,4,512]{3,2,1,0:T(4,128)}, u32[]{:S(2)}, u32[]{:S(2)}) async-start(f32[8,32,4,512]{3,2,1,0:T(4,128)} %bitcast.91), calls=%async_computation.1 | async-start | bytes 4194304 | tf_op jit(solution)/shard_map/all_to_all | solution.py:58
  53.3 4.2 %fusion.15 = f32[128,4,512]{2,1,0:T(4,128)S(1)} fusion(f32[128,6,512]{2,0,1:T(8,128)} %param.10, f32[2,4,6]{2,1,0:T(4,128)S(1)} %copy-done.2), kind=kOutput, calls=%fused_computation.25 | convolution fusion | flops 18874368 | bytes 2623488 | tf_op jit(solution)/shard_map/qc,tcv->tqv/dot_general | solution.py:54
  59.1 13.7 %scatter_fusion.1 = f32[256,4,512]{2,1,0:T(4,128)} fusion(f32[256,4,512]{2,1,0:T(4,128)} %broadcast.98.clone, s32[128]{0:T(128)S(1)} %get-tuple-element.134, f32[128,4,512]{2,1,0:T(4,128)S(1)} %fusion.15), kind=kCustom, calls=%fused_computation.3 | custom fusion | bytes 3146240 | tf_op jit(solution)/shard_map/scatter | solution.py:55
  74.6 25.4 %all-to-all-done.1 = f32[8,32,4,512]{3,2,1,0:T(4,128)} async-done(((f32[8,32,4,512]{3,2,1,0:T(4,128)}), f32[8,32,4,512]{3,2,1,0:T(4,128)}, u32[]{:S(2)}, u32[]{:S(2)}) %all-to-all-start.1) | async-done | bytes 2097184 | tf_op jit(solution)/shard_map/all_to_all | solution.py:58
  100.1 4.5 %all-to-all-start.3 = ((f32[8,32,4,512]{3,2,1,0:T(4,128)}), f32[8,32,4,512]{3,2,1,0:T(4,128)}, u32[]{:S(2)}, u32[]{:S(2)}) async-start(f32[8,32,4,512]{3,2,1,0:T(4,128)} %bitcast.90), calls=%async_computation.3 | async-start | bytes 4194304 | tf_op jit(solution)/shard_map/all_to_all | solution.py:58
  104.8 32.8 %while.22 = (s32[]{:T(128)}, f32[8,8192]{1,0:T(8,128)S(1)}, f32[4,64]{1,0:T(4,128)S(1)}, f32[4,64,4,512]{3,2,1,0:T(4,128)}, f32[16]{0:T(128)S(1)}, /*index=5*/s32[]{:T(128)}, s32[]{:T(128)}) while((s32[]{:T(128)}, f32[8,8192]{1,0:T(8,128)S(1)}, f32[4,64]{1,0:T(4,128)S(1)}, f32[4,64,4,512]{3,2,1,0:T(4,128)}, f32[16]{0:T(128)S(1)}, ...), condition=%wide.region_5.6_spmd.clone, body=%wide.region_3.5_spmd.clone.sunk | while | flops 58327552 | bytes 10486687 | solution.py:64
  105.9 2.2 exponential_reduce_fusion.4
  108.1 2.5 %copy.32 = f32[8,8,16,512]{3,1,2,0:T(8,128)} copy(f32[8,8,16,512]{3,2,1,0:T(8,128)S(1)} %bitcast.94) | data formatting | bytes 4194304 | tf_op jit(solution)/shard_map/while
  110.6 2.4 %convolution_add_fusion.4 = f32[8,8192]{1,0:T(8,128)S(1)} fusion(f32[64,8192]{1,0:T(8,128)} %bitcast.92, f32[8,8192]{1,0:T(8,128)S(1)} %get-tuple-element.230, pred[]{:T(512)S(6)} %compare.6, f32[64]{0:T(128)S(1)} %dynamic-slice_bitcast_fusion.9), kind=kOutput, calls=%fused_computation.6.clone.1 | convolution fusion | flops 50463232 | bytes 2621697 | tf_op jit(solution)/shard_map/while/body/eval_jaxpr/dot_general | solution.py:38
  116.3 2.5 %copy.32 = f32[8,8,16,512]{3,1,2,0:T(8,128)} copy(f32[8,8,16,512]{3,2,1,0:T(8,128)S(1)} %bitcast.94) | data formatting | bytes 4194304 | tf_op jit(solution)/shard_map/while
  118.8 2.4 %convolution_add_fusion.4 = f32[8,8192]{1,0:T(8,128)S(1)} fusion(f32[64,8192]{1,0:T(8,128)} %bitcast.92, f32[8,8192]{1,0:T(8,128)S(1)} %get-tuple-element.230, pred[]{:T(512)S(6)} %compare.6, f32[64]{0:T(128)S(1)} %dynamic-slice_bitcast_fusion.9), kind=kOutput, calls=%fused_computation.6.clone.1 | convolution fusion | flops 50463232 | bytes 2621697 | tf_op jit(solution)/shard_map/while/body/eval_jaxpr/dot_general | solution.py:38
  124.5 2.5 %copy.32 = f32[8,8,16,512]{3,1,2,0:T(8,128)} copy(f32[8,8,16,512]{3,2,1,0:T(8,128)S(1)} %bitcast.94) | data formatting | bytes 4194304 | tf_op jit(solution)/shard_map/while
  127.0 2.4 %convolution_add_fusion.4 = f32[8,8192]{1,0:T(8,128)S(1)} fusion(f32[64,8192]{1,0:T(8,128)} %bitcast.92, f32[8,8192]{1,0:T(8,128)S(1)} %get-tuple-element.230, pred[]{:T(512)S(6)} %compare.6, f32[64]{0:T(128)S(1)} %dynamic-slice_bitcast_fusion.9), kind=kOutput, calls=%fused_computation.6.clone.1 | convolution fusion | flops 50463232 | bytes 2621697 | tf_op jit(solution)/shard_map/while/body/eval_jaxpr/dot_general | solution.py:38
  132.7 2.5 %copy.32 = f32[8,8,16,512]{3,1,2,0:T(8,128)} copy(f32[8,8,16,512]{3,2,1,0:T(8,128)S(1)} %bitcast.94) | data formatting | bytes 4194304 | tf_op jit(solution)/shard_map/while
  135.2 2.4 %convolution_add_fusion.4 = f32[8,8192]{1,0:T(8,128)S(1)} fusion(f32[64,8192]{1,0:T(8,128)} %bitcast.92, f32[8,8192]{1,0:T(8,128)S(1)} %get-tuple-element.230, pred[]{:T(512)S(6)} %compare.6, f32[64]{0:T(128)S(1)} %dynamic-slice_bitcast_fusion.9), kind=kOutput, calls=%fused_computation.6.clone.1 | convolution fusion | flops 50463232 | bytes 2621697 | tf_op jit(solution)/shard_map/while/body/eval_jaxpr/dot_general | solution.py:38
  137.8 14.4 %all-to-all-done.3 = f32[8,32,4,512]{3,2,1,0:T(4,128)} async-done(((f32[8,32,4,512]{3,2,1,0:T(4,128)}), f32[8,32,4,512]{3,2,1,0:T(4,128)}, u32[]{:S(2)}, u32[]{:S(2)}) %all-to-all-start.3) | async-done | bytes 2097184 | tf_op jit(solution)/shard_map/all_to_all | solution.py:58
  152.2 32.6 %while.23 = (s32[]{:T(128)}, f32[8,8192]{1,0:T(8,128)S(1)}, f32[4,64]{1,0:T(4,128)S(1)}, f32[4,64,4,512]{3,2,1,0:T(4,128)}, f32[16]{0:T(128)S(1)}, /*index=5*/s32[]{:T(128)}, s32[]{:T(128)}) while((s32[]{:T(128)}, f32[8,8192]{1,0:T(8,128)S(1)}, f32[4,64]{1,0:T(4,128)S(1)}, f32[4,64,4,512]{3,2,1,0:T(4,128)}, f32[16]{0:T(128)S(1)}, ...), condition=%wide.region_11.12_spmd.clone, body=%wide.region_9.11_spmd.clone.sunk | while | flops 58327552 | bytes 10486687 | solution.py:64
  155.4 2.5 %copy.33 = f32[8,8,16,512]{3,1,2,0:T(8,128)} copy(f32[8,8,16,512]{3,2,1,0:T(8,128)S(1)} %bitcast.95) | data formatting | bytes 4194304 | tf_op jit(solution)/shard_map/while
  157.9 2.4 %convolution_add_fusion.5 = f32[8,8192]{1,0:T(8,128)S(1)} fusion(f32[64,8192]{1,0:T(8,128)} %bitcast.93, f32[8,8192]{1,0:T(8,128)S(1)} %get-tuple-element.209, pred[]{:T(512)S(6)} %compare.7, f32[64]{0:T(128)S(1)} %dynamic-slice_bitcast_fusion.11), kind=kOutput, calls=%fused_computation.12.clone.1 | convolution fusion | flops 50463232 | bytes 2621697 | tf_op jit(solution)/shard_map/while/body/eval_jaxpr/dot_general | solution.py:38
  163.6 2.5 %copy.33 = f32[8,8,16,512]{3,1,2,0:T(8,128)} copy(f32[8,8,16,512]{3,2,1,0:T(8,128)S(1)} %bitcast.95) | data formatting | bytes 4194304 | tf_op jit(solution)/shard_map/while
  166.1 2.4 %convolution_add_fusion.5 = f32[8,8192]{1,0:T(8,128)S(1)} fusion(f32[64,8192]{1,0:T(8,128)} %bitcast.93, f32[8,8192]{1,0:T(8,128)S(1)} %get-tuple-element.209, pred[]{:T(512)S(6)} %compare.7, f32[64]{0:T(128)S(1)} %dynamic-slice_bitcast_fusion.11), kind=kOutput, calls=%fused_computation.12.clone.1 | convolution fusion | flops 50463232 | bytes 2621697 | tf_op jit(solution)/shard_map/while/body/eval_jaxpr/dot_general | solution.py:38
  171.7 2.5 %copy.33 = f32[8,8,16,512]{3,1,2,0:T(8,128)} copy(f32[8,8,16,512]{3,2,1,0:T(8,128)S(1)} %bitcast.95) | data formatting | bytes 4194304 | tf_op jit(solution)/shard_map/while
  174.2 2.4 %convolution_add_fusion.5 = f32[8,8192]{1,0:T(8,128)S(1)} fusion(f32[64,8192]{1,0:T(8,128)} %bitcast.93, f32[8,8192]{1,0:T(8,128)S(1)} %get-tuple-element.209, pred[]{:T(512)S(6)} %compare.7, f32[64]{0:T(128)S(1)} %dynamic-slice_bitcast_fusion.11), kind=kOutput, calls=%fused_computation.12.clone.1 | convolution fusion | flops 50463232 | bytes 2621697 | tf_op jit(solution)/shard_map/while/body/eval_jaxpr/dot_general | solution.py:38
  179.9 2.5 %copy.33 = f32[8,8,16,512]{3,1,2,0:T(8,128)} copy(f32[8,8,16,512]{3,2,1,0:T(8,128)S(1)} %bitcast.95) | data formatting | bytes 4194304 | tf_op jit(solution)/shard_map/while
  182.4 2.4 %convolution_add_fusion.5 = f32[8,8192]{1,0:T(8,128)S(1)} fusion(f32[64,8192]{1,0:T(8,128)} %bitcast.93, f32[8,8192]{1,0:T(8,128)S(1)} %get-tuple-element.209, pred[]{:T(512)S(6)} %compare.7, f32[64]{0:T(128)S(1)} %dynamic-slice_bitcast_fusion.11), kind=kOutput, calls=%fused_computation.12.clone.1 | convolution fusion | flops 50463232 | bytes 2621697 | tf_op jit(solution)/shard_map/while/body/eval_jaxpr/dot_general | solution.py:38
  185.8 21.8 %all-gather.2.cloned.1.call-done = f32[2,8,16,2048]{3,2,1,0:T(8,128)} async-done(((f32[2,8,16,512]{3,2,1,0:T(8,128)}), f32[2,8,16,2048]{3,2,1,0:T(8,128)}) %all-gather.2.cloned.1.call-update) | async-done | bytes 2097168 | tf_op jit(solution)/shard_map/all_gather | solution.py:72
  207.6 4.2 %fusion.10 = f32[2,8,16,512]{3,2,1,0:T(8,128)} fusion(f32[2,8,16,2048]{3,2,1,0:T(8,128)} %all-gather.2.cloned.1.call-done, bf16[2048,512]{1,0:T(8,128)(2,1)S(1)} %copy-done), kind=kOutput, calls=%fused_computation.22 | convolution fusion | flops 3221225472 | bytes 4718592 | tf_op jit(solution)/shard_map/agrp,pk->agrk/dot_general | solution.py:70
  (56 shorter events, 36.2 us)
Async XLA Ops:
  6.5 201.1 %copy-start = (bf16[2048,512]{1,0:T(8,128)(2,1)S(1)}, bf16[2048,512]{1,0:T(8,128)(2,1)}, u32[]{:S(2)}) copy-start(bf16[2048,512]{1,0:T(8,128)(2,1)} %param.15) | copy-start | bytes 6291460
  10.6 13.7 %all-to-all-start = ((f32[8,1,32]{2,1,0:T(1,128)}), f32[8,1,32]{2,1,0:T(1,128)S(1)}, u32[]{:S(2)}, u32[]{:S(2)}) async-start(f32[8,1,32]{2,1,0:T(1,128)} %all_to_all.18), calls=%async_computation | async-start | bytes 8192 | tf_op jit(solution)/shard_map/all_to_all | solution.py:59
  24.4 22.8 %all-to-all-start.2 = ((f32[8,1,32]{2,1,0:T(1,128)}), f32[8,1,32]{2,1,0:T(1,128)S(1)}, u32[]{:S(2)}, u32[]{:S(2)}) async-start(f32[8,1,32]{2,1,0:T(1,128)} %all_to_all.21), calls=%async_computation.2 | async-start | bytes 8192 | tf_op jit(solution)/shard_map/all_to_all | solution.py:59
  47.2 6.1 %copy-start.2 = (f32[2,4,6]{2,1,0:T(4,128)S(1)}, f32[2,4,6]{2,1,0:T(4,128)}, u32[]{:S(2)}) copy-start(f32[2,4,6]{2,1,0:T(4,128)} %param.13) | copy-start | bytes 580
  47.2 52.9 %all-to-all-start.1 = ((f32[8,32,4,512]{3,2,1,0:T(4,128)}), f32[8,32,4,512]{3,2,1,0:T(4,128)}, u32[]{:S(2)}, u32[]{:S(2)}) async-start(f32[8,32,4,512]{3,2,1,0:T(4,128)} %bitcast.91), calls=%async_computation.1 | async-start | bytes 4194304 | tf_op jit(solution)/shard_map/all_to_all | solution.py:58
  100.1 4.7 %copy-start.1 = (f32[8,8192]{1,0:T(8,128)S(1)}, f32[8,8192]{1,0:T(8,128)}, u32[]{:S(2)}) copy-start(f32[8,8192]{1,0:T(8,128)} %custom-call) | copy-start | bytes 786436
  100.1 4.7 %copy-start.3 = (f32[16]{0:T(128)S(1)}, f32[16]{0:T(128)}, u32[]{:S(2)}) copy-start(f32[16]{0:T(128)} %param.14) | copy-start | bytes 196
  100.1 52.1 %all-to-all-start.3 = ((f32[8,32,4,512]{3,2,1,0:T(4,128)}), f32[8,32,4,512]{3,2,1,0:T(4,128)}, u32[]{:S(2)}, u32[]{:S(2)}) async-start(f32[8,32,4,512]{3,2,1,0:T(4,128)} %bitcast.90), calls=%async_computation.3 | async-start | bytes 4194304 | tf_op jit(solution)/shard_map/all_to_all | solution.py:58
  104.5 103.1 %all-gather.2.cloned.1.call-start = ((), (), s32[]{:S(2)}) async-start(), calls=%async_computation.4 | async-start | bytes 2621440 | tf_op jit(solution)/shard_map/all_gather | solution.py:72
Sparse Core Ops, SparseCore 0:
  185.9 21.6 all-gather.1
where the time goes:
time: 221 us; the launch traced here: 219 us
  waiting for transfers between devices  66.4 us (30%)
  local copies, waits for them, and re-layouts  64.5 us (29%)
  matrix products  31.4 us (14%)
  starting transfers between devices  21.4 us (10%)
  other arithmetic  21.1 us (10%)
  between operations  13.5 us (6%)
    all_to_all x2, waiting for transfers between devices, local(): lax.all_to_all(outgoing, 'slab', split_axis=0, concat_axis=0, tiled=True)  39.8 us
    scatter x2, local copies, waits for them, and re-layouts, local(): jnp.zeros((slots, qcount, vox_here), jnp.float32).at[slot].set(local_proj)  27.4 us
    all_gather x1, waiting for transfers between devices, local(): lax.all_gather(stacked, 'rock', axis=3, tiled=True)  21.8 us
    while x8, local copies, waits for them, and re-layouts  20.1 us
    dot_general x8, matrix products, add_block(): jnp.dot(onehot, summed.reshape(block_size, rocks * pix_here), precision=l...  18.9 us
    reduce_sum x8, other arithmetic, add_block(): jnp.sum(jnp.exp(-0.5 * (proj_block[:, :, None, :] - rock_angles[None, Non...  17.5 us
    all_to_all x2, starting transfers between devices, local(): lax.all_to_all(row_send, 'slab', split_axis=0, concat_axis=0, tiled=True)  10.6 us
    all_to_all x2, starting transfers between devices, local(): lax.all_to_all(outgoing, 'slab', split_axis=0, concat_axis=0, tiled=True)  10.6 us
  transfers between devices with their start and end apart: 5, of which 4 were waited for; matrix products, arithmetic and copies ran while one was open for 34% of the time, Pallas kernels for 0%

commit v1 on v0

--- a/solution.py
+++ b/solution.py
@@ -1,6 +1,10 @@
+import functools
+import math
 import jax
 import jax.numpy as jnp
 from jax import lax
+from jax.experimental import pallas as pl
+from jax.experimental.pallas import tpu as pltpu
 from jax.sharding import PartitionSpec as P
 
 TILES_DEV = 128
@@ -8,9 +12,12 @@
 QDIR = 4
 ROWS = 8
 ANGLES = 2
-
-
-def local(strain, dest, det_row, dirs, rock_angles, resolution):
+LANES = 128
+GROUP = 8
+SCALE = math.sqrt(0.5 / math.log(2.0))
+
+
+def by_tiles(strain, dest, det_row, dirs, rock_angles, resolution):
     slabs = lax.axis_size("slab")
     tiles_here = strain.shape[0]
     vox_here = strain.shape[2]
@@ -75,6 +82,220 @@
     )
 
 
+def image_kernel(count_ref, list_ref, dirs_ref, rock_ref, own_ref, other_ref, far_ref, near_ref, proj, acc):
+    comps, tiles, lanes = own_ref.shape
+    angles = count_ref.shape[0]
+    qcount = dirs_ref.shape[0] // (angles * comps)
+    rocks = rock_ref.shape[0]
+    step = 2 * GROUP
+
+    for half, ref in enumerate((own_ref, other_ref)):
+
+        @pl.loop(0, tiles // step)
+        def _(block):
+            rows = pl.ds(pl.multiple_of(block * step, step), step)
+            place = pl.ds(pl.multiple_of(half * tiles + block * step, step), step)
+            parts = [ref[c, rows, :] for c in range(comps)]
+            for k in range(angles * qcount):
+                total = parts[0] * dirs_ref[k * comps]
+                for c in range(1, comps):
+                    total = total + parts[c] * dirs_ref[k * comps + c]
+                proj[k, place, :] = total
+
+    acc[...] = jnp.zeros_like(acc)
+    rock = rock_ref[...]
+    for angle in range(angles):
+
+        @pl.loop(0, (count_ref[angle] + GROUP - 1) // GROUP)
+        def _(block):
+            sums = []
+            targets = []
+            for j in range(GROUP):
+                code = list_ref[angle, block * GROUP + j]
+                tile = code % (2 * tiles)
+                targets.append(pl.multiple_of(code // (2 * tiles) * rocks, rocks))
+                total = None
+                for q in range(qcount):
+                    p = proj[angle * qcount + q, pl.ds(tile, 1), :]
+                    d = jnp.broadcast_to(p, (rocks, lanes)) - rock
+                    e = jnp.exp2(-(d * d))
+                    total = e if total is None else total + e
+                sums.append(total)
+            for target, total in zip(targets, sums):
+                acc[pl.ds(target, rocks), :] += total
+
+    near = near_ref.shape[0]
+    far = far_ref.shape[0]
+    far_ref[...] = acc[pl.ds(0, far), :]
+    near_ref[...] = acc[pl.ds(far, near), :]
+
+
+def partial_images(counts, lists, dirs, rock, own, other, line):
+    comps, tiles, lanes = own.shape
+    angles = counts.shape[0]
+    qcount = dirs.shape[0] // (angles * comps)
+    rocks = rock.shape[0]
+    unit = angles * ROWS * rocks
+    smem = pl.BlockSpec(memory_space=pltpu.SMEM)
+    vmem = pl.BlockSpec(memory_space=pltpu.VMEM)
+    return pl.pallas_call(
+        image_kernel,
+        out_shape=(
+            jax.ShapeDtypeStruct(((line - 1) * unit, lanes), jnp.float32),
+            jax.ShapeDtypeStruct((unit, lanes), jnp.float32),
+        ),
+        in_specs=[smem, smem, smem, vmem, vmem, vmem],
+        out_specs=(vmem, vmem),
+        scratch_shapes=[
+            pltpu.VMEM((angles * qcount, 2 * tiles, lanes), jnp.float32),
+            pltpu.VMEM((line * unit + rocks, lanes), jnp.float32),
+        ],
+        cost_estimate=pl.CostEstimate(flops=6_000_000, bytes_accessed=2_000_000, transcendentals=0),
+        name="partial_images",
+    )(counts, lists, dirs, rock, own, other)
+
+
+def resolve_kernel(rock_ref, first, pix, norm, total_ref, res_ref, *rest):
+    parts, out_ref = rest[:-1], rest[-1]
+    lanes = parts[0].shape[1]
+    total = total_ref[...] if total_ref is not None else None
+    for j, part in enumerate(parts):
+        start = pl.multiple_of((rock_ref[0] ^ j) * pix + first, lanes)
+        block = res_ref[pl.ds(start, lanes), :]
+        value = part[...] * norm
+        high = value.astype(jnp.bfloat16)
+        low = (value - high.astype(jnp.float32)).astype(jnp.bfloat16)
+        added = jnp.dot(high, block, preferred_element_type=jnp.float32) + jnp.dot(
+            low, block, preferred_element_type=jnp.float32
+        )
+        total = added if total is None else total + added
+    out_ref[...] = total
+
+
+def resolve(rock_index, first, pix, norm, total, resolution, parts):
+    unit, lanes = parts[0].shape
+    cols = resolution.shape[1]
+    smem = pl.BlockSpec(memory_space=pltpu.SMEM)
+    vmem = pl.BlockSpec(memory_space=pltpu.VMEM)
+
+    def kernel(rock_ref, *refs):
+        if total is None:
+            resolve_kernel(rock_ref, first, pix, norm, None, *refs)
+        else:
+            resolve_kernel(rock_ref, first, pix, norm, *refs)
+
+    before = () if total is None else (total,)
+    return pl.pallas_call(
+        kernel,
+        out_shape=jax.ShapeDtypeStruct((unit, cols), jnp.float32),
+        in_specs=[smem] + [vmem] * (len(before) + 1 + len(parts)),
+        out_specs=vmem,
+        cost_estimate=pl.CostEstimate(flops=500_000_000, bytes_accessed=3_000_000, transcendentals=0),
+        name="resolve",
+    )(rock_index, *before, resolution, *parts)
+
+
+def line_sum(far, near, line, unit, pair):
+    half = line // 2
+    place = lax.axis_index("slab") // pair
+
+    def send(value, links):
+        pairs = [(a * pair + k, b * pair + k) for a, b in links for k in range(pair)]
+        return lax.ppermute(value, "slab", pairs)
+
+    held = far
+    for p in range(half - 1):
+        count = line - 1 - p
+        arrived = send(held[: count * unit], [(p, p + 1), (line - 1 - p, line - 2 - p)])
+        held = jnp.concatenate([held[: count * unit] + arrived, held[count * unit :]], axis=0)
+    own = [held[j * unit : (j + 1) * unit] for j in range(line - 1)] + [near]
+    middle = send(held[: half * unit], [(half - 1, half), (half, half - 1)])
+    carried = [middle[j * unit : (j + 1) * unit] for j in range(half)]
+    outer = []
+    for p in range(half, line - 1):
+        count = line - 1 - p
+        sent = jnp.concatenate([own[line - 1 - j] + carried[j] for j in range(count)], axis=0)
+        outer.append(sent)
+        arrived = send(sent, [(p, p + 1), (line - 1 - p, line - 2 - p)])
+        arrived = [arrived[j * unit : (j + 1) * unit] for j in range(count)]
+        carried = [carried[j] + arrived[j] for j in range(count)] + carried[count:]
+    fold = jnp.where(place < half, line - 1 - place, place)
+    result = own[line - 1] + carried[0]
+    for j in range(1, half):
+        result = jnp.where(fold == line - 1 - j, own[line - 1 - j] + carried[j], result)
+    return result
+
+
+def by_images(strain, dest, det_row, dirs, rock_angles, resolution):
+    slabs = lax.axis_size("slab")
+    rock_size = lax.axis_size("rock")
+    tiles = strain.shape[0]
+    pix = resolution.shape[1]
+    rocks = rock_angles.shape[0]
+    angles, qcount, comps = dirs.shape
+    norm = ROWS / (QDIR * DEPTH * TILES_DEV)
+    pair = 2
+    line = slabs // pair
+    unit = angles * ROWS * rocks
+    me = lax.axis_index("slab")
+    swap = [(i, i ^ 1) for i in range(slabs)]
+    chunks = pix // LANES
+
+    info = dest[:, :, 0] * ROWS + det_row
+    other_info = lax.ppermute(info, "slab", swap)
+    by_comp = strain.transpose(1, 0, 2)
+    own = [by_comp[:, :, c * LANES : (c + 1) * LANES] for c in range(chunks)]
+    other = [lax.ppermute(own[c], "slab", swap) for c in range(chunks)]
+
+    info = jnp.concatenate([info, other_info], axis=1)
+    owner = info // ROWS
+    place = owner // pair
+    keep = owner % pair == me % pair
+    position = jnp.where(me // pair < line // 2, line - 1 - place, place)
+    target = (position * angles + jnp.arange(angles)[:, None]) * ROWS + info % ROWS
+    number = jnp.arange(2 * tiles)
+    earlier = keep[:, None, :] & (number[None, None, :] < number[None, :, None])
+    rank = jnp.sum(earlier.astype(jnp.int32), axis=2)
+    rank = jnp.where(keep, rank, -1)
+    trash = line * angles * ROWS
+    code = number[None, :] + 2 * tiles * (target - trash)
+    lists = 2 * tiles * trash + jnp.sum(
+        jnp.where(rank[:, None, :] == number[None, :, None], code[:, None, :], 0), axis=2
+    )
+    counts = jnp.sum(keep.astype(jnp.int32), axis=1)
+
+    weights = (dirs * SCALE).reshape(-1)
+    rock = jnp.broadcast_to((rock_angles * SCALE)[:, None], (rocks, LANES))
+    rock_index = lax.axis_index("rock").reshape(1)
+
+    result = None
+    for c in range(chunks):
+        far, near = partial_images(counts, lists, weights, rock, own[c], other[c], line)
+        parts = [line_sum(far, near, line, unit, pair)]
+        bit = rock_size // 2
+        order = [0]
+        while bit:
+            links = [(i, i ^ bit) for i in range(rock_size)]
+            parts = parts + [lax.ppermute(part, "rock", links) for part in parts]
+            order = order + [k ^ bit for k in order]
+            bit //= 2
+        parts = [parts[order.index(k)] for k in range(rock_size)]
+        result = resolve(rock_index, c * LANES, pix, norm, result, resolution, parts)
+    return result.reshape(angles, ROWS, rocks, pix)
+
+
+def local(strain, dest, det_row, dirs, rock_angles, resolution):
+    slabs = lax.axis_size("slab")
+    rock_size = lax.axis_size("rock")
+    tiles, unused, vox = strain.shape
+    pix = resolution.shape[1]
+    slots = slabs * (2 * tiles // slabs)
+    images_smaller = slabs * ROWS * rock_angles.shape[0] * pix <= slots * dirs.shape[1] * vox
+    regular = slabs % 4 == 0 and rock_size & (rock_size - 1) == 0 and vox == pix and pix % LANES == 0
+    plan = by_images if images_smaller and regular else by_tiles
+    return plan(strain, dest, det_row, dirs, rock_angles, resolution)
+
+
 def solution(mesh):
     placed = (
         P("slab", None, "rock"),

time: 221 us -> 109 us (0.49)
  the two profiles are of different devices: /device:TPU:0 before, /device:TPU:9 now
where the time goes in v1:
time: 109 us
  Pallas kernels  36.7 us (34%)
  starting transfers between devices  36.5 us (33%)
  waiting for transfers between devices  20.2 us (19%)
  local copies, waits for them, and re-layouts  9.03 us (8%)
  other arithmetic  5.7 us (5%)
    pallas_call x4, Pallas kernels, partial_images(): pl.pallas_call(image_kernel, out_shape=(jax.ShapeDtypeStruct(((line - 1)...  23.5 us
    ppermute x12, starting transfers between devices, send(): return lax.ppermute(value, 'slab', pairs)  21.5 us
    pallas_call x4, Pallas kernels, resolve(): pl.pallas_call(kernel, out_shape=jax.ShapeDtypeStruct((unit, cols), jnp.f...  13.2 us
    ppermute x12, starting transfers between devices, by_images(): parts = parts + [lax.ppermute(part, 'rock', links) for part in parts]  10.7 us
    ppermute x12, waiting for transfers between devices, send(): return lax.ppermute(value, 'slab', pairs)  8.6 us
    unnamed x68, local copies, waits for them, and re-layouts  6.11 us
    ppermute x12, waiting for transfers between devices, by_images(): parts = parts + [lax.ppermute(part, 'rock', links) for part in parts]  5.85 us
    ppermute x4, waiting for transfers between devices, by_images(): other = [lax.ppermute(own[c], 'slab', swap) for c in range(chunks)]  5.78 us
  transfers between devices with their start and end apart: 29, of which 10 were waited for; matrix products, arithmetic and copies ran while one was open for 7% of the time, Pallas kernels for 31%

profile of v1, /device:TPU:9, one launch (start us, length us, event | category | flops | bytes accessed | tf_op | source)
XLA Modules:
  0.0 108.7 jit_solution(17966150490671327485)
XLA Ops:
  1.9 1.5 %fusion.10 = (f32[6,128,128]{2,1,0:T(8,128)S(1)}, f32[6,128,128]{2,1,0:T(8,128)S(1)}, f32[6,128,128]{2,1,0:T(8,128)S(1)}, f32[6,128,128]{2,1,0:T(8,128)S(1)}) fusion(f32[6,128,512]{2,1,0:T(8,128)} %bitcast.6), kind=kLoop, calls=%fused_computation.44 | loop fusion | bytes 3145728 | tf_op jit(solution)/shard_map/slice | solution.py:247
  8.8 4.4 %collective-permute-done.1.other_ref = f32[6,128,128]{2,1,0:T(8,128)S(1)} collective-permute-done((f32[6,128,128]{2,1,0:T(8,128)S(1)}, f32[6,128,128]{2,1,0:T(8,128)S(1)}, u32[]{:S(2)}, u32[]{:S(2)}) %collective-permute-start.1) | collective-permute-done | bytes 393248 | tf_op jit(solution)/shard_map/ppermute | solution.py:248
  14.0 5.9 %partial_images.4 = (f32[768,128]{1,0:T(8,128)}, f32[256,128]{1,0:T(8,128)}) custom-call(s32[2]{0:T(128)} %get-tuple-element.23.count_ref, s32[2,256]{1,0:T(2,128)} %broadcast_add_fusion.list_ref, f32[48]{0:T(128)} %reshape.241.dirs_ref, f32[16,128]{1,0:T(8,128)} %broadcast_in_dim.18.rock_ref, f32[6,128,128]{2,1,0:T(8,128)} %copy-done.3, ...), custom_call_target="tpu_custom_call" | custom-call | flops 6000000 | bytes 2000000 | tf_op jit(solution)/shard_map/partial_images/pallas_call | solution.py:141
  19.8 1.4 %collective-permute-start.2 = (f32[768,128]{1,0:T(8,128)}, f32[768,128]{1,0:T(8,128)}, u32[]{:S(2)}, u32[]{:S(2)}) collective-permute-start(f32[768,128]{1,0:T(8,128)} %get-tuple-element.13), channel_id=1, source_target_pairs={{0,8},{4,12},{24,16},{28,20},{1,9},{5,13},{25,17},{29,21},{2,10},{... | collective-permute-start | bytes 1179656 | tf_op jit(solution)/shard_map/ppermute | solution.py:204
  22.4 5.9 %partial_images.5 = (f32[768,128]{1,0:T(8,128)}, f32[256,128]{1,0:T(8,128)}) custom-call(s32[2]{0:T(128)} %get-tuple-element.23.count_ref, s32[2,256]{1,0:T(2,128)} %broadcast_add_fusion.list_ref, f32[48]{0:T(128)} %reshape.241.dirs_ref, f32[16,128]{1,0:T(8,128)} %broadcast_in_dim.18.rock_ref, f32[6,128,128]{2,1,0:T(8,128)} %copy-done.2, ...), custom_call_target="tpu_custom_call" | custom-call | flops 6000000 | bytes 2000000 | tf_op jit(solution)/shard_map/partial_images/pallas_call | solution.py:141
  28.3 1.4 %collective-permute-start.9 = (f32[768,128]{1,0:T(8,128)}, f32[768,128]{1,0:T(8,128)}, u32[]{:S(2)}, u32[]{:S(2)}) collective-permute-start(f32[768,128]{1,0:T(8,128)} %get-tuple-element.15), channel_id=1, source_target_pairs={{0,8},{4,12},{24,16},{28,20},{1,9},{5,13},{25,17},{29,21},{2,10},{... | collective-permute-start | bytes 1179656 | tf_op jit(solution)/shard_map/ppermute | solution.py:204
  30.9 5.9 %partial_images.6 = (f32[768,128]{1,0:T(8,128)}, f32[256,128]{1,0:T(8,128)}) custom-call(s32[2]{0:T(128)} %get-tuple-element.23.count_ref, s32[2,256]{1,0:T(2,128)} %broadcast_add_fusion.list_ref, f32[48]{0:T(128)} %reshape.241.dirs_ref, f32[16,128]{1,0:T(8,128)} %broadcast_in_dim.18.rock_ref, f32[6,128,128]{2,1,0:T(8,128)} %copy-done.1, ...), custom_call_target="tpu_custom_call" | custom-call | flops 6000000 | bytes 2000000 | tf_op jit(solution)/shard_map/partial_images/pallas_call | solution.py:141
  36.8 1.3 %collective-permute-start.16 = (f32[768,128]{1,0:T(8,128)}, f32[768,128]{1,0:T(8,128)S(1)}, u32[]{:S(2)}, u32[]{:S(2)}) collective-permute-start(f32[768,128]{1,0:T(8,128)} %get-tuple-element.17), channel_id=1, source_target_pairs={{0,8},{4,12},{24,16},{28,20},{1,9},{5,13},{25,17},{29,21},{2,10},{... | collective-permute-start | bytes 1179656 | tf_op jit(solution)/shard_map/ppermute | solution.py:204
  39.4 5.9 %partial_images.7 = (f32[768,128]{1,0:T(8,128)}, f32[256,128]{1,0:T(8,128)}) custom-call(s32[2]{0:T(128)} %get-tuple-element.23.count_ref, s32[2,256]{1,0:T(2,128)} %broadcast_add_fusion.list_ref, f32[48]{0:T(128)} %reshape.241.dirs_ref, f32[16,128]{1,0:T(8,128)} %broadcast_in_dim.18.rock_ref, f32[6,128,128]{2,1,0:T(8,128)} %copy-done, f32[6,128,128]{2,1,0:T(8,128)} %copy-done.12), custom_call_target="tpu_custom_call" | custom-call | flops 6000000 | bytes 2000000 | tf_op jit(solution)/shard_map/partial_images/pallas_call | solution.py:141
  45.2 1.4 %collective-permute-start.23 = (f32[768,128]{1,0:T(8,128)}, f32[768,128]{1,0:T(8,128)}, u32[]{:S(2)}, u32[]{:S(2)}) collective-permute-start(f32[768,128]{1,0:T(8,128)} %get-tuple-element.19), channel_id=1, source_target_pairs={{0,8},{4,12},{24,16},{28,20},{1,9},{5,13},{25,17},{29,21},{2,10},{... | collective-permute-start | bytes 1179656 | tf_op jit(solution)/shard_map/ppermute | solution.py:204
  47.7 3.3 %collective-permute-start.3 = (f32[512,128]{1,0:T(8,128)S(1)}, f32[512,128]{1,0:T(8,128)S(1)}, u32[]{:S(2)}, u32[]{:S(2)}) collective-permute-start(f32[512,128]{1,0:T(8,128)S(1)} %slice.82), channel_id=1, source_target_pairs={{8,16},{12,20},{16,8},{20,12},{9,17},{13,21},{17,9},{21,13},{10,18... | collective-permute-start | bytes 786440 | tf_op jit(solution)/shard_map/ppermute | solution.py:204
  52.2 2.1 %collective-permute-start.10 = (f32[512,128]{1,0:T(8,128)S(1)}, f32[512,128]{1,0:T(8,128)S(1)}, u32[]{:S(2)}, u32[]{:S(2)}) collective-permute-start(f32[512,128]{1,0:T(8,128)S(1)} %slice.87), channel_id=1, source_target_pairs={{8,16},{12,20},{16,8},{20,12},{9,17},{13,21},{17,9},{21,13},{10,18... | collective-permute-start | bytes 786440 | tf_op jit(solution)/shard_map/ppermute | solution.py:204
  54.4 3.3 %collective-permute-start.17 = (f32[512,128]{1,0:T(8,128)S(1)}, f32[512,128]{1,0:T(8,128)S(1)}, u32[]{:S(2)}, u32[]{:S(2)}) collective-permute-start(f32[512,128]{1,0:T(8,128)S(1)} %slice.92), channel_id=1, source_target_pairs={{8,16},{12,20},{16,8},{20,12},{9,17},{13,21},{17,9},{21,13},{10,18... | collective-permute-start | bytes 786440 | tf_op jit(solution)/shard_map/ppermute | solution.py:204
  58.8 2.1 %collective-permute-start.24 = (f32[512,128]{1,0:T(8,128)S(1)}, f32[512,128]{1,0:T(8,128)S(1)}, u32[]{:S(2)}, u32[]{:S(2)}) collective-permute-start(f32[512,128]{1,0:T(8,128)S(1)} %slice.97), channel_id=1, source_target_pairs={{8,16},{12,20},{16,8},{20,12},{9,17},{13,21},{17,9},{21,13},{10,18... | collective-permute-start | bytes 786440 | tf_op jit(solution)/shard_map/ppermute | solution.py:204
  61.0 1.3 %collective-permute-start.4 = (f32[256,128]{1,0:T(8,128)S(1)}, f32[256,128]{1,0:T(8,128)S(1)}, u32[]{:S(2)}, u32[]{:S(2)}) collective-permute-start(f32[256,128]{1,0:T(8,128)S(1)} %slice_add_fusion.7), channel_id=1, source_target_pairs={{16,24},{20,28},{8,0},{12,4},{17,25},{21,29},{9,1},{13,5},{18,26},... | collective-permute-start | bytes 393224 | tf_op jit(solution)/shard_map/ppermute | solution.py:204
  62.3 1.3 %collective-permute-start.11 = (f32[256,128]{1,0:T(8,128)S(1)}, f32[256,128]{1,0:T(8,128)S(1)}, u32[]{:S(2)}, u32[]{:S(2)}) collective-permute-start(f32[256,128]{1,0:T(8,128)S(1)} %slice_add_fusion.6), channel_id=1, source_target_pairs={{16,24},{20,28},{8,0},{12,4},{17,25},{21,29},{9,1},{13,5},{18,26},... | collective-permute-start | bytes 393224 | tf_op jit(solution)/shard_map/ppermute | solution.py:204
  63.6 4.3 %collective-permute-done.17 = f32[512,128]{1,0:T(8,128)S(1)} collective-permute-done((f32[512,128]{1,0:T(8,128)S(1)}, f32[512,128]{1,0:T(8,128)S(1)}, u32[]{:S(2)}, u32[]{:S(2)}) %collective-permute-start.17) | collective-permute-done | bytes 262176 | tf_op jit(solution)/shard_map/ppermute | solution.py:204
  67.9 1.3 %collective-permute-start.18 = (f32[256,128]{1,0:T(8,128)S(1)}, f32[256,128]{1,0:T(8,128)S(1)}, u32[]{:S(2)}, u32[]{:S(2)}) collective-permute-start(f32[256,128]{1,0:T(8,128)S(1)} %slice_add_fusion.5), channel_id=1, source_target_pairs={{16,24},{20,28},{8,0},{12,4},{17,25},{21,29},{9,1},{13,5},{18,26},... | collective-permute-start | bytes 393224 | tf_op jit(solution)/shard_map/ppermute | solution.py:204
  69.2 4.3 %collective-permute-done.24 = f32[512,128]{1,0:T(8,128)S(1)} collective-permute-done((f32[512,128]{1,0:T(8,128)S(1)}, f32[512,128]{1,0:T(8,128)S(1)}, u32[]{:S(2)}, u32[]{:S(2)}) %collective-permute-start.24) | collective-permute-done | bytes 262176 | tf_op jit(solution)/shard_map/ppermute | solution.py:204
  73.5 1.3 %collective-permute-start.25 = (f32[256,128]{1,0:T(8,128)S(1)}, f32[256,128]{1,0:T(8,128)S(1)}, u32[]{:S(2)}, u32[]{:S(2)}) collective-permute-start(f32[256,128]{1,0:T(8,128)S(1)} %slice_add_fusion.4), channel_id=1, source_target_pairs={{16,24},{20,28},{8,0},{12,4},{17,25},{21,29},{9,1},{13,5},{18,26},... | collective-permute-start | bytes 393224 | tf_op jit(solution)/shard_map/ppermute | solution.py:204
  74.9 2.3 %collective-permute-start.5 = (f32[256,128]{1,0:T(8,128)S(1)}, f32[256,128]{1,0:T(8,128)S(1)}, u32[]{:S(2)}, u32[]{:S(2)}) collective-permute-start(f32[256,128]{1,0:T(8,128)S(1)} %fusion.3.refs_1_), channel_id=1, source_target_pairs={{0,1},{1,0},{2,3},{3,2},{4,5},{5,4},{6,7},{7,6},{8,9},{9,8},{10,11... | collective-permute-start | bytes 393224 | tf_op jit(solution)/shard_map/ppermute | solution.py:279
  80.9 1.4 %collective-permute-done.6.refs_3_ = f32[256,128]{1,0:T(8,128)S(1)} collective-permute-done((f32[256,128]{1,0:T(8,128)S(1)}, f32[256,128]{1,0:T(8,128)S(1)}, u32[]{:S(2)}, u32[]{:S(2)}) %collective-permute-start.6) | collective-permute-done | bytes 131104 | tf_op jit(solution)/shard_map/ppermute | solution.py:279
  82.3 1.3 %collective-permute-start.7 = (f32[256,128]{1,0:T(8,128)S(1)}, f32[256,128]{1,0:T(8,128)S(1)}, u32[]{:S(2)}, u32[]{:S(2)}) collective-permute-start(f32[256,128]{1,0:T(8,128)S(1)} %collective-permute-done.6.refs_3_), channel_id=1, source_target_pairs={{0,1},{1,0},{2,3},{3,2},{4,5},{5,4},{6,7},{7,6},{8,9},{9,8},{10,11... | collective-permute-start | bytes 393224 | tf_op jit(solution)/shard_map/ppermute | solution.py:279
  83.6 1.5 %collective-permute-done.13.refs_4_ = f32[256,128]{1,0:T(8,128)S(1)} collective-permute-done((f32[256,128]{1,0:T(8,128)S(1)}, f32[256,128]{1,0:T(8,128)S(1)}, u32[]{:S(2)}, u32[]{:S(2)}) %collective-permute-start.13) | collective-permute-done | bytes 131104 | tf_op jit(solution)/shard_map/ppermute | solution.py:279
  85.1 1.3 %collective-permute-start.14 = (f32[256,128]{1,0:T(8,128)S(1)}, f32[256,128]{1,0:T(8,128)S(1)}, u32[]{:S(2)}, u32[]{:S(2)}) collective-permute-start(f32[256,128]{1,0:T(8,128)S(1)} %collective-permute-done.13.refs_4_), channel_id=1, source_target_pairs={{0,1},{1,0},{2,3},{3,2},{4,5},{5,4},{6,7},{7,6},{8,9},{9,8},{10,11... | collective-permute-start | bytes 393224 | tf_op jit(solution)/shard_map/ppermute | solution.py:279
  86.5 1.4 %collective-permute-done.20.refs_4_ = f32[256,128]{1,0:T(8,128)S(1)} collective-permute-done((f32[256,128]{1,0:T(8,128)S(1)}, f32[256,128]{1,0:T(8,128)S(1)}, u32[]{:S(2)}, u32[]{:S(2)}) %collective-permute-start.20) | collective-permute-done | bytes 131104 | tf_op jit(solution)/shard_map/ppermute | solution.py:279
  87.9 1.3 %collective-permute-start.21 = (f32[256,128]{1,0:T(8,128)S(1)}, f32[256,128]{1,0:T(8,128)S(1)}, u32[]{:S(2)}, u32[]{:S(2)}) collective-permute-start(f32[256,128]{1,0:T(8,128)S(1)} %collective-permute-done.20.refs_4_), channel_id=1, source_target_pairs={{0,1},{1,0},{2,3},{3,2},{4,5},{5,4},{6,7},{7,6},{8,9},{9,8},{10,11... | collective-permute-start | bytes 393224 | tf_op jit(solution)/shard_map/ppermute | solution.py:279
  89.2 1.5 %collective-permute-done.27.refs_4_ = f32[256,128]{1,0:T(8,128)S(1)} collective-permute-done((f32[256,128]{1,0:T(8,128)S(1)}, f32[256,128]{1,0:T(8,128)S(1)}, u32[]{:S(2)}, u32[]{:S(2)}) %collective-permute-start.27) | collective-permute-done | bytes 131104 | tf_op jit(solution)/shard_map/ppermute | solution.py:279
  92.2 3.2 %resolve.4.refs_0_ = f32[256,512]{1,0:T(8,128)} custom-call(s32[1]{0:T(128)} %bitcast.rock_ref, bf16[2048,512]{1,0:T(8,128)(2,1)} %refs_1_.5, f32[256,128]{1,0:T(8,128)} %copy-done.11, f32[256,128]{1,0:T(8,128)} %copy-done.29, f32[256,128]{1,0:T(8,128)} %copy-done.30, f32[256,128]{1,0:T(8,128)} %copy-done.31), custom_call_target="tpu_custom_call" | custom-call | flops 500000000 | bytes 3000000 | tf_op jit(solution)/shard_map/resolve/pallas_call | solution.py:188
  96.2 3.3 %resolve.5.refs_0_ = f32[256,512]{1,0:T(8,128)} custom-call(s32[1]{0:T(128)} %bitcast.rock_ref, f32[256,512]{1,0:T(8,128)} %resolve.4.refs_0_, bf16[2048,512]{1,0:T(8,128)(2,1)} %refs_1_.5, f32[256,128]{1,0:T(8,128)} %copy-done.8, f32[256,128]{1,0:T(8,128)} %copy-done.20, f32[256,128]{1,0:T(8,128)} %copy-done.21, f32[256,128]{1,0:T(8,128)} %copy-done.25), custom_call_target="tpu_custom_call" | custom-call | flops 500000000 | bytes 3000000 | tf_op jit(solution)/shard_map/resolve/pallas_call | solution.py:188
  100.8 3.3 %resolve.6.refs_0_ = f32[256,512]{1,0:T(8,128)} custom-call(s32[1]{0:T(128)} %bitcast.rock_ref, f32[256,512]{1,0:T(8,128)} %resolve.5.refs_0_, bf16[2048,512]{1,0:T(8,128)(2,1)} %refs_1_.5, f32[256,128]{1,0:T(8,128)} %copy-done.9, f32[256,128]{1,0:T(8,128)} %copy-done.24, f32[256,128]{1,0:T(8,128)} %copy-done.22, f32[256,128]{1,0:T(8,128)} %copy-done.26), custom_call_target="tpu_custom_call" | custom-call | flops 500000000 | bytes 3000000 | tf_op jit(solution)/shard_map/resolve/pallas_call | solution.py:188
  105.4 3.3 %resolve.7 = f32[256,512]{1,0:T(8,128)} custom-call(s32[1]{0:T(128)} %bitcast.rock_ref, f32[256,512]{1,0:T(8,128)} %resolve.6.refs_0_, bf16[2048,512]{1,0:T(8,128)(2,1)} %refs_1_.5, f32[256,128]{1,0:T(8,128)} %copy-done.10, f32[256,128]{1,0:T(8,128)} %copy-done.27, f32[256,128]{1,0:T(8,128)} %copy-done.23, f32[256,128]{1,0:T(8,128)} %copy-done.28), custom_call_target="tpu_custom_call" | custom-call | flops 500000000 | bytes 3000000 | tf_op jit(solution)/shard_map/resolve/pallas_call | solution.py:188
  (131 shorter events, 23.4 us)
Async XLA Ops:
  0.7 6.5 %collective-permute-start = (s32[2,128]{1,0:T(2,128)S(1)}, s32[2,128]{1,0:T(2,128)S(1)}, u32[]{:S(2)}, u32[]{:S(2)}) collective-permute-start(s32[2,128]{1,0:T(2,128)S(1)} %bitcast_add_fusion), channel_id=1, source_target_pairs={{0,4},{4,0},{8,12},{12,8},{16,20},{20,16},{24,28},{28,24},{1,5},{5... | collective-permute-start | bytes 3080 | tf_op jit(solution)/shard_map/ppermute | solution.py:245
  3.5 26.7 %copy-start.1 = (f32[6,128,128]{2,1,0:T(8,128)}, f32[6,128,128]{2,1,0:T(8,128)S(1)}, u32[]{:S(2)}) copy-start(f32[6,128,128]{2,1,0:T(8,128)S(1)} %get-tuple-element.26.own_ref) | copy-start | bytes 1179652
  3.5 35.1 %copy-start = (f32[6,128,128]{2,1,0:T(8,128)}, f32[6,128,128]{2,1,0:T(8,128)S(1)}, u32[]{:S(2)}) copy-start(f32[6,128,128]{2,1,0:T(8,128)S(1)} %get-tuple-element.25.own_ref) | copy-start | bytes 1179652
  3.5 9.7 %collective-permute-start.1 = (f32[6,128,128]{2,1,0:T(8,128)S(1)}, f32[6,128,128]{2,1,0:T(8,128)S(1)}, u32[]{:S(2)}, u32[]{:S(2)}) collective-permute-start(f32[6,128,128]{2,1,0:T(8,128)S(1)} %get-tuple-element.28.own_ref), channel_id=1, source_target_pairs={{0,4},{4,0},{8,12},{12,8},{16,20},{20,16},{24,28},{28,24},{1,5},{5... | collective-permute-start | bytes 1179656 | tf_op jit(solution)/shard_map/ppermute | solution.py:248
  3.8 17.9 %collective-permute-start.8 = (f32[6,128,128]{2,1,0:T(8,128)S(1)}, f32[6,128,128]{2,1,0:T(8,128)S(1)}, u32[]{:S(2)}, u32[]{:S(2)}) collective-permute-start(f32[6,128,128]{2,1,0:T(8,128)S(1)} %get-tuple-element.27.own_ref), channel_id=1, source_target_pairs={{0,4},{4,0},{8,12},{12,8},{16,20},{20,16},{24,28},{28,24},{1,5},{5... | collective-permute-start | bytes 1179656 | tf_op jit(solution)/shard_map/ppermute | solution.py:248
  5.0 25.2 %collective-permute-start.15 = (f32[6,128,128]{2,1,0:T(8,128)S(1)}, f32[6,128,128]{2,1,0:T(8,128)S(1)}, u32[]{:S(2)}, u32[]{:S(2)}) collective-permute-start(f32[6,128,128]{2,1,0:T(8,128)S(1)} %get-tuple-element.26.own_ref), channel_id=1, source_target_pairs={{0,4},{4,0},{8,12},{12,8},{16,20},{20,16},{24,28},{28,24},{1,5},{5... | collective-permute-start | bytes 1179656 | tf_op jit(solution)/shard_map/ppermute | solution.py:248
  5.2 33.4 %collective-permute-start.22 = (f32[6,128,128]{2,1,0:T(8,128)S(1)}, f32[6,128,128]{2,1,0:T(8,128)S(1)}, u32[]{:S(2)}, u32[]{:S(2)}) collective-permute-start(f32[6,128,128]{2,1,0:T(8,128)S(1)} %get-tuple-element.25.own_ref), channel_id=1, source_target_pairs={{0,4},{4,0},{8,12},{12,8},{16,20},{20,16},{24,28},{28,24},{1,5},{5... | collective-permute-start | bytes 1179656 | tf_op jit(solution)/shard_map/ppermute | solution.py:248
  19.8 26.8 %copy-start.18 = (f32[768,128]{1,0:T(8,128)S(1)}, f32[768,128]{1,0:T(8,128)}, u32[]{:S(2)}) copy-start(f32[768,128]{1,0:T(8,128)} %get-tuple-element.13) | copy-start | bytes 1179652
  19.8 26.8 %collective-permute-start.2 = (f32[768,128]{1,0:T(8,128)}, f32[768,128]{1,0:T(8,128)}, u32[]{:S(2)}, u32[]{:S(2)}) collective-permute-start(f32[768,128]{1,0:T(8,128)} %get-tuple-element.13), channel_id=1, source_target_pairs={{0,8},{4,12},{24,16},{28,20},{1,9},{5,13},{25,17},{29,21},{2,10},{... | collective-permute-start | bytes 1179656 | tf_op jit(solution)/shard_map/ppermute | solution.py:204
  28.3 22.8 %collective-permute-start.9 = (f32[768,128]{1,0:T(8,128)}, f32[768,128]{1,0:T(8,128)}, u32[]{:S(2)}, u32[]{:S(2)}) collective-permute-start(f32[768,128]{1,0:T(8,128)} %get-tuple-element.15), channel_id=1, source_target_pairs={{0,8},{4,12},{24,16},{28,20},{1,9},{5,13},{25,17},{29,21},{2,10},{... | collective-permute-start | bytes 1179656 | tf_op jit(solution)/shard_map/ppermute | solution.py:204
  36.8 17.5 %collective-permute-start.16 = (f32[768,128]{1,0:T(8,128)}, f32[768,128]{1,0:T(8,128)S(1)}, u32[]{:S(2)}, u32[]{:S(2)}) collective-permute-start(f32[768,128]{1,0:T(8,128)} %get-tuple-element.17), channel_id=1, source_target_pairs={{0,8},{4,12},{24,16},{28,20},{1,9},{5,13},{25,17},{29,21},{2,10},{... | collective-permute-start | bytes 1179656 | tf_op jit(solution)/shard_map/ppermute | solution.py:204
  45.2 12.5 %collective-permute-start.23 = (f32[768,128]{1,0:T(8,128)}, f32[768,128]{1,0:T(8,128)}, u32[]{:S(2)}, u32[]{:S(2)}) collective-permute-start(f32[768,128]{1,0:T(8,128)} %get-tuple-element.19), channel_id=1, source_target_pairs={{0,8},{4,12},{24,16},{28,20},{1,9},{5,13},{25,17},{29,21},{2,10},{... | collective-permute-start | bytes 1179656 | tf_op jit(solution)/shard_map/ppermute | solution.py:204
  47.7 13.2 %collective-permute-start.3 = (f32[512,128]{1,0:T(8,128)S(1)}, f32[512,128]{1,0:T(8,128)S(1)}, u32[]{:S(2)}, u32[]{:S(2)}) collective-permute-start(f32[512,128]{1,0:T(8,128)S(1)} %slice.82), channel_id=1, source_target_pairs={{8,16},{12,20},{16,8},{20,12},{9,17},{13,21},{17,9},{21,13},{10,18... | collective-permute-start | bytes 786440 | tf_op jit(solution)/shard_map/ppermute | solution.py:204
  52.2 10.1 %collective-permute-start.10 = (f32[512,128]{1,0:T(8,128)S(1)}, f32[512,128]{1,0:T(8,128)S(1)}, u32[]{:S(2)}, u32[]{:S(2)}) collective-permute-start(f32[512,128]{1,0:T(8,128)S(1)} %slice.87), channel_id=1, source_target_pairs={{8,16},{12,20},{16,8},{20,12},{9,17},{13,21},{17,9},{21,13},{10,18... | collective-permute-start | bytes 786440 | tf_op jit(solution)/shard_map/ppermute | solution.py:204
  54.4 13.5 %collective-permute-start.17 = (f32[512,128]{1,0:T(8,128)S(1)}, f32[512,128]{1,0:T(8,128)S(1)}, u32[]{:S(2)}, u32[]{:S(2)}) collective-permute-start(f32[512,128]{1,0:T(8,128)S(1)} %slice.92), channel_id=1, source_target_pairs={{8,16},{12,20},{16,8},{20,12},{9,17},{13,21},{17,9},{21,13},{10,18... | collective-permute-start | bytes 786440 | tf_op jit(solution)/shard_map/ppermute | solution.py:204
  58.8 14.7 %collective-permute-start.24 = (f32[512,128]{1,0:T(8,128)S(1)}, f32[512,128]{1,0:T(8,128)S(1)}, u32[]{:S(2)}, u32[]{:S(2)}) collective-permute-start(f32[512,128]{1,0:T(8,128)S(1)} %slice.97), channel_id=1, source_target_pairs={{8,16},{12,20},{16,8},{20,12},{9,17},{13,21},{17,9},{21,13},{10,18... | collective-permute-start | bytes 786440 | tf_op jit(solution)/shard_map/ppermute | solution.py:204
  61.0 13.9 %collective-permute-start.4 = (f32[256,128]{1,0:T(8,128)S(1)}, f32[256,128]{1,0:T(8,128)S(1)}, u32[]{:S(2)}, u32[]{:S(2)}) collective-permute-start(f32[256,128]{1,0:T(8,128)S(1)} %slice_add_fusion.7), channel_id=1, source_target_pairs={{16,24},{20,28},{8,0},{12,4},{17,25},{21,29},{9,1},{13,5},{18,26},... | collective-permute-start | bytes 393224 | tf_op jit(solution)/shard_map/ppermute | solution.py:204
  62.3 16.1 %collective-permute-start.11 = (f32[256,128]{1,0:T(8,128)S(1)}, f32[256,128]{1,0:T(8,128)S(1)}, u32[]{:S(2)}, u32[]{:S(2)}) collective-permute-start(f32[256,128]{1,0:T(8,128)S(1)} %slice_add_fusion.6), channel_id=1, source_target_pairs={{16,24},{20,28},{8,0},{12,4},{17,25},{21,29},{9,1},{13,5},{18,26},... | collective-permute-start | bytes 393224 | tf_op jit(solution)/shard_map/ppermute | solution.py:204
  67.9 11.0 %collective-permute-start.18 = (f32[256,128]{1,0:T(8,128)S(1)}, f32[256,128]{1,0:T(8,128)S(1)}, u32[]{:S(2)}, u32[]{:S(2)}) collective-permute-start(f32[256,128]{1,0:T(8,128)S(1)} %slice_add_fusion.5), channel_id=1, source_target_pairs={{16,24},{20,28},{8,0},{12,4},{17,25},{21,29},{9,1},{13,5},{18,26},... | collective-permute-start | bytes 393224 | tf_op jit(solution)/shard_map/ppermute | solution.py:204
  73.5 5.7 %collective-permute-start.25 = (f32[256,128]{1,0:T(8,128)S(1)}, f32[256,128]{1,0:T(8,128)S(1)}, u32[]{:S(2)}, u32[]{:S(2)}) collective-permute-start(f32[256,128]{1,0:T(8,128)S(1)} %slice_add_fusion.4), channel_id=1, source_target_pairs={{16,24},{20,28},{8,0},{12,4},{17,25},{21,29},{9,1},{13,5},{18,26},... | collective-permute-start | bytes 393224 | tf_op jit(solution)/shard_map/ppermute | solution.py:204
  74.9 5.6 %collective-permute-start.5 = (f32[256,128]{1,0:T(8,128)S(1)}, f32[256,128]{1,0:T(8,128)S(1)}, u32[]{:S(2)}, u32[]{:S(2)}) collective-permute-start(f32[256,128]{1,0:T(8,128)S(1)} %fusion.3.refs_1_), channel_id=1, source_target_pairs={{0,1},{1,0},{2,3},{3,2},{4,5},{5,4},{6,7},{7,6},{8,9},{9,8},{10,11... | collective-permute-start | bytes 393224 | tf_op jit(solution)/shard_map/ppermute | solution.py:279
  77.2 5.1 %collective-permute-start.6 = (f32[256,128]{1,0:T(8,128)S(1)}, f32[256,128]{1,0:T(8,128)S(1)}, u32[]{:S(2)}, u32[]{:S(2)}) collective-permute-start(f32[256,128]{1,0:T(8,128)S(1)} %fusion.3.refs_1_), channel_id=1, source_target_pairs={{0,2},{1,3},{2,0},{3,1},{4,6},{5,7},{6,4},{7,5},{8,10},{9,11},{10,... | collective-permute-start | bytes 393224 | tf_op jit(solution)/shard_map/ppermute | solution.py:279
  78.5 7.9 %collective-permute-start.12 = (f32[256,128]{1,0:T(8,128)S(1)}, f32[256,128]{1,0:T(8,128)S(1)}, u32[]{:S(2)}, u32[]{:S(2)}) collective-permute-start(f32[256,128]{1,0:T(8,128)S(1)} %fusion.2.refs_2_), channel_id=1, source_target_pairs={{0,1},{1,0},{2,3},{3,2},{4,5},{5,4},{6,7},{7,6},{8,9},{9,8},{10,11... | collective-permute-start | bytes 393224 | tf_op jit(solution)/shard_map/ppermute | solution.py:279
  78.9 6.2 %collective-permute-start.13 = (f32[256,128]{1,0:T(8,128)S(1)}, f32[256,128]{1,0:T(8,128)S(1)}, u32[]{:S(2)}, u32[]{:S(2)}) collective-permute-start(f32[256,128]{1,0:T(8,128)S(1)} %fusion.2.refs_2_), channel_id=1, source_target_pairs={{0,2},{1,3},{2,0},{3,1},{4,6},{5,7},{6,4},{7,5},{8,10},{9,11},{10,... | collective-permute-start | bytes 393224 | tf_op jit(solution)/shard_map/ppermute | solution.py:279
  79.2 8.7 %collective-permute-start.20 = (f32[256,128]{1,0:T(8,128)S(1)}, f32[256,128]{1,0:T(8,128)S(1)}, u32[]{:S(2)}, u32[]{:S(2)}) collective-permute-start(f32[256,128]{1,0:T(8,128)S(1)} %fusion.1.refs_2_), channel_id=1, source_target_pairs={{0,2},{1,3},{2,0},{3,1},{4,6},{5,7},{6,4},{7,5},{8,10},{9,11},{10,... | collective-permute-start | bytes 393224 | tf_op jit(solution)/shard_map/ppermute | solution.py:279
  80.6 10.1 %collective-permute-start.27 = (f32[256,128]{1,0:T(8,128)S(1)}, f32[256,128]{1,0:T(8,128)S(1)}, u32[]{:S(2)}, u32[]{:S(2)}) collective-permute-start(f32[256,128]{1,0:T(8,128)S(1)} %fusion.refs_2_), channel_id=1, source_target_pairs={{0,2},{1,3},{2,0},{3,1},{4,6},{5,7},{6,4},{7,5},{8,10},{9,11},{10,... | collective-permute-start | bytes 393224 | tf_op jit(solution)/shard_map/ppermute | solution.py:279
  82.3 9.3 %collective-permute-start.7 = (f32[256,128]{1,0:T(8,128)S(1)}, f32[256,128]{1,0:T(8,128)S(1)}, u32[]{:S(2)}, u32[]{:S(2)}) collective-permute-start(f32[256,128]{1,0:T(8,128)S(1)} %collective-permute-done.6.refs_3_), channel_id=1, source_target_pairs={{0,1},{1,0},{2,3},{3,2},{4,5},{5,4},{6,7},{7,6},{8,9},{9,8},{10,11... | collective-permute-start | bytes 393224 | tf_op jit(solution)/shard_map/ppermute | solution.py:279
  85.1 10.4 %collective-permute-start.14 = (f32[256,128]{1,0:T(8,128)S(1)}, f32[256,128]{1,0:T(8,128)S(1)}, u32[]{:S(2)}, u32[]{:S(2)}) collective-permute-start(f32[256,128]{1,0:T(8,128)S(1)} %collective-permute-done.13.refs_4_), channel_id=1, source_target_pairs={{0,1},{1,0},{2,3},{3,2},{4,5},{5,4},{6,7},{7,6},{8,9},{9,8},{10,11... | collective-permute-start | bytes 393224 | tf_op jit(solution)/shard_map/ppermute | solution.py:279
  86.4 13.1 %collective-permute-start.19 = (f32[256,128]{1,0:T(8,128)S(1)}, f32[256,128]{1,0:T(8,128)S(1)}, u32[]{:S(2)}, u32[]{:S(2)}) collective-permute-start(f32[256,128]{1,0:T(8,128)S(1)} %fusion.1.refs_2_), channel_id=1, source_target_pairs={{0,1},{1,0},{2,3},{3,2},{4,5},{5,4},{6,7},{7,6},{8,9},{9,8},{10,11... | collective-permute-start | bytes 393224 | tf_op jit(solution)/shard_map/ppermute | solution.py:279
  87.9 11.6 %collective-permute-start.21 = (f32[256,128]{1,0:T(8,128)S(1)}, f32[256,128]{1,0:T(8,128)S(1)}, u32[]{:S(2)}, u32[]{:S(2)}) collective-permute-start(f32[256,128]{1,0:T(8,128)S(1)} %collective-permute-done.20.refs_4_), channel_id=1, source_target_pairs={{0,1},{1,0},{2,3},{3,2},{4,5},{5,4},{6,7},{7,6},{8,9},{9,8},{10,11... | collective-permute-start | bytes 393224 | tf_op jit(solution)/shard_map/ppermute | solution.py:279
  90.7 13.4 %collective-permute-start.26 = (f32[256,128]{1,0:T(8,128)S(1)}, f32[256,128]{1,0:T(8,128)S(1)}, u32[]{:S(2)}, u32[]{:S(2)}) collective-permute-start(f32[256,128]{1,0:T(8,128)S(1)} %fusion.refs_2_), channel_id=1, source_target_pairs={{0,1},{1,0},{2,3},{3,2},{4,5},{5,4},{6,7},{7,6},{8,9},{9,8},{10,11... | collective-permute-start | bytes 393224 | tf_op jit(solution)/shard_map/ppermute | solution.py:279
  91.6 12.5 %collective-permute-start.28 = (f32[256,128]{1,0:T(8,128)S(1)}, f32[256,128]{1,0:T(8,128)S(1)}, u32[]{:S(2)}, u32[]{:S(2)}) collective-permute-start(f32[256,128]{1,0:T(8,128)S(1)} %collective-permute-done.27.refs_4_), channel_id=1, source_target_pairs={{0,1},{1,0},{2,3},{3,2},{4,5},{5,4},{6,7},{7,6},{8,9},{9,8},{10,11... | collective-permute-start | bytes 393224 | tf_op jit(solution)/shard_map/ppermute | solution.py:279
  (31 other events, 251.2 us)

commit v2 on v0

--- a/solution.py
+++ b/solution.py
@@ -1,6 +1,9 @@
+import math
 import jax
 import jax.numpy as jnp
 from jax import lax
+from jax.experimental import pallas as pl
+from jax.experimental.pallas import tpu as pltpu
 from jax.sharding import PartitionSpec as P
 
 TILES_DEV = 128
@@ -8,9 +11,13 @@
 QDIR = 4
 ROWS = 8
 ANGLES = 2
-
-
-def local(strain, dest, det_row, dirs, rock_angles, resolution):
+LANES = 128
+GROUP = 8
+VMEM_LIMIT = 12 * 1024 * 1024
+SCALE = math.sqrt(0.5 / math.log(2.0))
+
+
+def by_tiles(strain, dest, det_row, dirs, rock_angles, resolution):
     slabs = lax.axis_size("slab")
     tiles_here = strain.shape[0]
     vox_here = strain.shape[2]
@@ -75,6 +82,237 @@
     )
 
 
+def image_kernel(count_ref, list_ref, dirs_ref, rock_ref, strain_ref, *rest):
+    proj = rest[-1]
+    comps, tiles, pix = strain_ref.shape
+    angles = count_ref.shape[0]
+    qcount = dirs_ref.shape[0] // (angles * comps)
+    rocks = rock_ref.shape[0]
+    step = 2 * GROUP
+    if len(rest) == 2:
+        init, outs = None, rest[:1]
+    else:
+        init, outs = rest[0], rest[1:-2]
+    acc = outs[0] if init is None else rest[-2]
+    blocks = pix // LANES
+    rows_out = acc.shape[0] // blocks
+    rock = rock_ref[...]
+    if init is None:
+        acc[...] = jnp.zeros_like(acc)
+    else:
+        acc[...] = init[...]
+
+    for b in range(blocks):
+        lanes = slice(b * LANES, (b + 1) * LANES)
+
+        @pl.loop(0, tiles // step)
+        def _(block):
+            rows = pl.ds(pl.multiple_of(block * step, step), step)
+            parts = [strain_ref[c, rows, lanes] for c in range(comps)]
+            for k in range(angles * qcount):
+                total = parts[0] * dirs_ref[k * comps]
+                for c in range(1, comps):
+                    total = total + parts[c] * dirs_ref[k * comps + c]
+                proj[k, rows, :] = total
+
+        for angle in range(angles):
+
+            @pl.loop(0, (count_ref[angle] + GROUP - 1) // GROUP)
+            def _(block):
+                sums = []
+                targets = []
+                for j in range(GROUP):
+                    code = list_ref[angle, block * GROUP + j]
+                    tile = code & (tiles - 1)
+                    target = (code >> (tiles - 1).bit_length()) * rocks
+                    targets.append(pl.multiple_of(target + b * rows_out, rocks))
+                    total = None
+                    for q in range(qcount):
+                        p = proj[angle * qcount + q, pl.ds(tile, 1), :]
+                        d = jnp.broadcast_to(p, (rocks, LANES)) - rock
+                        e = jnp.exp2(-(d * d))
+                        total = e if total is None else total + e
+                    sums.append(total)
+                for target, total in zip(targets, sums):
+                    acc[pl.ds(target, rocks), :] += total
+
+    if init is not None:
+        start = 0
+        for out in outs:
+            out[...] = acc[pl.ds(start, out.shape[0]), :]
+            start += out.shape[0]
+
+
+def add_images(name, listing, weights, rock, strain, init, sizes, cost):
+    counts, lists = listing
+    comps, tiles, pix = strain.shape
+    angles = counts.shape[0]
+    qcount = weights.shape[0] // (angles * comps)
+    smem = pl.BlockSpec(memory_space=pltpu.SMEM)
+    vmem = pl.BlockSpec(memory_space=pltpu.VMEM)
+    scratch = [pltpu.VMEM((angles * qcount, tiles, LANES), jnp.float32)]
+    before = ()
+    if init is not None:
+        before = (init,)
+        scratch = [pltpu.VMEM(init.shape, jnp.float32)] + scratch
+    return pl.pallas_call(
+        image_kernel,
+        out_shape=tuple(jax.ShapeDtypeStruct((size, LANES), jnp.float32) for size in sizes),
+        in_specs=[smem, smem, smem] + [vmem] * (2 + len(before)),
+        out_specs=tuple(vmem for size in sizes),
+        scratch_shapes=scratch,
+        compiler_params=pltpu.CompilerParams(vmem_limit_bytes=VMEM_LIMIT),
+        cost_estimate=pl.CostEstimate(flops=cost, bytes_accessed=1_000_000, transcendentals=0),
+        name=name,
+    )(counts, lists, weights, rock, strain, *before)
+
+
+def resolve(rock_index, firsts, pix, norm, total, resolution, parts):
+    count = len(firsts)
+    unit = parts[0].shape[0] // count
+    lanes = parts[0].shape[1]
+    cols = resolution.shape[1]
+    smem = pl.BlockSpec(memory_space=pltpu.SMEM)
+    vmem = pl.BlockSpec(memory_space=pltpu.VMEM)
+
+    def kernel(rock_ref, res_ref, *refs):
+        part_refs, out_ref = refs[: len(parts)], refs[-1]
+        values = []
+        blocks = []
+        for j, part in enumerate(part_refs):
+            for c, first in enumerate(firsts):
+                start = pl.multiple_of((rock_ref[0] ^ j) * pix + first, lanes)
+                blocks.append(res_ref[pl.ds(start, lanes), :])
+                values.append(part[pl.ds(c * unit, unit), :] * norm)
+        block = jnp.concatenate(blocks, axis=0)
+        value = jnp.concatenate(values, axis=1)
+        high = value.astype(jnp.bfloat16)
+        low = (value - high.astype(jnp.float32)).astype(jnp.bfloat16)
+        result = jnp.dot(high, block, preferred_element_type=jnp.float32) + jnp.dot(
+            low, block, preferred_element_type=jnp.float32
+        )
+        if total is not None:
+            result = result + refs[len(parts)][...]
+        out_ref[...] = result
+
+    before = () if total is None else (total,)
+    return pl.pallas_call(
+        kernel,
+        out_shape=jax.ShapeDtypeStruct((unit, cols), jnp.float32),
+        in_specs=[smem] + [vmem] * (1 + len(parts) + len(before)),
+        out_specs=vmem,
+        compiler_params=pltpu.CompilerParams(vmem_limit_bytes=VMEM_LIMIT),
+        cost_estimate=pl.CostEstimate(flops=500_000_000, bytes_accessed=1_000_000, transcendentals=0),
+        name="resolve",
+    )(rock_index, resolution, *parts, *before)
+
+
+def bit(value, number):
+    return (value >> number) & 1
+
+
+def listing(info, me, raw, halves, angles, units):
+    tiles = info.shape[1]
+    owner = info // ROWS
+    keep = bit(owner, raw) == bit(me, raw)
+    position = jnp.zeros_like(owner)
+    for number in halves:
+        position = 2 * position + (bit(owner, number) == bit(me, number)).astype(jnp.int32)
+    target = (position * angles + jnp.arange(angles)[:, None]) * ROWS + info % ROWS
+    number = jnp.arange(tiles)
+    earlier = keep[:, None, :] & (number[None, None, :] < number[None, :, None])
+    rank = jnp.where(keep, jnp.sum(earlier.astype(jnp.int32), axis=2), -1)
+    code = number[None, :] + tiles * (target - units)
+    lists = tiles * units + jnp.sum(
+        jnp.where(rank[:, None, :] == number[None, :, None], code[:, None, :], 0), axis=2
+    )
+    return jnp.sum(keep.astype(jnp.int32), axis=1), lists
+
+
+def by_images(strain, dest, det_row, dirs, rock_angles, resolution):
+    slabs = lax.axis_size("slab")
+    rock_size = lax.axis_size("rock")
+    tiles = strain.shape[0]
+    pix = resolution.shape[1]
+    rocks = rock_angles.shape[0]
+    angles, qcount, comps = dirs.shape
+    norm = ROWS / (QDIR * DEPTH * TILES_DEV)
+    bits = slabs.bit_length() - 1
+    unit = angles * ROWS * rocks
+    units = slabs // 2 * angles * ROWS
+    image_rows = units * rocks
+    me = lax.axis_index("slab")
+    chunks = pix // LANES
+
+    def swap(value, number, axis="slab"):
+        size = lax.axis_size(axis)
+        return lax.ppermute(value, axis, [(i, i ^ (1 << number)) for i in range(size)])
+
+    plans = [(0, tuple(range(1, bits))), (1, (0,) + tuple(range(2, bits)))]
+    plan_of = [0] * (chunks - 1) + [1] if chunks > 1 else [0]
+    order = sorted(range(chunks), key=lambda c: -plan_of[c])
+
+    by_comp = strain.transpose(1, 0, 2)
+    own = [by_comp[:, :, c * LANES : (c + 1) * LANES] for c in range(chunks)]
+    info = dest[:, :, 0] * ROWS + det_row
+    other = {c: swap(own[c], plans[plan_of[c]][0]) for c in order}
+    used = sorted(set(plan_of))
+    other_info = {k: swap(info, plans[k][0]) for k in used}
+    own_list = {k: listing(info, me, *plans[k], angles, units) for k in used}
+    other_list = {k: listing(other_info[k], me, *plans[k], angles, units) for k in used}
+
+    weights = (dirs * SCALE).reshape(-1)
+    rock = jnp.broadcast_to((rock_angles * SCALE)[:, None], (rocks, LANES))
+    rock_index = lax.axis_index("rock").reshape(1)
+
+    partial = {}
+    for c in order:
+        (partial[c],) = add_images(
+            "own_images", own_list[plan_of[c]], weights, rock, own[c], None, [image_rows + rocks], 3_000_000
+        )
+
+    image = {}
+    for c in order:
+        k = plan_of[c]
+        held = image_rows // 2
+        sent, kept = add_images(
+            "other_images", other_list[k], weights, rock, other[c], partial[c], [held, held], 3_000_000
+        )
+        for number in plans[k][1]:
+            arrived = swap(sent, number)
+            if held > unit:
+                held = held // 2
+                sent, kept = kept[:held] + arrived[:held], kept[held:] + arrived[held:]
+            else:
+                image[c] = kept + arrived
+
+    def gather(value):
+        parts = [value]
+        for number in reversed(range(rock_size.bit_length() - 1)):
+            parts = [x for part in parts for x in (part, swap(part, number, "rock"))]
+        return parts
+
+    groups = [order[:-1], order[-1:]]
+    result = None
+    for group in groups:
+        value = jnp.concatenate([image[c] for c in group], axis=0) if len(group) > 1 else image[group[0]]
+        result = resolve(rock_index, [c * LANES for c in group], pix, norm, result, resolution, gather(value))
+    return result.reshape(angles, ROWS, rocks, pix)
+
+
+def local(strain, dest, det_row, dirs, rock_angles, resolution):
+    slabs = lax.axis_size("slab")
+    rock_size = lax.axis_size("rock")
+    tiles, unused, vox = strain.shape
+    pix = resolution.shape[1]
+    slots = slabs * (2 * tiles // slabs)
+    images_smaller = slabs * ROWS * rock_angles.shape[0] * pix <= slots * dirs.shape[1] * vox
+    powers = all(size & (size - 1) == 0 for size in (slabs, rock_size, tiles))
+    regular = powers and slabs >= 4 and tiles % (2 * GROUP) == 0 and vox == pix and pix % LANES == 0
+    plan = by_images if images_smaller and regular else by_tiles
+    return plan(strain, dest, det_row, dirs, rock_angles, resolution)
+
+
 def solution(mesh):
     placed = (
         P("slab", None, "rock"),

time: 221 us -> 78.5 us (0.36)
  local copies, waits for them, and re-layouts: 64.5 us -> 1.67 us
  matrix products: 31.4 us -> 0 us
  waiting for transfers between devices: 66.4 us -> 35.6 us
  other arithmetic: 21.1 us -> 2.12 us
  Pallas kernels: 0 us -> 18.1 us
  between operations: 13.5 us -> 0.21 us
    all_to_all x4 -> x0, waiting for transfers between devices: 44.6 us -> none  [the longest x2 39.8 us: local(): lax.all_to_all(outgoing, 'slab', split_axis=0, concat_axis=0, tiled=True)]
    ppermute x0 -> x20, waiting for transfers between devices: none -> 35.6 us  [swap(): lax.ppermute(value, axis, [(i, i ^ 1 << number) for i in range(size)])]
    dot_general x11 -> x0, matrix products: 31.4 us -> none  [the longest x8 18.9 us: add_block(): jnp.dot(onehot, summed.reshape(block_size, rocks * pix_here), precision=l...]
    scatter x4 -> x0, local copies, waits for them, and re-layouts: 29.4 us -> none  [the longest x2 27.4 us: local(): jnp.zeros((slots, qcount, vox_here), jnp.float32).at[slot].set(local_proj)]
    all_gather x1 -> x0, waiting for transfers between devices: 21.8 us -> none  [local(): lax.all_gather(stacked, 'rock', axis=3, tiled=True)]
    all_to_all x4 -> x0, starting transfers between devices: 21.1 us -> none  [the longest x2 10.6 us: local(): lax.all_to_all(row_send, 'slab', split_axis=0, concat_axis=0, tiled=True)]
    ppermute x0 -> x20, starting transfers between devices: none -> 20.6 us  [swap(): lax.ppermute(value, axis, [(i, i ^ 1 << number) for i in range(size)])]
    while x8 -> x0, local copies, waits for them, and re-layouts: 20.1 us -> none
  transfers between devices with their start and end apart: 5 -> 20, of which waited for: 4 -> 9; matrix products, arithmetic and copies ran while one was open for 34% -> 4% of each run, Pallas kernels for 0% -> 20%
where the time goes in v2:
time: 78.5 us; the launch traced here: 78.3 us
  waiting for transfers between devices  35.6 us (45%)
  starting transfers between devices  20.6 us (26%)
  Pallas kernels  18.1 us (23%)
  other arithmetic  2.12 us (3%)
  local copies, waits for them, and re-layouts  1.67 us (2%)
    ppermute x20, waiting for transfers between devices, swap(): lax.ppermute(value, axis, [(i, i ^ 1 << number) for i in range(size)])  35.6 us
    ppermute x20, starting transfers between devices, swap(): lax.ppermute(value, axis, [(i, i ^ 1 << number) for i in range(size)])  20.6 us
    pallas_call x8, Pallas kernels, add_images(): pl.pallas_call(image_kernel, out_shape=tuple((jax.ShapeDtypeStruct((size,...  13.9 us
    pallas_call x2, Pallas kernels, resolve(): pl.pallas_call(kernel, out_shape=jax.ShapeDtypeStruct((unit, cols), jnp.f...  4.18 us
  transfers between devices with their start and end apart: 20, of which 9 were waited for; matrix products, arithmetic and copies ran while one was open for 4% of the time, Pallas kernels for 20%

profile of v2, /device:TPU:0, one launch (start us, length us, event | category | flops | bytes accessed | tf_op | source)
XLA Modules:
  0.0 78.3 jit_solution(13454669177945733632)
XLA Ops:
  0.0 0.7 multiply_add_fusion
  0.7 3.1 %collective-permute-start.7 = (s32[2,128]{1,0:T(2,128)S(1)}, s32[2,128]{1,0:T(2,128)S(1)}, u32[]{:S(2)}, u32[]{:S(2)}) collective-permute-start(s32[2,128]{1,0:T(2,128)S(1)} %get-tuple-element.28), channel_id=1, source_target_pairs={{0,8},{4,12},{8,0},{12,4},{16,24},{20,28},{24,16},{28,20},{1,9},{5... | collective-permute-start | bytes 3080 | tf_op jit(solution)/shard_map/ppermute | solution.py:249
  3.8 1.5 %collective-permute-start = (s32[2,128]{1,0:T(2,128)S(1)}, s32[2,128]{1,0:T(2,128)S(1)}, u32[]{:S(2)}, u32[]{:S(2)}) collective-permute-start(s32[2,128]{1,0:T(2,128)S(1)} %get-tuple-element.28), channel_id=1, source_target_pairs={{0,4},{4,0},{8,12},{12,8},{16,20},{20,16},{24,28},{28,24},{1,5},{5... | collective-permute-start | bytes 3080 | tf_op jit(solution)/shard_map/ppermute | solution.py:249
  5.3 1.5 %fusion.12 = (f32[6,128,128]{2,1,0:T(8,128)S(1)}, f32[6,128,128]{2,1,0:T(8,128)S(1)}, f32[6,128,128]{2,1,0:T(8,128)S(1)}, f32[6,128,128]{2,1,0:T(8,128)S(1)}) fusion(f32[6,128,512]{2,1,0:T(8,128)} %bitcast.7), kind=kLoop, calls=%fused_computation.83 | loop fusion | bytes 3145728 | tf_op jit(solution)/shard_map/slice | solution.py:256
  6.8 0.5 collective-permute-start.8
  7.5 1.9 %collective-permute-start.14 = (f32[6,128,128]{2,1,0:T(8,128)S(1)}, f32[6,128,128]{2,1,0:T(8,128)S(1)}, u32[]{:S(2)}, u32[]{:S(2)}) collective-permute-start(f32[6,128,128]{2,1,0:T(8,128)S(1)} %get-tuple-element.40.strain_ref), channel_id=1, source_target_pairs={{0,4},{4,0},{8,12},{12,8},{16,20},{20,16},{24,28},{28,24},{1,5},{5... | collective-permute-start | bytes 1179656 | tf_op jit(solution)/shard_map/ppermute | solution.py:249
  10.9 2.0 %own_images.5.rest_0_ = f32[1040,128]{1,0:T(8,128)S(1)} custom-call(s32[2]{0:T(128)S(1)} %get-tuple-element.29.count_ref, s32[2,128]{1,0:T(2,128)S(1)} %broadcast_add_fusion.list_ref, f32[48]{0:T(128)S(1)} %reshape.40.dirs_ref, f32[16,128]{1,0:T(8,128)S(1)} %broadcast_in_dim.39.rock_ref, f32[6,128,128]{2,1,0:T(8,128)S(1)} %get-tuple-element.39.strain_ref), custom_call_target="tpu_custom_call" | custom-call | flops 3000000 | bytes 1000000 | tf_op jit(solution)/shard_map/own_images/pallas_call | solution.py:158
  12.9 4.3 %collective-permute-done.8.strain_ref = f32[6,128,128]{2,1,0:T(8,128)S(1)} collective-permute-done((f32[6,128,128]{2,1,0:T(8,128)S(1)}, f32[6,128,128]{2,1,0:T(8,128)S(1)}, u32[]{:S(2)}, u32[]{:S(2)}) %collective-permute-start.8) | collective-permute-done | bytes 393248 | tf_op jit(solution)/shard_map/ppermute | solution.py:249
  17.2 2.0 %other_images.5 = (f32[512,128]{1,0:T(8,128)S(1)}, f32[512,128]{1,0:T(8,128)S(1)}) custom-call(s32[2]{0:T(128)S(1)} %get-tuple-element.33.count_ref, s32[2,128]{1,0:T(2,128)S(1)} %broadcast_add_fusion.1.list_ref, f32[48]{0:T(128)S(1)} %reshape.40.dirs_ref, f32[16,128]{1,0:T(8,128)S(1)} %broadcast_in_dim.39.rock_ref, ...), custom_call_target="tpu_custom_call" | custom-call | flops 3000000 | bytes 1000000 | tf_op jit(solution)/shard_map/other_images/pallas_call | solution.py:158
  19.2 0.6 collective-permute-start.9
  19.9 1.6 %own_images.6.rest_0_ = f32[1040,128]{1,0:T(8,128)S(1)} custom-call(s32[2]{0:T(128)S(1)} %get-tuple-element.47.count_ref, s32[2,128]{1,0:T(2,128)S(1)} %broadcast_add_fusion.2.list_ref, f32[48]{0:T(128)S(1)} %reshape.40.dirs_ref, f32[16,128]{1,0:T(8,128)S(1)} %broadcast_in_dim.39.rock_ref, f32[6,128,128]{2,1,0:T(8,128)S(1)} %get-tuple-element.41.strain_ref), custom_call_target="tpu_custom_call" | custom-call | flops 3000000 | bytes 1000000 | tf_op jit(solution)/shard_map/own_images/pallas_call | solution.py:158
  21.5 1.7 %other_images.6 = (f32[512,128]{1,0:T(8,128)S(1)}, f32[512,128]{1,0:T(8,128)S(1)}) custom-call(s32[2]{0:T(128)S(1)} %get-tuple-element.37.count_ref, s32[2,128]{1,0:T(2,128)S(1)} %broadcast_add_fusion.3.list_ref, f32[48]{0:T(128)S(1)} %reshape.40.dirs_ref, f32[16,128]{1,0:T(8,128)S(1)} %broadcast_in_dim.39.rock_ref, ...), custom_call_target="tpu_custom_call" | custom-call | flops 3000000 | bytes 1000000 | tf_op jit(solution)/shard_map/other_images/pallas_call | solution.py:158
  23.5 1.6 %own_images.7.rest_0_ = f32[1040,128]{1,0:T(8,128)S(1)} custom-call(s32[2]{0:T(128)S(1)} %get-tuple-element.47.count_ref, s32[2,128]{1,0:T(2,128)S(1)} %broadcast_add_fusion.2.list_ref, f32[48]{0:T(128)S(1)} %reshape.40.dirs_ref, f32[16,128]{1,0:T(8,128)S(1)} %broadcast_in_dim.39.rock_ref, f32[6,128,128]{2,1,0:T(8,128)S(1)} %get-tuple-element.40.strain_ref), custom_call_target="tpu_custom_call" | custom-call | flops 3000000 | bytes 1000000 | tf_op jit(solution)/shard_map/own_images/pallas_call | solution.py:158
  25.1 1.6 %own_images.4.rest_0_ = f32[1040,128]{1,0:T(8,128)S(1)} custom-call(s32[2]{0:T(128)S(1)} %get-tuple-element.47.count_ref, s32[2,128]{1,0:T(2,128)S(1)} %broadcast_add_fusion.2.list_ref, f32[48]{0:T(128)S(1)} %reshape.40.dirs_ref, f32[16,128]{1,0:T(8,128)S(1)} %broadcast_in_dim.39.rock_ref, f32[6,128,128]{2,1,0:T(8,128)S(1)} %get-tuple-element.42.strain_ref), custom_call_target="tpu_custom_call" | custom-call | flops 3000000 | bytes 1000000 | tf_op jit(solution)/shard_map/own_images/pallas_call | solution.py:158
  26.7 1.1 %collective-permute-done.14.strain_ref = f32[6,128,128]{2,1,0:T(8,128)S(1)} collective-permute-done((f32[6,128,128]{2,1,0:T(8,128)S(1)}, f32[6,128,128]{2,1,0:T(8,128)S(1)}, u32[]{:S(2)}, u32[]{:S(2)}) %collective-permute-start.14) | collective-permute-done | bytes 393248 | tf_op jit(solution)/shard_map/ppermute | solution.py:249
  27.8 1.7 %other_images.7 = (f32[512,128]{1,0:T(8,128)S(1)}, f32[512,128]{1,0:T(8,128)S(1)}) custom-call(s32[2]{0:T(128)S(1)} %get-tuple-element.37.count_ref, s32[2,128]{1,0:T(2,128)S(1)} %broadcast_add_fusion.3.list_ref, f32[48]{0:T(128)S(1)} %reshape.40.dirs_ref, f32[16,128]{1,0:T(8,128)S(1)} %broadcast_in_dim.39.rock_ref, ...), custom_call_target="tpu_custom_call" | custom-call | flops 3000000 | bytes 1000000 | tf_op jit(solution)/shard_map/other_images/pallas_call | solution.py:158
  29.6 1.6 %collective-permute-start.15 = (f32[512,128]{1,0:T(8,128)S(1)}, f32[512,128]{1,0:T(8,128)S(1)}, u32[]{:S(2)}, u32[]{:S(2)}) collective-permute-start(f32[512,128]{1,0:T(8,128)S(1)} %get-tuple-element.20), channel_id=1, source_target_pairs={{0,8},{4,12},{8,0},{12,4},{16,24},{20,28},{24,16},{28,20},{1,9},{5... | collective-permute-start | bytes 786440 | tf_op jit(solution)/shard_map/ppermute | solution.py:249
  31.1 5.1 %collective-permute-done.1.strain_ref = f32[6,128,128]{2,1,0:T(8,128)S(1)} collective-permute-done((f32[6,128,128]{2,1,0:T(8,128)S(1)}, f32[6,128,128]{2,1,0:T(8,128)S(1)}, u32[]{:S(2)}, u32[]{:S(2)}) %collective-permute-start.1) | collective-permute-done | bytes 393248 | tf_op jit(solution)/shard_map/ppermute | solution.py:249
  36.3 1.7 %other_images.4 = (f32[512,128]{1,0:T(8,128)S(1)}, f32[512,128]{1,0:T(8,128)S(1)}) custom-call(s32[2]{0:T(128)S(1)} %get-tuple-element.37.count_ref, s32[2,128]{1,0:T(2,128)S(1)} %broadcast_add_fusion.3.list_ref, f32[48]{0:T(128)S(1)} %reshape.40.dirs_ref, f32[16,128]{1,0:T(8,128)S(1)} %broadcast_in_dim.39.rock_ref, ...), custom_call_target="tpu_custom_call" | custom-call | flops 3000000 | bytes 1000000 | tf_op jit(solution)/shard_map/other_images/pallas_call | solution.py:158
  38.0 1.6 %collective-permute-start.2 = (f32[512,128]{1,0:T(8,128)S(1)}, f32[512,128]{1,0:T(8,128)S(1)}, u32[]{:S(2)}, u32[]{:S(2)}) collective-permute-start(f32[512,128]{1,0:T(8,128)S(1)} %get-tuple-element.14), channel_id=1, source_target_pairs={{0,8},{4,12},{8,0},{12,4},{16,24},{20,28},{24,16},{28,20},{1,9},{5... | collective-permute-start | bytes 786440 | tf_op jit(solution)/shard_map/ppermute | solution.py:249
  39.9 2.7 %collective-permute-start.10 = (f32[256,128]{1,0:T(8,128)S(1)}, f32[256,128]{1,0:T(8,128)S(1)}, u32[]{:S(2)}, u32[]{:S(2)}) collective-permute-start(f32[256,128]{1,0:T(8,128)S(1)} %slice_add_fusion.4), channel_id=1, source_target_pairs={{0,16},{4,20},{8,24},{12,28},{16,0},{20,4},{24,8},{28,12},{1,17},{... | collective-permute-start | bytes 393224 | tf_op jit(solution)/shard_map/ppermute | solution.py:249
  42.5 0.4 collective-permute-start.13
  43.0 2.7 %collective-permute-start.16 = (f32[256,128]{1,0:T(8,128)S(1)}, f32[256,128]{1,0:T(8,128)S(1)}, u32[]{:S(2)}, u32[]{:S(2)}) collective-permute-start(f32[256,128]{1,0:T(8,128)S(1)} %slice_add_fusion), channel_id=1, source_target_pairs={{0,16},{4,20},{8,24},{12,28},{16,0},{20,4},{24,8},{28,12},{1,17},{... | collective-permute-start | bytes 393224 | tf_op jit(solution)/shard_map/ppermute | solution.py:249
  45.6 8.7 %collective-permute-done.10 = f32[256,128]{1,0:T(8,128)S(1)} collective-permute-done((f32[256,128]{1,0:T(8,128)S(1)}, f32[256,128]{1,0:T(8,128)S(1)}, u32[]{:S(2)}, u32[]{:S(2)}) %collective-permute-start.10) | collective-permute-done | bytes 131104 | tf_op jit(solution)/shard_map/ppermute | solution.py:249
  54.3 2.6 %collective-permute-done.13 = f32[256,128]{1,0:T(8,128)S(1)} collective-permute-done((f32[256,128]{1,0:T(8,128)S(1)}, f32[256,128]{1,0:T(8,128)S(1)}, u32[]{:S(2)}, u32[]{:S(2)}) %collective-permute-start.13) | collective-permute-done | bytes 131104 | tf_op jit(solution)/shard_map/ppermute | solution.py:249
  57.0 1.4 %collective-permute-done.16 = f32[256,128]{1,0:T(8,128)S(1)} collective-permute-done((f32[256,128]{1,0:T(8,128)S(1)}, f32[256,128]{1,0:T(8,128)S(1)}, u32[]{:S(2)}, u32[]{:S(2)}) %collective-permute-start.16) | collective-permute-done | bytes 131104 | tf_op jit(solution)/shard_map/ppermute | solution.py:249
  58.4 1.6 %collective-permute-start.18 = (f32[768,128]{1,0:T(8,128)S(1)}, f32[768,128]{1,0:T(8,128)S(1)}, u32[]{:S(2)}, u32[]{:S(2)}) collective-permute-start(f32[768,128]{1,0:T(8,128)S(1)} %pad_maximum_fusion.refs_0_), channel_id=1, source_target_pairs={{0,2},{1,3},{2,0},{3,1},{4,6},{5,7},{6,4},{7,5},{8,10},{9,11},{10,... | collective-permute-start | bytes 1179656 | tf_op jit(solution)/shard_map/ppermute | solution.py:249
  60.1 7.9 %collective-permute-done.18.refs_2_ = f32[768,128]{1,0:T(8,128)S(1)} collective-permute-done((f32[768,128]{1,0:T(8,128)S(1)}, f32[768,128]{1,0:T(8,128)S(1)}, u32[]{:S(2)}, u32[]{:S(2)}) %collective-permute-start.18) | collective-permute-done | bytes 393248 | tf_op jit(solution)/shard_map/ppermute | solution.py:249
  68.1 1.6 %collective-permute-start.5 = (f32[256,128]{1,0:T(8,128)S(1)}, f32[256,128]{1,0:T(8,128)S(1)}, u32[]{:S(2)}, u32[]{:S(2)}) collective-permute-start(f32[256,128]{1,0:T(8,128)S(1)} %fusion.3.refs_0_), channel_id=1, source_target_pairs={{0,2},{1,3},{2,0},{3,1},{4,6},{5,7},{6,4},{7,5},{8,10},{9,11},{10,... | collective-permute-start | bytes 393224 | tf_op jit(solution)/shard_map/ppermute | solution.py:249
  69.9 4.2 %collective-permute-done.5.refs_2_ = f32[256,128]{1,0:T(8,128)S(1)} collective-permute-done((f32[256,128]{1,0:T(8,128)S(1)}, f32[256,128]{1,0:T(8,128)S(1)}, u32[]{:S(2)}, u32[]{:S(2)}) %collective-permute-start.5) | collective-permute-done | bytes 131104 | tf_op jit(solution)/shard_map/ppermute | solution.py:249
  74.1 2.0 %resolve.2.refs_4_ = f32[256,512]{1,0:T(8,128)S(1)} custom-call(s32[1]{0:T(128)} %bitcast.rock_ref, bf16[2048,512]{1,0:T(8,128)(2,1)S(1)} %copy-done, f32[768,128]{1,0:T(8,128)S(1)} %pad_maximum_fusion.refs_0_, f32[768,128]{1,0:T(8,128)S(1)} %collective-permute-done.17.refs_1_, f32[768,128]{1,0:T(8,128)S(1)} %collective-permute-done.18.refs_2_, ...), custom_call_target="tpu_custom_call" | custom-call | flops 500000000 | bytes 1000000 | tf_op jit(solution)/shard_map/resolve/pallas_call | solution.py:199
  76.1 2.2 %resolve.3 = f32[256,512]{1,0:T(8,128)} custom-call(s32[1]{0:T(128)} %bitcast.rock_ref, bf16[2048,512]{1,0:T(8,128)(2,1)S(1)} %copy-done, f32[256,128]{1,0:T(8,128)S(1)} %fusion.3.refs_0_, f32[256,128]{1,0:T(8,128)} %collective-permute-done.4.refs_1_, f32[256,128]{1,0:T(8,128)S(1)} %collective-permute-done.5.refs_2_, ...), custom_call_target="tpu_custom_call" | custom-call | flops 500000000 | bytes 1000000 | tf_op jit(solution)/shard_map/resolve/pallas_call | solution.py:199
  (56 shorter events, 2.9 us)
Async XLA Ops:
  0.7 8.9 %collective-permute-start.7 = (s32[2,128]{1,0:T(2,128)S(1)}, s32[2,128]{1,0:T(2,128)S(1)}, u32[]{:S(2)}, u32[]{:S(2)}) collective-permute-start(s32[2,128]{1,0:T(2,128)S(1)} %get-tuple-element.28), channel_id=1, source_target_pairs={{0,8},{4,12},{8,0},{12,4},{16,24},{20,28},{24,16},{28,20},{1,9},{5... | collective-permute-start | bytes 3080 | tf_op jit(solution)/shard_map/ppermute | solution.py:249
  3.8 6.2 %collective-permute-start = (s32[2,128]{1,0:T(2,128)S(1)}, s32[2,128]{1,0:T(2,128)S(1)}, u32[]{:S(2)}, u32[]{:S(2)}) collective-permute-start(s32[2,128]{1,0:T(2,128)S(1)} %get-tuple-element.28), channel_id=1, source_target_pairs={{0,4},{4,0},{8,12},{12,8},{16,20},{20,16},{24,28},{28,24},{1,5},{5... | collective-permute-start | bytes 3080 | tf_op jit(solution)/shard_map/ppermute | solution.py:249
  5.3 4.0 %copy-start.2 = (f32[16]{0:T(128)S(1)}, f32[16]{0:T(128)}, u32[]{:S(2)}) copy-start(f32[16]{0:T(128)} %param.10) | copy-start | bytes 196
  5.3 4.1 %copy-start.1 = (f32[2,4,6]{2,1,0:T(4,128)S(1)}, f32[2,4,6]{2,1,0:T(4,128)}, u32[]{:S(2)}) copy-start(f32[2,4,6]{2,1,0:T(4,128)} %param.9) | copy-start | bytes 580
  6.8 10.4 %collective-permute-start.8 = (f32[6,128,128]{2,1,0:T(8,128)S(1)}, f32[6,128,128]{2,1,0:T(8,128)S(1)}, u32[]{:S(2)}, u32[]{:S(2)}) collective-permute-start(f32[6,128,128]{2,1,0:T(8,128)S(1)} %get-tuple-element.39.strain_ref), channel_id=1, source_target_pairs={{0,8},{4,12},{8,0},{12,4},{16,24},{20,28},{24,16},{28,20},{1,9},{5... | collective-permute-start | bytes 1179656 | tf_op jit(solution)/shard_map/ppermute | solution.py:249
  7.3 14.1 %collective-permute-start.11 = (f32[6,128,128]{2,1,0:T(8,128)S(1)}, f32[6,128,128]{2,1,0:T(8,128)S(1)}, u32[]{:S(2)}, u32[]{:S(2)}) collective-permute-start(f32[6,128,128]{2,1,0:T(8,128)S(1)} %get-tuple-element.41.strain_ref), channel_id=1, source_target_pairs={{0,4},{4,0},{8,12},{12,8},{16,20},{20,16},{24,28},{28,24},{1,5},{5... | collective-permute-start | bytes 1179656 | tf_op jit(solution)/shard_map/ppermute | solution.py:249
  7.5 20.3 %collective-permute-start.14 = (f32[6,128,128]{2,1,0:T(8,128)S(1)}, f32[6,128,128]{2,1,0:T(8,128)S(1)}, u32[]{:S(2)}, u32[]{:S(2)}) collective-permute-start(f32[6,128,128]{2,1,0:T(8,128)S(1)} %get-tuple-element.40.strain_ref), channel_id=1, source_target_pairs={{0,4},{4,0},{8,12},{12,8},{16,20},{20,16},{24,28},{28,24},{1,5},{5... | collective-permute-start | bytes 1179656 | tf_op jit(solution)/shard_map/ppermute | solution.py:249
  9.6 26.6 %collective-permute-start.1 = (f32[6,128,128]{2,1,0:T(8,128)S(1)}, f32[6,128,128]{2,1,0:T(8,128)S(1)}, u32[]{:S(2)}, u32[]{:S(2)}) collective-permute-start(f32[6,128,128]{2,1,0:T(8,128)S(1)} %get-tuple-element.42.strain_ref), channel_id=1, source_target_pairs={{0,4},{4,0},{8,12},{12,8},{16,20},{20,16},{24,28},{28,24},{1,5},{5... | collective-permute-start | bytes 1179656 | tf_op jit(solution)/shard_map/ppermute | solution.py:249
  19.2 20.6 %collective-permute-start.9 = (f32[512,128]{1,0:T(8,128)S(1)}, f32[512,128]{1,0:T(8,128)S(1)}, u32[]{:S(2)}, u32[]{:S(2)}) collective-permute-start(f32[512,128]{1,0:T(8,128)S(1)} %get-tuple-element.16), channel_id=1, source_target_pairs={{0,4},{4,0},{8,12},{12,8},{16,20},{20,16},{24,28},{28,24},{1,5},{5... | collective-permute-start | bytes 786440 | tf_op jit(solution)/shard_map/ppermute | solution.py:249
  23.2 19.3 %collective-permute-start.12 = (f32[512,128]{1,0:T(8,128)S(1)}, f32[512,128]{1,0:T(8,128)S(1)}, u32[]{:S(2)}, u32[]{:S(2)}) collective-permute-start(f32[512,128]{1,0:T(8,128)S(1)} %get-tuple-element.18), channel_id=1, source_target_pairs={{0,8},{4,12},{8,0},{12,4},{16,24},{20,28},{24,16},{28,20},{1,9},{5... | collective-permute-start | bytes 786440 | tf_op jit(solution)/shard_map/ppermute | solution.py:249
  29.6 13.4 %collective-permute-start.15 = (f32[512,128]{1,0:T(8,128)S(1)}, f32[512,128]{1,0:T(8,128)S(1)}, u32[]{:S(2)}, u32[]{:S(2)}) collective-permute-start(f32[512,128]{1,0:T(8,128)S(1)} %get-tuple-element.20), channel_id=1, source_target_pairs={{0,8},{4,12},{8,0},{12,4},{16,24},{20,28},{24,16},{28,20},{1,9},{5... | collective-permute-start | bytes 786440 | tf_op jit(solution)/shard_map/ppermute | solution.py:249
  38.0 22.0 %collective-permute-start.2 = (f32[512,128]{1,0:T(8,128)S(1)}, f32[512,128]{1,0:T(8,128)S(1)}, u32[]{:S(2)}, u32[]{:S(2)}) collective-permute-start(f32[512,128]{1,0:T(8,128)S(1)} %get-tuple-element.14), channel_id=1, source_target_pairs={{0,8},{4,12},{8,0},{12,4},{16,24},{20,28},{24,16},{28,20},{1,9},{5... | collective-permute-start | bytes 786440 | tf_op jit(solution)/shard_map/ppermute | solution.py:249
  39.9 14.4 %collective-permute-start.10 = (f32[256,128]{1,0:T(8,128)S(1)}, f32[256,128]{1,0:T(8,128)S(1)}, u32[]{:S(2)}, u32[]{:S(2)}) collective-permute-start(f32[256,128]{1,0:T(8,128)S(1)} %slice_add_fusion.4), channel_id=1, source_target_pairs={{0,16},{4,20},{8,24},{12,28},{16,0},{20,4},{24,8},{28,12},{1,17},{... | collective-permute-start | bytes 393224 | tf_op jit(solution)/shard_map/ppermute | solution.py:249
  42.5 14.4 %collective-permute-start.13 = (f32[256,128]{1,0:T(8,128)S(1)}, f32[256,128]{1,0:T(8,128)S(1)}, u32[]{:S(2)}, u32[]{:S(2)}) collective-permute-start(f32[256,128]{1,0:T(8,128)S(1)} %slice_add_fusion.2), channel_id=1, source_target_pairs={{0,16},{4,20},{8,24},{12,28},{16,0},{20,4},{24,8},{28,12},{1,17},{... | collective-permute-start | bytes 393224 | tf_op jit(solution)/shard_map/ppermute | solution.py:249
  43.0 31.1 %copy-start = (bf16[2048,512]{1,0:T(8,128)(2,1)S(1)}, bf16[2048,512]{1,0:T(8,128)(2,1)}, u32[]{:S(2)}) copy-start(bf16[2048,512]{1,0:T(8,128)(2,1)} %res_ref.3) | copy-start | bytes 6291460
  43.0 15.4 %collective-permute-start.16 = (f32[256,128]{1,0:T(8,128)S(1)}, f32[256,128]{1,0:T(8,128)S(1)}, u32[]{:S(2)}, u32[]{:S(2)}) collective-permute-start(f32[256,128]{1,0:T(8,128)S(1)} %slice_add_fusion), channel_id=1, source_target_pairs={{0,16},{4,20},{8,24},{12,28},{16,0},{20,4},{24,8},{28,12},{1,17},{... | collective-permute-start | bytes 393224 | tf_op jit(solution)/shard_map/ppermute | solution.py:249
  58.4 9.6 %collective-permute-start.18 = (f32[768,128]{1,0:T(8,128)S(1)}, f32[768,128]{1,0:T(8,128)S(1)}, u32[]{:S(2)}, u32[]{:S(2)}) collective-permute-start(f32[768,128]{1,0:T(8,128)S(1)} %pad_maximum_fusion.refs_0_), channel_id=1, source_target_pairs={{0,2},{1,3},{2,0},{3,1},{4,6},{5,7},{6,4},{7,5},{8,10},{9,11},{10,... | collective-permute-start | bytes 1179656 | tf_op jit(solution)/shard_map/ppermute | solution.py:249
  60.0 8.1 %collective-permute-start.3 = (f32[256,128]{1,0:T(8,128)S(1)}, f32[256,128]{1,0:T(8,128)S(1)}, u32[]{:S(2)}, u32[]{:S(2)}) collective-permute-start(f32[256,128]{1,0:T(8,128)S(1)} %slice_add_fusion.6), channel_id=1, source_target_pairs={{0,16},{4,20},{8,24},{12,28},{16,0},{20,4},{24,8},{28,12},{1,17},{... | collective-permute-start | bytes 393224 | tf_op jit(solution)/shard_map/ppermute | solution.py:249
  60.1 14.0 %collective-permute-start.17 = (f32[768,128]{1,0:T(8,128)S(1)}, f32[768,128]{1,0:T(8,128)S(1)}, u32[]{:S(2)}, u32[]{:S(2)}) collective-permute-start(f32[768,128]{1,0:T(8,128)S(1)} %pad_maximum_fusion.refs_0_), channel_id=1, source_target_pairs={{0,1},{1,0},{2,3},{3,2},{4,5},{5,4},{6,7},{7,6},{8,9},{9,8},{10,11... | collective-permute-start | bytes 1179656 | tf_op jit(solution)/shard_map/ppermute | solution.py:249
  68.0 6.0 %collective-permute-start.19 = (f32[768,128]{1,0:T(8,128)S(1)}, f32[768,128]{1,0:T(8,128)}, u32[]{:S(2)}, u32[]{:S(2)}) collective-permute-start(f32[768,128]{1,0:T(8,128)S(1)} %collective-permute-done.18.refs_2_), channel_id=1, source_target_pairs={{0,1},{1,0},{2,3},{3,2},{4,5},{5,4},{6,7},{7,6},{8,9},{9,8},{10,11... | collective-permute-start | bytes 1179656 | tf_op jit(solution)/shard_map/ppermute | solution.py:249
  68.1 6.0 %collective-permute-start.5 = (f32[256,128]{1,0:T(8,128)S(1)}, f32[256,128]{1,0:T(8,128)S(1)}, u32[]{:S(2)}, u32[]{:S(2)}) collective-permute-start(f32[256,128]{1,0:T(8,128)S(1)} %fusion.3.refs_0_), channel_id=1, source_target_pairs={{0,2},{1,3},{2,0},{3,1},{4,6},{5,7},{6,4},{7,5},{8,10},{9,11},{10,... | collective-permute-start | bytes 393224 | tf_op jit(solution)/shard_map/ppermute | solution.py:249
  69.6 6.4 %collective-permute-start.4 = (f32[256,128]{1,0:T(8,128)S(1)}, f32[256,128]{1,0:T(8,128)}, u32[]{:S(2)}, u32[]{:S(2)}) collective-permute-start(f32[256,128]{1,0:T(8,128)S(1)} %fusion.3.refs_0_), channel_id=1, source_target_pairs={{0,1},{1,0},{2,3},{3,2},{4,5},{5,4},{6,7},{7,6},{8,9},{9,8},{10,11... | collective-permute-start | bytes 393224 | tf_op jit(solution)/shard_map/ppermute | solution.py:249
  74.0 2.0 %collective-permute-start.6 = (f32[256,128]{1,0:T(8,128)S(1)}, f32[256,128]{1,0:T(8,128)}, u32[]{:S(2)}, u32[]{:S(2)}) collective-permute-start(f32[256,128]{1,0:T(8,128)S(1)} %collective-permute-done.5.refs_2_), channel_id=1, source_target_pairs={{0,1},{1,0},{2,3},{3,2},{4,5},{5,4},{6,7},{7,6},{8,9},{9,8},{10,11... | collective-permute-start | bytes 393224 | tf_op jit(solution)/shard_map/ppermute | solution.py:249

commit v3 on v2

--- a/solution.py
+++ b/solution.py
@@ -14,6 +14,32 @@
 LANES = 128
 GROUP = 8
 VMEM_LIMIT = 12 * 1024 * 1024
+COST = 1024
+SCHEDULE = (
+    ("begin", 0),
+    ("begin", 3),
+    ("first", 0),
+    ("first", 3),
+    ("begin", 1),
+    ("begin", 2),
+    ("first", 1),
+    ("middle", 0),
+    ("rows", 0, 3, 1, 2),
+    ("middle", 3),
+    ("first", 2),
+    ("middle", 1),
+    ("final", 0),
+    ("final", 3),
+    ("middle", 2),
+    ("final", 1),
+    ("arrive", 0),
+    ("arrive", 3),
+    ("final", 2),
+    ("near", 0, 3, 1, 2),
+    ("arrive", 1),
+    ("far", 0, 3, 1, 2),
+    ("multiply", 0, 3, 1, 2),
+)
 SCALE = math.sqrt(0.5 / math.log(2.0))
 
 
@@ -86,9 +112,9 @@
     proj = rest[-1]
     comps, tiles, pix = strain_ref.shape
     angles = count_ref.shape[0]
-    qcount = dirs_ref.shape[0] // (angles * comps)
+    qcount = dirs_ref.shape[1]
     rocks = rock_ref.shape[0]
-    step = 2 * GROUP
+    step = 4 * GROUP
     if len(rest) == 2:
         init, outs = None, rest[:1]
     else:
@@ -96,7 +122,10 @@
     acc = outs[0] if init is None else rest[-2]
     blocks = pix // LANES
     rows_out = acc.shape[0] // blocks
-    rock = rock_ref[...]
+    row = lax.broadcasted_iota(jnp.int32, (rocks, LANES), 0)
+    rock = jnp.zeros((rocks, LANES), jnp.float32)
+    for i in range(rocks):
+        rock = jnp.where(row == i, rock_ref[i] * SCALE, rock)
     if init is None:
         acc[...] = jnp.zeros_like(acc)
     else:
@@ -105,14 +134,13 @@
     for b in range(blocks):
         lanes = slice(b * LANES, (b + 1) * LANES)
 
-        @pl.loop(0, tiles // step)
-        def _(block):
-            rows = pl.ds(pl.multiple_of(block * step, step), step)
-            parts = [strain_ref[c, rows, lanes] for c in range(comps)]
-            for k in range(angles * qcount):
-                total = parts[0] * dirs_ref[k * comps]
+        for k in range(angles * qcount):
+            scaled = [dirs_ref[k // qcount, k % qcount, c] * SCALE for c in range(comps)]
+            for start in range(0, tiles, step):
+                rows = pl.ds(start, step)
+                total = strain_ref[0, rows, lanes] * scaled[0]
                 for c in range(1, comps):
-                    total = total + parts[c] * dirs_ref[k * comps + c]
+                    total = total + strain_ref[c, rows, lanes] * scaled[c]
                 proj[k, rows, :] = total
 
         for angle in range(angles):
@@ -143,11 +171,11 @@
             start += out.shape[0]
 
 
-def add_images(name, listing, weights, rock, strain, init, sizes, cost):
+def add_images(name, listing, weights, rock, strain, init, sizes):
     counts, lists = listing
     comps, tiles, pix = strain.shape
     angles = counts.shape[0]
-    qcount = weights.shape[0] // (angles * comps)
+    qcount = weights.shape[1]
     smem = pl.BlockSpec(memory_space=pltpu.SMEM)
     vmem = pl.BlockSpec(memory_space=pltpu.VMEM)
     scratch = [pltpu.VMEM((angles * qcount, tiles, LANES), jnp.float32)]
@@ -158,53 +186,69 @@
     return pl.pallas_call(
         image_kernel,
         out_shape=tuple(jax.ShapeDtypeStruct((size, LANES), jnp.float32) for size in sizes),
-        in_specs=[smem, smem, smem] + [vmem] * (2 + len(before)),
+        in_specs=[smem, smem, smem, smem] + [vmem] * (1 + len(before)),
         out_specs=tuple(vmem for size in sizes),
         scratch_shapes=scratch,
         compiler_params=pltpu.CompilerParams(vmem_limit_bytes=VMEM_LIMIT),
-        cost_estimate=pl.CostEstimate(flops=cost, bytes_accessed=1_000_000, transcendentals=0),
+        cost_estimate=pl.CostEstimate(flops=COST, bytes_accessed=COST, transcendentals=0),
         name=name,
     )(counts, lists, weights, rock, strain, *before)
 
 
-def resolve(rock_index, firsts, pix, norm, total, resolution, parts):
-    count = len(firsts)
-    unit = parts[0].shape[0] // count
-    lanes = parts[0].shape[1]
-    cols = resolution.shape[1]
-    smem = pl.BlockSpec(memory_space=pltpu.SMEM)
+def resolve(norm, unit, total, blocks, parts):
+    cols = blocks[0].shape[1]
     vmem = pl.BlockSpec(memory_space=pltpu.VMEM)
-
-    def kernel(rock_ref, res_ref, *refs):
-        part_refs, out_ref = refs[: len(parts)], refs[-1]
-        values = []
-        blocks = []
-        for j, part in enumerate(part_refs):
-            for c, first in enumerate(firsts):
-                start = pl.multiple_of((rock_ref[0] ^ j) * pix + first, lanes)
-                blocks.append(res_ref[pl.ds(start, lanes), :])
-                values.append(part[pl.ds(c * unit, unit), :] * norm)
-        block = jnp.concatenate(blocks, axis=0)
+    before = () if total is None else (total,)
+
+    def kernel(*refs):
+        block_refs, part_refs, out_ref = refs[: len(blocks)], refs[len(blocks) : len(blocks) + len(parts)], refs[-1]
+        values = [
+            part[pl.ds(start, unit), :] * norm for part in part_refs for start in range(0, part.shape[0], unit)
+        ]
         value = jnp.concatenate(values, axis=1)
+        block = jnp.concatenate([ref[...] for ref in block_refs], axis=0)
         high = value.astype(jnp.bfloat16)
         low = (value - high.astype(jnp.float32)).astype(jnp.bfloat16)
-        result = jnp.dot(high, block, preferred_element_type=jnp.float32) + jnp.dot(
+        sums = jnp.dot(high, block, preferred_element_type=jnp.float32) + jnp.dot(
             low, block, preferred_element_type=jnp.float32
         )
-        if total is not None:
-            result = result + refs[len(parts)][...]
-        out_ref[...] = result
-
-    before = () if total is None else (total,)
+        out_ref[...] = sums if total is None else sums + refs[-2][...]
+
     return pl.pallas_call(
         kernel,
         out_shape=jax.ShapeDtypeStruct((unit, cols), jnp.float32),
-        in_specs=[smem] + [vmem] * (1 + len(parts) + len(before)),
+        in_specs=[vmem] * (len(blocks) + len(parts) + len(before)),
         out_specs=vmem,
         compiler_params=pltpu.CompilerParams(vmem_limit_bytes=VMEM_LIMIT),
-        cost_estimate=pl.CostEstimate(flops=500_000_000, bytes_accessed=1_000_000, transcendentals=0),
+        cost_estimate=pl.CostEstimate(flops=COST, bytes_accessed=COST, transcendentals=0),
         name="resolve",
-    )(rock_index, resolution, *parts, *before)
+    )(*blocks, *parts, *before)
+
+
+def cut(by_comp):
+    comps, tiles, pix = by_comp.shape
+    count = pix // LANES
+
+    def kernel(source, *rest):
+        outs, sems = rest[:count], rest[count]
+        copies = [
+            pltpu.make_async_copy(source.at[:, :, pl.ds(c * LANES, LANES)], outs[c], sems.at[c]) for c in range(count)
+        ]
+        for copy in copies:
+            copy.start()
+        for copy in copies:
+            copy.wait()
+
+    return pl.pallas_call(
+        kernel,
+        out_shape=[jax.ShapeDtypeStruct((comps, tiles, LANES), jnp.float32)] * count,
+        in_specs=[pl.BlockSpec(memory_space=pl.ANY)],
+        out_specs=[pl.BlockSpec(memory_space=pltpu.VMEM)] * count,
+        scratch_shapes=[pltpu.SemaphoreType.DMA((count,))],
+        compiler_params=pltpu.CompilerParams(vmem_limit_bytes=VMEM_LIMIT),
+        cost_estimate=pl.CostEstimate(flops=COST, bytes_accessed=COST, transcendentals=0),
+        name="cut",
+    )(by_comp)
 
 
 def bit(value, number):
@@ -248,56 +292,119 @@
         size = lax.axis_size(axis)
         return lax.ppermute(value, axis, [(i, i ^ (1 << number)) for i in range(size)])
 
-    plans = [(0, tuple(range(1, bits))), (1, (0,) + tuple(range(2, bits)))]
+    plans = [(0, tuple(range(1, bits))), (1, tuple(range(2, bits)) + (0,))]
     plan_of = [0] * (chunks - 1) + [1] if chunks > 1 else [0]
-    order = sorted(range(chunks), key=lambda c: -plan_of[c])
-
-    by_comp = strain.transpose(1, 0, 2)
-    own = [by_comp[:, :, c * LANES : (c + 1) * LANES] for c in range(chunks)]
-    info = dest[:, :, 0] * ROWS + det_row
-    other = {c: swap(own[c], plans[plan_of[c]][0]) for c in order}
+    early = [c for c in range(chunks) if plan_of[c] == 0]
+    late = [c for c in range(chunks) if plan_of[c] == 1]
+    last = []
+
+    def tie(value):
+        return lax.optimization_barrier((value, *last))[0]
+
+    def mark(value):
+        last[:] = [value]
+        return value
+
+    own = cut(strain.transpose(1, 0, 2))
+    other = {c: swap(own[c], plans[plan_of[c]][0]) for c in early[:1] + late + early[1:]}
+    mark(own[0])
+    info = tie(dest[:, :, 0] * ROWS + det_row)
     used = sorted(set(plan_of))
     other_info = {k: swap(info, plans[k][0]) for k in used}
     own_list = {k: listing(info, me, *plans[k], angles, units) for k in used}
     other_list = {k: listing(other_info[k], me, *plans[k], angles, units) for k in used}
 
-    weights = (dirs * SCALE).reshape(-1)
-    rock = jnp.broadcast_to((rock_angles * SCALE)[:, None], (rocks, LANES))
-    rock_index = lax.axis_index("rock").reshape(1)
 
     partial = {}
-    for c in order:
+    held = {}
+    flying = {}
+    half = image_rows // 2
+
+    def begin(c):
         (partial[c],) = add_images(
-            "own_images", own_list[plan_of[c]], weights, rock, own[c], None, [image_rows + rocks], 3_000_000
-        )
-
+            "own_images",
+            own_list[plan_of[c]],
+            dirs,
+            rock_angles,
+            tie(own[c]),
+            None,
+            [image_rows + rocks],
+        )
+        mark(partial[c])
+
+    def first(c):
+        k = plan_of[c]
+        sent, held[c] = add_images(
+            "other_images", other_list[k], dirs, rock_angles, tie(other[c]), partial[c], [half, half]
+        )
+        mark(sent)
+        flying[c] = swap(sent, plans[k][1][0])
+
+    def middle(c):
+        arrived = tie(flying[c])
+        for number in plans[plan_of[c]][1][1:]:
+            rows = held[c].shape[0] // 2
+            sent = mark(held[c][:rows] + arrived[:rows])
+            flying[c] = swap(sent, number)
+            held[c] = held[c][rows:] + arrived[rows:]
+            arrived = flying[c]
+
+    lower = list(reversed(range(max(rock_size.bit_length() - 2, 0))))
     image = {}
-    for c in order:
-        k = plan_of[c]
-        held = image_rows // 2
-        sent, kept = add_images(
-            "other_images", other_list[k], weights, rock, other[c], partial[c], [held, held], 3_000_000
-        )
-        for number in plans[k][1]:
-            arrived = swap(sent, number)
-            if held > unit:
-                held = held // 2
-                sent, kept = kept[:held] + arrived[:held], kept[held:] + arrived[held:]
-            else:
-                image[c] = kept + arrived
-
-    def gather(value):
-        parts = [value]
-        for number in reversed(range(rock_size.bit_length() - 1)):
-            parts = [x for part in parts for x in (part, swap(part, number, "rock"))]
-        return parts
-
-    groups = [order[:-1], order[-1:]]
-    result = None
-    for group in groups:
-        value = jnp.concatenate([image[c] for c in group], axis=0) if len(group) > 1 else image[group[0]]
-        result = resolve(rock_index, [c * LANES for c in group], pix, norm, result, resolution, gather(value))
-    return result.reshape(angles, ROWS, rocks, pix)
+    beside = {}
+
+    def spread(part):
+        found = [part]
+        for number in lower:
+            found = [x for p in found for x in (p, swap(p, number, "rock"))]
+        return found
+
+    def final(c):
+        image[c] = mark(held[c] + tie(flying[c]))
+        if rock_size > 1:
+            beside[c] = swap(image[c], len(lower), "rock")
+
+    def arrive(c):
+        if rock_size > 1:
+            beside[c] = mark(tie(beside[c]))
+
+    def join(values):
+        return jnp.concatenate(values, axis=0) if len(values) > 1 else values[0]
+
+    rock_index = lax.axis_index("rock")
+    found = {}
+    blocks = {}
+    result = []
+
+    def near(*group):
+        found[group] = spread(mark(join([image[c] for c in group])))
+
+    def far(*group):
+        if rock_size > 1:
+            found[group] = found[group] + spread(mark(tie(join([beside[c] for c in group]))))
+
+    def rows(*group):
+        source = tie(resolution)
+        places = [(rock_index ^ j) * pix + c * LANES for j in range(rock_size) for c in group]
+        blocks[group] = [lax.dynamic_slice(source, (at, 0), (LANES, resolution.shape[1])) for at in places]
+        mark(blocks[group][-1])
+
+    def multiply(*group):
+        parts = found[group]
+        total = result[-1] if result else None
+        result.append(mark(resolve(norm, unit, total, blocks[group], [tie(parts[0])] + parts[1:])))
+
+    if (len(early), len(late)) == (3, 1):
+        steps = SCHEDULE
+    else:
+        every = early + late
+        steps = [(name, c) for name in ("begin", "first", "middle", "final") for c in every]
+        steps += [("rows", *every), ("near", *every), ("far", *every), ("multiply", *every)]
+    doing = dict(begin=begin, first=first, middle=middle, final=final, arrive=arrive, near=near, far=far, rows=rows)
+    doing["multiply"] = multiply
+    for name, *group in steps:
+        doing[name](*group)
+    return result[-1].reshape(angles, ROWS, rocks, pix)
 
 
 def local(strain, dest, det_row, dirs, rock_angles, resolution):
@@ -308,7 +415,7 @@
     slots = slabs * (2 * tiles // slabs)
     images_smaller = slabs * ROWS * rock_angles.shape[0] * pix <= slots * dirs.shape[1] * vox
     powers = all(size & (size - 1) == 0 for size in (slabs, rock_size, tiles))
-    regular = powers and slabs >= 4 and tiles % (2 * GROUP) == 0 and vox == pix and pix % LANES == 0
+    regular = powers and slabs >= 4 and tiles % (4 * GROUP) == 0 and vox == pix and pix % LANES == 0
     plan = by_images if images_smaller and regular else by_tiles
     return plan(strain, dest, det_row, dirs, rock_angles, resolution)
 

time: 78.5 us -> 65.6 us (0.84)
  waiting for transfers between devices: 35.6 us -> 16.3 us
  starting transfers between devices: 20.6 us -> 26 us
  local copies, waits for them, and re-layouts: 1.67 us -> 2.99 us
    ppermute x20, waiting for transfers between devices: 35.6 us -> 16.3 us  [swap(): lax.ppermute(value, axis, [(i, i ^ 1 << number) for i in range(size)])]
    ppermute x20, starting transfers between devices: 20.6 us -> 26 us  [swap(): lax.ppermute(value, axis, [(i, i ^ 1 << number) for i in range(size)])]
    unnamed x6 -> x12, local copies, waits for them, and re-layouts: 0.01 us -> 2.76 us
    pallas_call x2 -> x1, Pallas kernels: 4.18 us -> 2.12 us  [resolve(): pl.pallas_call(kernel, out_shape=jax.ShapeDtypeStruct((unit, cols), jnp.f...]
    slice x1 -> x0, local copies, waits for them, and re-layouts: 1.5 us -> none  [by_images(): own = [by_comp[:, :, c * LANES:(c + 1) * LANES] for c in range(chunks)]]
    pallas_call x8, Pallas kernels: 13.9 us -> 15.1 us  [add_images(): pl.pallas_call(image_kernel, out_shape=tuple((jax.ShapeDtypeStruct((size,...]
  transfers between devices with their start and end apart: 20 -> 20, of which waited for: 9 -> 7; matrix products, arithmetic and copies ran while one was open for 4% -> 3% of each run, Pallas kernels for 20% -> 23%
where the time goes in v3:
time: 65.6 us; the launch traced here: 65.3 us
  starting transfers between devices  26 us (40%)
  Pallas kernels  17.5 us (27%)
  waiting for transfers between devices  16.3 us (25%)
  local copies, waits for them, and re-layouts  2.99 us (5%)
  other arithmetic  2.15 us (3%)
    ppermute x20, starting transfers between devices, swap(): lax.ppermute(value, axis, [(i, i ^ 1 << number) for i in range(size)])  26 us
    ppermute x20, waiting for transfers between devices, swap(): lax.ppermute(value, axis, [(i, i ^ 1 << number) for i in range(size)])  16.3 us
    pallas_call x8, Pallas kernels, add_images(): pl.pallas_call(image_kernel, out_shape=tuple((jax.ShapeDtypeStruct((size,...  15.1 us
    unnamed x12, local copies, waits for them, and re-layouts  2.76 us
    pallas_call x1, Pallas kernels, resolve(): pl.pallas_call(kernel, out_shape=jax.ShapeDtypeStruct((unit, cols), jnp.f...  2.12 us
  transfers between devices with their start and end apart: 20, of which 7 were waited for; matrix products, arithmetic and copies ran while one was open for 3% of the time, Pallas kernels for 23%

profile of v3, /device:TPU:0, one launch (start us, length us, event | category | flops | bytes accessed | tf_op | source)
XLA Modules:
  0.0 65.3 jit_solution(18043607164046238957)
XLA Ops:
  0.0 1.4 %copy-done = f32[128,6,512]{2,0,1:T(8,128)S(1)} copy-done((f32[128,6,512]{2,0,1:T(8,128)S(1)}, f32[128,6,512]{2,0,1:T(8,128)}, u32[]{:S(2)}) %copy-start) | copy-done | bytes 1572888
  1.7 0.7 %bitcast_add_fusion = s32[2,128]{1,0:T(2,128)S(1)} fusion(s32[2,128]{1,0:T(2,128)} %param.8, s32[2,128,1]{1,0,2:T(2,128)} %bitcast.6), kind=kLoop, calls=%fused_computation.72 | loop fusion | flops 512 | bytes 3072 | tf_op jit(solution)/shard_map/add | solution.py:311
  2.4 3.0 %collective-permute-start.4 = (s32[2,128]{1,0:T(2,128)S(1)}, s32[2,128]{1,0:T(2,128)S(1)}, u32[]{:S(2)}, u32[]{:S(2)}) collective-permute-start(s32[2,128]{1,0:T(2,128)S(1)} %bitcast_add_fusion), channel_id=1, source_target_pairs={{0,8},{4,12},{8,0},{12,4},{16,24},{20,28},{24,16},{28,20},{1,9},{5... | collective-permute-start | bytes 3080 | tf_op jit(solution)/shard_map/ppermute | solution.py:293
  5.4 1.5 %collective-permute-start = (s32[2,128]{1,0:T(2,128)S(1)}, s32[2,128]{1,0:T(2,128)S(1)}, u32[]{:S(2)}, u32[]{:S(2)}) collective-permute-start(s32[2,128]{1,0:T(2,128)S(1)} %bitcast_add_fusion), channel_id=1, source_target_pairs={{0,4},{4,0},{8,12},{12,8},{16,20},{20,16},{24,28},{28,24},{1,5},{5... | collective-permute-start | bytes 3080 | tf_op jit(solution)/shard_map/ppermute | solution.py:293
  7.4 2.0 %collective-permute-start.3 = (f32[6,128,128]{2,1,0:T(8,128)S(1)}, f32[6,128,128]{2,1,0:T(8,128)S(1)}, u32[]{:S(2)}, u32[]{:S(2)}) collective-permute-start(f32[6,128,128]{2,1,0:T(8,128)S(1)} %get-tuple-element.52.strain_ref), channel_id=1, source_target_pairs={{0,4},{4,0},{8,12},{12,8},{16,20},{20,16},{24,28},{28,24},{1,5},{5... | collective-permute-start | bytes 1179656 | tf_op jit(solution)/shard_map/ppermute | solution.py:293
  10.8 0.7 %copy-done.1 = f32[2,4,6]{2,1,0:T(4,128)S(1)} copy-done((f32[2,4,6]{2,1,0:T(4,128)S(1)}, f32[2,4,6]{2,1,0:T(4,128)}, u32[]{:S(2)}) %copy-start.1) | copy-done | bytes 216
  11.5 0.7 %copy-done.3 = f32[16]{0:T(128)S(1)} copy-done((f32[16]{0:T(128)S(1)}, f32[16]{0:T(128)}, u32[]{:S(2)}) %copy-start.3) | copy-done | bytes 88
  12.1 1.8 %own_images.4.rest_0_ = f32[1040,128]{1,0:T(8,128)S(1)} custom-call(s32[2]{0:T(128)S(1)} %get-tuple-element.86.count_ref, s32[2,128]{1,0:T(2,128)S(1)} %broadcast_add_fusion.1.list_ref, f32[2,4,6]{2,1,0:T(4,128)S(1)} %copy-done.1, f32[16]{0:T(128)S(1)} %copy-done.3, f32[6,128,128]{2,1,0:T(8,128)S(1)} %get-tuple-element.43.strain_ref), custom_call_target="tpu_custom_call" | custom-call | flops 1024 | bytes 1024 | tf_op jit(solution)/shard_map/own_images/pallas_call | solution.py:186
  13.9 2.0 %own_images.5.rest_0_ = f32[1040,128]{1,0:T(8,128)S(1)} custom-call(s32[2]{0:T(128)S(1)} %get-tuple-element.112.count_ref, s32[2,128]{1,0:T(2,128)S(1)} %broadcast_add_fusion.2.list_ref, f32[2,4,6]{2,1,0:T(4,128)S(1)} %copy-done.2, f32[16]{0:T(128)S(1)} %copy-done.3, f32[6,128,128]{2,1,0:T(8,128)S(1)} %get-tuple-element.44.strain_ref), custom_call_target="tpu_custom_call" | custom-call | flops 1024 | bytes 1024 | tf_op jit(solution)/shard_map/own_images/pallas_call | solution.py:186
  16.0 3.0 %collective-permute-done.1.strain_ref = f32[6,128,128]{2,1,0:T(8,128)S(1)} collective-permute-done((f32[6,128,128]{2,1,0:T(8,128)S(1)}, f32[6,128,128]{2,1,0:T(8,128)S(1)}, u32[]{:S(2)}, u32[]{:S(2)}) %collective-permute-start.1) | collective-permute-done | bytes 393248 | tf_op jit(solution)/shard_map/ppermute | solution.py:293
  19.0 1.9 %other_images.4 = (f32[512,128]{1,0:T(8,128)S(1)}, f32[512,128]{1,0:T(8,128)S(1)}) custom-call(s32[2]{0:T(128)S(1)} %get-tuple-element.90.count_ref, s32[2,128]{1,0:T(2,128)S(1)} %broadcast_add_fusion.3.list_ref, f32[2,4,6]{2,1,0:T(4,128)S(1)} %copy-done.2, f32[16]{0:T(128)S(1)} %copy-done.3, f32[6,128,128]{2,1,0:T(8,128)S(1)} %collective-permute-done.1.strain_ref, ...), custom_call_target="tpu_custom_call" | custom-call | flops 1024 | bytes 1024 | tf_op jit(solution)/shard_map/other_images/pallas_call | solution.py:186
  21.5 2.0 %other_images.5 = (f32[512,128]{1,0:T(8,128)S(1)}, f32[512,128]{1,0:T(8,128)S(1)}) custom-call(s32[2]{0:T(128)S(1)} %get-tuple-element.81.count_ref, s32[2,128]{1,0:T(2,128)S(1)} %broadcast_add_fusion.list_ref, f32[2,4,6]{2,1,0:T(4,128)S(1)} %copy-done.2, f32[16]{0:T(128)S(1)} %copy-done.3, f32[6,128,128]{2,1,0:T(8,128)S(1)} %collective-permute-done.5.strain_ref, ...), custom_call_target="tpu_custom_call" | custom-call | flops 1024 | bytes 1024 | tf_op jit(solution)/shard_map/other_images/pallas_call | solution.py:186
  23.5 2.7 %collective-permute-start.9 = (f32[512,128]{1,0:T(8,128)S(1)}, f32[512,128]{1,0:T(8,128)S(1)}, u32[]{:S(2)}, u32[]{:S(2)}) collective-permute-start(f32[512,128]{1,0:T(8,128)S(1)} %get-tuple-element.51), channel_id=1, source_target_pairs={{0,16},{4,20},{8,24},{12,28},{16,0},{20,4},{24,8},{28,12},{1,17},{... | collective-permute-start | bytes 786440 | tf_op jit(solution)/shard_map/ppermute | solution.py:293
  26.2 1.8 %own_images.6.rest_0_ = f32[1040,128]{1,0:T(8,128)S(1)} custom-call(s32[2]{0:T(128)S(1)} %get-tuple-element.86.count_ref, s32[2,128]{1,0:T(2,128)S(1)} %broadcast_add_fusion.1.list_ref, f32[2,4,6]{2,1,0:T(4,128)S(1)} %copy-done.2, f32[16]{0:T(128)S(1)} %copy-done.3, f32[6,128,128]{2,1,0:T(8,128)S(1)} %get-tuple-element.52.strain_ref), custom_call_target="tpu_custom_call" | custom-call | flops 1024 | bytes 1024 | tf_op jit(solution)/shard_map/own_images/pallas_call | solution.py:186
  27.9 1.8 %own_images.7.rest_0_ = f32[1040,128]{1,0:T(8,128)S(1)} custom-call(s32[2]{0:T(128)S(1)} %get-tuple-element.86.count_ref, s32[2,128]{1,0:T(2,128)S(1)} %broadcast_add_fusion.1.list_ref, f32[2,4,6]{2,1,0:T(4,128)S(1)} %copy-done.2, f32[16]{0:T(128)S(1)} %copy-done.3, f32[6,128,128]{2,1,0:T(8,128)S(1)} %get-tuple-element.53.strain_ref), custom_call_target="tpu_custom_call" | custom-call | flops 1024 | bytes 1024 | tf_op jit(solution)/shard_map/own_images/pallas_call | solution.py:186
  29.7 1.9 %other_images.6 = (f32[512,128]{1,0:T(8,128)S(1)}, f32[512,128]{1,0:T(8,128)S(1)}) custom-call(s32[2]{0:T(128)S(1)} %get-tuple-element.90.count_ref, s32[2,128]{1,0:T(2,128)S(1)} %broadcast_add_fusion.3.list_ref, f32[2,4,6]{2,1,0:T(4,128)S(1)} %copy-done.2, f32[16]{0:T(128)S(1)} %copy-done.3, f32[6,128,128]{2,1,0:T(8,128)S(1)} %collective-permute-done.3.strain_ref, ...), custom_call_target="tpu_custom_call" | custom-call | flops 1024 | bytes 1024 | tf_op jit(solution)/shard_map/other_images/pallas_call | solution.py:186
  31.7 1.8 %collective-permute-start.7 = (f32[512,128]{1,0:T(8,128)S(1)}, f32[512,128]{1,0:T(8,128)S(1)}, u32[]{:S(2)}, u32[]{:S(2)}) collective-permute-start(f32[512,128]{1,0:T(8,128)S(1)} %get-tuple-element.55), channel_id=1, source_target_pairs={{0,8},{4,12},{8,0},{12,4},{16,24},{20,28},{24,16},{28,20},{1,9},{5... | collective-permute-start | bytes 786440 | tf_op jit(solution)/shard_map/ppermute | solution.py:293
  33.9 3.8 %collective-permute-start.10 = (f32[256,128]{1,0:T(8,128)S(1)}, f32[256,128]{1,0:T(8,128)S(1)}, u32[]{:S(2)}, u32[]{:S(2)}) collective-permute-start(f32[256,128]{1,0:T(8,128)S(1)} %slice_add_fusion.2), channel_id=1, source_target_pairs={{0,4},{4,0},{8,12},{12,8},{16,20},{20,16},{24,28},{28,24},{1,5},{5... | collective-permute-start | bytes 393224 | tf_op jit(solution)/shard_map/ppermute | solution.py:293
  37.8 1.9 %other_images.7 = (f32[512,128]{1,0:T(8,128)S(1)}, f32[512,128]{1,0:T(8,128)S(1)}) custom-call(s32[2]{0:T(128)S(1)} %get-tuple-element.90.count_ref, s32[2,128]{1,0:T(2,128)S(1)} %broadcast_add_fusion.3.list_ref, f32[2,4,6]{2,1,0:T(4,128)S(1)} %copy-done.2, f32[16]{0:T(128)S(1)} %copy-done.4, f32[6,128,128]{2,1,0:T(8,128)S(1)} %collective-permute-done.8.strain_ref, ...), custom_call_target="tpu_custom_call" | custom-call | flops 1024 | bytes 1024 | tf_op jit(solution)/shard_map/other_images/pallas_call | solution.py:186
  39.7 1.2 %collective-permute-start.12 = (f32[512,128]{1,0:T(8,128)S(1)}, f32[512,128]{1,0:T(8,128)S(1)}, u32[]{:S(2)}, u32[]{:S(2)}) collective-permute-start(f32[512,128]{1,0:T(8,128)S(1)} %get-tuple-element.62), channel_id=1, source_target_pairs={{0,8},{4,12},{8,0},{12,4},{16,24},{20,28},{24,16},{28,20},{1,9},{5... | collective-permute-start | bytes 786440 | tf_op jit(solution)/shard_map/ppermute | solution.py:293
  40.9 1.3 %collective-permute-done.7 = f32[512,128]{1,0:T(8,128)S(1)} collective-permute-done((f32[512,128]{1,0:T(8,128)S(1)}, f32[512,128]{1,0:T(8,128)S(1)}, u32[]{:S(2)}, u32[]{:S(2)}) %collective-permute-start.7) | collective-permute-done | bytes 262176 | tf_op jit(solution)/shard_map/ppermute | solution.py:293
  42.3 2.4 %collective-permute-start.11 = (f32[256,128]{1,0:T(8,128)S(1)}, f32[256,128]{1,0:T(8,128)S(1)}, u32[]{:S(2)}, u32[]{:S(2)}) collective-permute-start(f32[256,128]{1,0:T(8,128)S(1)} %slice_add_fusion.1), channel_id=1, source_target_pairs={{0,16},{4,20},{8,24},{12,28},{16,0},{20,4},{24,8},{28,12},{1,17},{... | collective-permute-start | bytes 393224 | tf_op jit(solution)/shard_map/ppermute | solution.py:293
  44.6 1.7 %collective-permute-start.15 = (f32[256,128]{1,0:T(8,128)S(1)}, f32[256,128]{1,0:T(8,128)S(1)}, u32[]{:S(2)}, u32[]{:S(2)}) collective-permute-start(f32[256,128]{1,0:T(8,128)S(1)} %add_add_fusion.3), channel_id=1, source_target_pairs={{0,2},{1,3},{2,0},{3,1},{4,6},{5,7},{6,4},{7,5},{8,10},{9,11},{10,... | collective-permute-start | bytes 393224 | tf_op jit(solution)/shard_map/ppermute | solution.py:293
  46.8 1.9 %collective-permute-done.12 = f32[512,128]{1,0:T(8,128)S(1)} collective-permute-done((f32[512,128]{1,0:T(8,128)S(1)}, f32[512,128]{1,0:T(8,128)S(1)}, u32[]{:S(2)}, u32[]{:S(2)}) %collective-permute-start.12) | collective-permute-done | bytes 262176 | tf_op jit(solution)/shard_map/ppermute | solution.py:293
  48.8 1.0 %collective-permute-start.13 = (f32[256,128]{1,0:T(8,128)S(1)}, f32[256,128]{1,0:T(8,128)S(1)}, u32[]{:S(2)}, u32[]{:S(2)}) collective-permute-start(f32[256,128]{1,0:T(8,128)S(1)} %slice_add_fusion), channel_id=1, source_target_pairs={{0,16},{4,20},{8,24},{12,28},{16,0},{20,4},{24,8},{28,12},{1,17},{... | collective-permute-start | bytes 393224 | tf_op jit(solution)/shard_map/ppermute | solution.py:293
  49.7 1.6 %collective-permute-start.16 = (f32[256,128]{1,0:T(8,128)S(1)}, f32[256,128]{1,0:T(8,128)S(1)}, u32[]{:S(2)}, u32[]{:S(2)}) collective-permute-start(f32[256,128]{1,0:T(8,128)S(1)} %add_add_fusion.1), channel_id=1, source_target_pairs={{0,2},{1,3},{2,0},{3,1},{4,6},{5,7},{6,4},{7,5},{8,10},{9,11},{10,... | collective-permute-start | bytes 393224 | tf_op jit(solution)/shard_map/ppermute | solution.py:293
  51.3 1.2 %collective-permute-done.14 = f32[256,128]{1,0:T(8,128)S(1)} collective-permute-done((f32[256,128]{1,0:T(8,128)S(1)}, f32[256,128]{1,0:T(8,128)S(1)}, u32[]{:S(2)}, u32[]{:S(2)}) %collective-permute-start.14) | collective-permute-done | bytes 131104 | tf_op jit(solution)/shard_map/ppermute | solution.py:293
  52.5 3.6 %collective-permute-done.13 = f32[256,128]{1,0:T(8,128)S(1)} collective-permute-done((f32[256,128]{1,0:T(8,128)S(1)}, f32[256,128]{1,0:T(8,128)S(1)}, u32[]{:S(2)}, u32[]{:S(2)}) %collective-permute-start.13) | collective-permute-done | bytes 131104 | tf_op jit(solution)/shard_map/ppermute | solution.py:293
  56.1 1.6 %collective-permute-start.17 = (f32[256,128]{1,0:T(8,128)S(1)}, f32[256,128]{1,0:T(8,128)S(1)}, u32[]{:S(2)}, u32[]{:S(2)}) collective-permute-start(f32[256,128]{1,0:T(8,128)S(1)} %add_add_fusion), channel_id=1, source_target_pairs={{0,2},{1,3},{2,0},{3,1},{4,6},{5,7},{6,4},{7,5},{8,10},{9,11},{10,... | collective-permute-start | bytes 393224 | tf_op jit(solution)/shard_map/ppermute | solution.py:293
  57.8 3.3 %collective-permute-done.17 = f32[256,128]{1,0:T(8,128)S(1)} collective-permute-done((f32[256,128]{1,0:T(8,128)S(1)}, f32[256,128]{1,0:T(8,128)S(1)}, u32[]{:S(2)}, u32[]{:S(2)}) %collective-permute-start.17) | collective-permute-done | bytes 131104 | tf_op jit(solution)/shard_map/ppermute | solution.py:293
  61.3 1.9 %collective-permute-done.19.refs_19_ = f32[1024,128]{1,0:T(8,128)S(1)} collective-permute-done((f32[1024,128]{1,0:T(8,128)S(1)}, f32[1024,128]{1,0:T(8,128)S(1)}, u32[]{:S(2)}, u32[]{:S(2)}) %collective-permute-start.19) | collective-permute-done | bytes 524320 | tf_op jit(solution)/shard_map/ppermute | solution.py:293
  63.2 2.1 %resolve.1 = f32[256,512]{1,0:T(8,128)} custom-call(bf16[128,512]{1,0:T(8,128)(2,1)S(1)} %get-tuple-element.107.refs_0_, bf16[128,512]{1,0:T(8,128)(2,1)S(1)} %get-tuple-element.106.refs_1_, bf16[128,512]{1,0:T(8,128)(2,1)S(1)} %get-tuple-element.105.refs_2_, bf16[128,512]{1,0:T(8,128)(2,1)S(1)} %get-tuple-element.104.refs_3_, ...), custom_call_target="tpu_custom_call" | custom-call | flops 1024 | bytes 1024 | tf_op jit(solution)/shard_map/resolve/pallas_call | solution.py:217
  (60 shorter events, 3.8 us)
Async XLA Ops:
  0.0 1.4 %copy-start = (f32[128,6,512]{2,0,1:T(8,128)S(1)}, f32[128,6,512]{2,0,1:T(8,128)}, u32[]{:S(2)}) copy-start(f32[128,6,512]{2,0,1:T(8,128)} %param.6) | copy-start | bytes 4718596
  1.4 12.5 %copy-start.2 = (f32[2,4,6]{2,1,0:T(4,128)S(1)}, f32[2,4,6]{2,1,0:T(4,128)}, u32[]{:S(2)}) copy-start(f32[2,4,6]{2,1,0:T(4,128)} %dirs_ref.15) | copy-start | bytes 580
  2.4 7.3 %collective-permute-start.4 = (s32[2,128]{1,0:T(2,128)S(1)}, s32[2,128]{1,0:T(2,128)S(1)}, u32[]{:S(2)}, u32[]{:S(2)}) collective-permute-start(s32[2,128]{1,0:T(2,128)S(1)} %bitcast_add_fusion), channel_id=1, source_target_pairs={{0,8},{4,12},{8,0},{12,4},{16,24},{20,28},{24,16},{28,20},{1,9},{5... | collective-permute-start | bytes 3080 | tf_op jit(solution)/shard_map/ppermute | solution.py:293
  5.4 4.5 %collective-permute-start = (s32[2,128]{1,0:T(2,128)S(1)}, s32[2,128]{1,0:T(2,128)S(1)}, u32[]{:S(2)}, u32[]{:S(2)}) collective-permute-start(s32[2,128]{1,0:T(2,128)S(1)} %bitcast_add_fusion), channel_id=1, source_target_pairs={{0,4},{4,0},{8,12},{12,8},{16,20},{20,16},{24,28},{28,24},{1,5},{5... | collective-permute-start | bytes 3080 | tf_op jit(solution)/shard_map/ppermute | solution.py:293
  6.9 12.1 %collective-permute-start.1 = (f32[6,128,128]{2,1,0:T(8,128)S(1)}, f32[6,128,128]{2,1,0:T(8,128)S(1)}, u32[]{:S(2)}, u32[]{:S(2)}) collective-permute-start(f32[6,128,128]{2,1,0:T(8,128)S(1)} %get-tuple-element.43.strain_ref), channel_id=1, source_target_pairs={{0,4},{4,0},{8,12},{12,8},{16,20},{20,16},{24,28},{28,24},{1,5},{5... | collective-permute-start | bytes 1179656 | tf_op jit(solution)/shard_map/ppermute | solution.py:293
  7.4 14.1 %collective-permute-start.5 = (f32[6,128,128]{2,1,0:T(8,128)S(1)}, f32[6,128,128]{2,1,0:T(8,128)S(1)}, u32[]{:S(2)}, u32[]{:S(2)}) collective-permute-start(f32[6,128,128]{2,1,0:T(8,128)S(1)} %get-tuple-element.44.strain_ref), channel_id=1, source_target_pairs={{0,8},{4,12},{8,0},{12,4},{16,24},{20,28},{24,16},{28,20},{1,9},{5... | collective-permute-start | bytes 1179656 | tf_op jit(solution)/shard_map/ppermute | solution.py:293
  7.4 22.3 %collective-permute-start.3 = (f32[6,128,128]{2,1,0:T(8,128)S(1)}, f32[6,128,128]{2,1,0:T(8,128)S(1)}, u32[]{:S(2)}, u32[]{:S(2)}) collective-permute-start(f32[6,128,128]{2,1,0:T(8,128)S(1)} %get-tuple-element.52.strain_ref), channel_id=1, source_target_pairs={{0,4},{4,0},{8,12},{12,8},{16,20},{20,16},{24,28},{28,24},{1,5},{5... | collective-permute-start | bytes 1179656 | tf_op jit(solution)/shard_map/ppermute | solution.py:293
  9.7 28.1 %collective-permute-start.8 = (f32[6,128,128]{2,1,0:T(8,128)S(1)}, f32[6,128,128]{2,1,0:T(8,128)S(1)}, u32[]{:S(2)}, u32[]{:S(2)}) collective-permute-start(f32[6,128,128]{2,1,0:T(8,128)S(1)} %get-tuple-element.53.strain_ref), channel_id=1, source_target_pairs={{0,4},{4,0},{8,12},{12,8},{16,20},{20,16},{24,28},{28,24},{1,5},{5... | collective-permute-start | bytes 1179656 | tf_op jit(solution)/shard_map/ppermute | solution.py:293
  10.8 0.7 %copy-start.1 = (f32[2,4,6]{2,1,0:T(4,128)S(1)}, f32[2,4,6]{2,1,0:T(4,128)}, u32[]{:S(2)}) copy-start(f32[2,4,6]{2,1,0:T(4,128)} %dirs_ref.15) | copy-start | bytes 580
  11.5 0.7 %copy-start.3 = (f32[16]{0:T(128)S(1)}, f32[16]{0:T(128)}, u32[]{:S(2)}) copy-start(f32[16]{0:T(128)} %rock_ref.15) | copy-start | bytes 196
  20.9 12.7 %copy-start.5 = (bf16[2048,512]{1,0:T(8,128)(2,1)S(1)}, bf16[2048,512]{1,0:T(8,128)(2,1)}, u32[]{:S(2)}) copy-start(bf16[2048,512]{1,0:T(8,128)(2,1)} %param.11) | copy-start | bytes 6291460
  20.9 12.5 %collective-permute-start.2 = (f32[512,128]{1,0:T(8,128)S(1)}, f32[512,128]{1,0:T(8,128)S(1)}, u32[]{:S(2)}, u32[]{:S(2)}) collective-permute-start(f32[512,128]{1,0:T(8,128)S(1)} %get-tuple-element.47), channel_id=1, source_target_pairs={{0,8},{4,12},{8,0},{12,4},{16,24},{20,28},{24,16},{28,20},{1,9},{5... | collective-permute-start | bytes 786440 | tf_op jit(solution)/shard_map/ppermute | solution.py:293
  23.5 10.4 %collective-permute-start.9 = (f32[512,128]{1,0:T(8,128)S(1)}, f32[512,128]{1,0:T(8,128)S(1)}, u32[]{:S(2)}, u32[]{:S(2)}) collective-permute-start(f32[512,128]{1,0:T(8,128)S(1)} %get-tuple-element.51), channel_id=1, source_target_pairs={{0,16},{4,20},{8,24},{12,28},{16,0},{20,4},{24,8},{28,12},{1,17},{... | collective-permute-start | bytes 786440 | tf_op jit(solution)/shard_map/ppermute | solution.py:293
  31.7 10.6 %collective-permute-start.7 = (f32[512,128]{1,0:T(8,128)S(1)}, f32[512,128]{1,0:T(8,128)S(1)}, u32[]{:S(2)}, u32[]{:S(2)}) collective-permute-start(f32[512,128]{1,0:T(8,128)S(1)} %get-tuple-element.55), channel_id=1, source_target_pairs={{0,8},{4,12},{8,0},{12,4},{16,24},{20,28},{24,16},{28,20},{1,9},{5... | collective-permute-start | bytes 786440 | tf_op jit(solution)/shard_map/ppermute | solution.py:293
  33.5 4.3 %copy-start.4 = (f32[16]{0:T(128)S(1)}, f32[16]{0:T(128)}, u32[]{:S(2)}) copy-start(f32[16]{0:T(128)} %rock_ref.15) | copy-start | bytes 196
  33.5 11.1 %collective-permute-start.6 = (f32[256,128]{1,0:T(8,128)S(1)}, f32[256,128]{1,0:T(8,128)S(1)}, u32[]{:S(2)}, u32[]{:S(2)}) collective-permute-start(f32[256,128]{1,0:T(8,128)S(1)} %slice_add_fusion.3), channel_id=1, source_target_pairs={{0,16},{4,20},{8,24},{12,28},{16,0},{20,4},{24,8},{28,12},{1,17},{... | collective-permute-start | bytes 393224 | tf_op jit(solution)/shard_map/ppermute | solution.py:293
  33.9 12.4 %collective-permute-start.10 = (f32[256,128]{1,0:T(8,128)S(1)}, f32[256,128]{1,0:T(8,128)S(1)}, u32[]{:S(2)}, u32[]{:S(2)}) collective-permute-start(f32[256,128]{1,0:T(8,128)S(1)} %slice_add_fusion.2), channel_id=1, source_target_pairs={{0,4},{4,0},{8,12},{12,8},{16,20},{20,16},{24,28},{28,24},{1,5},{5... | collective-permute-start | bytes 393224 | tf_op jit(solution)/shard_map/ppermute | solution.py:293
  39.7 9.0 %collective-permute-start.12 = (f32[512,128]{1,0:T(8,128)S(1)}, f32[512,128]{1,0:T(8,128)S(1)}, u32[]{:S(2)}, u32[]{:S(2)}) collective-permute-start(f32[512,128]{1,0:T(8,128)S(1)} %get-tuple-element.62), channel_id=1, source_target_pairs={{0,8},{4,12},{8,0},{12,4},{16,24},{20,28},{24,16},{28,20},{1,9},{5... | collective-permute-start | bytes 786440 | tf_op jit(solution)/shard_map/ppermute | solution.py:293
  42.3 7.5 %collective-permute-start.11 = (f32[256,128]{1,0:T(8,128)S(1)}, f32[256,128]{1,0:T(8,128)S(1)}, u32[]{:S(2)}, u32[]{:S(2)}) collective-permute-start(f32[256,128]{1,0:T(8,128)S(1)} %slice_add_fusion.1), channel_id=1, source_target_pairs={{0,16},{4,20},{8,24},{12,28},{16,0},{20,4},{24,8},{28,12},{1,17},{... | collective-permute-start | bytes 393224 | tf_op jit(solution)/shard_map/ppermute | solution.py:293
  44.6 6.7 %collective-permute-start.15 = (f32[256,128]{1,0:T(8,128)S(1)}, f32[256,128]{1,0:T(8,128)S(1)}, u32[]{:S(2)}, u32[]{:S(2)}) collective-permute-start(f32[256,128]{1,0:T(8,128)S(1)} %add_add_fusion.3), channel_id=1, source_target_pairs={{0,2},{1,3},{2,0},{3,1},{4,6},{5,7},{6,4},{7,5},{8,10},{9,11},{10,... | collective-permute-start | bytes 393224 | tf_op jit(solution)/shard_map/ppermute | solution.py:293
  46.4 6.1 %collective-permute-start.14 = (f32[256,128]{1,0:T(8,128)S(1)}, f32[256,128]{1,0:T(8,128)S(1)}, u32[]{:S(2)}, u32[]{:S(2)}) collective-permute-start(f32[256,128]{1,0:T(8,128)S(1)} %add_add_fusion.2), channel_id=1, source_target_pairs={{0,2},{1,3},{2,0},{3,1},{4,6},{5,7},{6,4},{7,5},{8,10},{9,11},{10,... | collective-permute-start | bytes 393224 | tf_op jit(solution)/shard_map/ppermute | solution.py:293
  48.8 7.3 %collective-permute-start.13 = (f32[256,128]{1,0:T(8,128)S(1)}, f32[256,128]{1,0:T(8,128)S(1)}, u32[]{:S(2)}, u32[]{:S(2)}) collective-permute-start(f32[256,128]{1,0:T(8,128)S(1)} %slice_add_fusion), channel_id=1, source_target_pairs={{0,16},{4,20},{8,24},{12,28},{16,0},{20,4},{24,8},{28,12},{1,17},{... | collective-permute-start | bytes 393224 | tf_op jit(solution)/shard_map/ppermute | solution.py:293
  49.7 8.1 %collective-permute-start.16 = (f32[256,128]{1,0:T(8,128)S(1)}, f32[256,128]{1,0:T(8,128)S(1)}, u32[]{:S(2)}, u32[]{:S(2)}) collective-permute-start(f32[256,128]{1,0:T(8,128)S(1)} %add_add_fusion.1), channel_id=1, source_target_pairs={{0,2},{1,3},{2,0},{3,1},{4,6},{5,7},{6,4},{7,5},{8,10},{9,11},{10,... | collective-permute-start | bytes 393224 | tf_op jit(solution)/shard_map/ppermute | solution.py:293
  56.1 5.0 %collective-permute-start.17 = (f32[256,128]{1,0:T(8,128)S(1)}, f32[256,128]{1,0:T(8,128)S(1)}, u32[]{:S(2)}, u32[]{:S(2)}) collective-permute-start(f32[256,128]{1,0:T(8,128)S(1)} %add_add_fusion), channel_id=1, source_target_pairs={{0,2},{1,3},{2,0},{3,1},{4,6},{5,7},{6,4},{7,5},{8,10},{9,11},{10,... | collective-permute-start | bytes 393224 | tf_op jit(solution)/shard_map/ppermute | solution.py:293
  57.7 3.6 %collective-permute-start.18 = (f32[1024,128]{1,0:T(8,128)S(1)}, f32[1024,128]{1,0:T(8,128)S(1)}, u32[]{:S(2)}, u32[]{:S(2)}) collective-permute-start(f32[1024,128]{1,0:T(8,128)S(1)} %pad_maximum_fusion.refs_16_), channel_id=1, source_target_pairs={{0,1},{1,0},{2,3},{3,2},{4,5},{5,4},{6,7},{7,6},{8,9},{9,8},{10,11... | collective-permute-start | bytes 1572872 | tf_op jit(solution)/shard_map/ppermute | solution.py:293
  61.2 2.0 %collective-permute-start.19 = (f32[1024,128]{1,0:T(8,128)S(1)}, f32[1024,128]{1,0:T(8,128)S(1)}, u32[]{:S(2)}, u32[]{:S(2)}) collective-permute-start(f32[1024,128]{1,0:T(8,128)S(1)} %pad_maximum_fusion.1.refs_18_), channel_id=1, source_target_pairs={{0,1},{1,0},{2,3},{3,2},{4,5},{5,4},{6,7},{7,6},{8,9},{9,8},{10,11... | collective-permute-start | bytes 1572872 | tf_op jit(solution)/shard_map/ppermute | solution.py:293

commit v4 on v3

--- a/solution.py
+++ b/solution.py
@@ -16,30 +16,33 @@
 VMEM_LIMIT = 12 * 1024 * 1024
 COST = 1024
 SCHEDULE = (
-    ("begin", 0),
-    ("begin", 3),
+    ("begin", 0, 1),
     ("first", 0),
+    ("first", 1),
+    ("begin", 2, 3),
+    ("middle", 0),
+    ("first", 2),
+    ("rows", 0, 1),
+    ("rows", 2, 3),
+    ("middle", 1),
     ("first", 3),
-    ("begin", 1),
-    ("begin", 2),
-    ("first", 1),
-    ("middle", 0),
-    ("rows", 0, 3, 1, 2),
-    ("middle", 3),
-    ("first", 2),
-    ("middle", 1),
     ("final", 0),
-    ("final", 3),
     ("middle", 2),
     ("final", 1),
     ("arrive", 0),
-    ("arrive", 3),
+    ("middle", 3),
     ("final", 2),
-    ("near", 0, 3, 1, 2),
     ("arrive", 1),
-    ("far", 0, 3, 1, 2),
-    ("multiply", 0, 3, 1, 2),
+    ("near", 0, 1),
+    ("far", 0, 1),
+    ("final", 3),
+    ("multiply", 0, 1),
+    ("near", 2, 3),
+    ("arrive", 2),
+    ("far", 2, 3),
+    ("multiply", 2, 3),
 )
+SCHEDULED = (1, 1, 1, 1)
 SCALE = math.sqrt(0.5 / math.log(2.0))
 
 
@@ -108,91 +111,109 @@
     )
 
 
-def image_kernel(count_ref, list_ref, dirs_ref, rock_ref, strain_ref, *rest):
-    proj = rest[-1]
-    comps, tiles, pix = strain_ref.shape
-    angles = count_ref.shape[0]
-    qcount = dirs_ref.shape[1]
+def prepared_rocks(rock_ref):
     rocks = rock_ref.shape[0]
-    step = 4 * GROUP
-    if len(rest) == 2:
-        init, outs = None, rest[:1]
-    else:
-        init, outs = rest[0], rest[1:-2]
-    acc = outs[0] if init is None else rest[-2]
-    blocks = pix // LANES
-    rows_out = acc.shape[0] // blocks
     row = lax.broadcasted_iota(jnp.int32, (rocks, LANES), 0)
     rock = jnp.zeros((rocks, LANES), jnp.float32)
     for i in range(rocks):
         rock = jnp.where(row == i, rock_ref[i] * SCALE, rock)
-    if init is None:
-        acc[...] = jnp.zeros_like(acc)
-    else:
-        acc[...] = init[...]
-
-    for b in range(blocks):
-        lanes = slice(b * LANES, (b + 1) * LANES)
-
-        for k in range(angles * qcount):
-            scaled = [dirs_ref[k // qcount, k % qcount, c] * SCALE for c in range(comps)]
-            for start in range(0, tiles, step):
-                rows = pl.ds(start, step)
-                total = strain_ref[0, rows, lanes] * scaled[0]
-                for c in range(1, comps):
-                    total = total + strain_ref[c, rows, lanes] * scaled[c]
-                proj[k, rows, :] = total
-
-        for angle in range(angles):
-
-            @pl.loop(0, (count_ref[angle] + GROUP - 1) // GROUP)
-            def _(block):
-                sums = []
-                targets = []
-                for j in range(GROUP):
-                    code = list_ref[angle, block * GROUP + j]
-                    tile = code & (tiles - 1)
-                    target = (code >> (tiles - 1).bit_length()) * rocks
-                    targets.append(pl.multiple_of(target + b * rows_out, rocks))
-                    total = None
-                    for q in range(qcount):
-                        p = proj[angle * qcount + q, pl.ds(tile, 1), :]
-                        d = jnp.broadcast_to(p, (rocks, LANES)) - rock
-                        e = jnp.exp2(-(d * d))
-                        total = e if total is None else total + e
-                    sums.append(total)
-                for target, total in zip(targets, sums):
-                    acc[pl.ds(target, rocks), :] += total
-
-    if init is not None:
-        start = 0
-        for out in outs:
-            out[...] = acc[pl.ds(start, out.shape[0]), :]
-            start += out.shape[0]
-
-
-def add_images(name, listing, weights, rock, strain, init, sizes):
-    counts, lists = listing
-    comps, tiles, pix = strain.shape
-    angles = counts.shape[0]
-    qcount = weights.shape[1]
+    return rock
+
+
+def add_tiles(count_ref, list_ref, dirs_ref, rock, strain_ref, proj, acc):
+    angles, qcount, comps = dirs_ref.shape
+    tiles, lanes = proj.shape[1:]
+    rocks = rock.shape[0]
+    step = 4 * GROUP
+    twice = rock + rock
+    for k in range(angles * qcount):
+        scaled = [dirs_ref[k // qcount, k % qcount, c] * SCALE for c in range(comps)]
+        for start in range(0, tiles, step):
+            total = None
+            for c in range(comps):
+                part = strain_ref[pl.ds((c * tiles + start) // GROUP, step // GROUP)] * scaled[c]
+                total = part if total is None else total + part
+            proj[k, pl.ds(start, step), :] = total.reshape(step, lanes)
+
+    for angle in range(angles):
+
+        @pl.loop(0, (count_ref[angle] + GROUP - 1) // GROUP)
+        def _(block):
+            sums = []
+            targets = []
+            for j in range(GROUP):
+                code = list_ref[angle, block * GROUP + j]
+                tile = code & (tiles - 1)
+                target = (code >> (tiles - 1).bit_length()) * rocks
+                targets.append(pl.multiple_of(target, rocks))
+                total = None
+                for q in range(qcount):
+                    p = jnp.broadcast_to(proj[angle * qcount + q, pl.ds(tile, 1), :], (rocks, lanes))
+                    e = jnp.exp2(p * (twice - p))
+                    total = e if total is None else total + e
+                sums.append(total)
+            for target, total in zip(targets, sums):
+                acc[pl.ds(target, rocks), :] += total
+
+
+def own_images(plan_of, listings, dirs, rock, strains, tiles, rows):
+    used = len(listings)
+    count = len(strains)
+    angles, qcount, comps = dirs.shape
+
+    def kernel(*refs):
+        list_refs = refs[: 2 * used]
+        dirs_ref, rock_ref = refs[2 * used : 2 * used + 2]
+        strain_refs = refs[2 * used + 2 : 2 * used + 2 + count]
+        outs, proj = refs[-1 - count : -1], refs[-1]
+        rock = prepared_rocks(rock_ref)
+        for c in range(count):
+            k = plan_of[c]
+            outs[c][...] = jnp.zeros_like(outs[c])
+            add_tiles(list_refs[2 * k], list_refs[2 * k + 1], dirs_ref, rock, strain_refs[c], proj, outs[c])
+
     smem = pl.BlockSpec(memory_space=pltpu.SMEM)
     vmem = pl.BlockSpec(memory_space=pltpu.VMEM)
-    scratch = [pltpu.VMEM((angles * qcount, tiles, LANES), jnp.float32)]
-    before = ()
-    if init is not None:
-        before = (init,)
-        scratch = [pltpu.VMEM(init.shape, jnp.float32)] + scratch
     return pl.pallas_call(
-        image_kernel,
-        out_shape=tuple(jax.ShapeDtypeStruct((size, LANES), jnp.float32) for size in sizes),
-        in_specs=[smem, smem, smem, smem] + [vmem] * (1 + len(before)),
-        out_specs=tuple(vmem for size in sizes),
-        scratch_shapes=scratch,
-        compiler_params=pltpu.CompilerParams(vmem_limit_bytes=VMEM_LIMIT),
+        kernel,
+        out_shape=[jax.ShapeDtypeStruct((rows, LANES), jnp.float32)] * count,
+        in_specs=[smem] * (2 * used + 2) + [vmem] * count,
+        out_specs=[vmem] * count,
+        scratch_shapes=[pltpu.VMEM((angles * qcount, tiles, LANES), jnp.float32)],
+        compiler_params=pltpu.CompilerParams(vmem_limit_bytes=VMEM_LIMIT // 2),
         cost_estimate=pl.CostEstimate(flops=COST, bytes_accessed=COST, transcendentals=0),
-        name=name,
-    )(counts, lists, weights, rock, strain, *before)
+        name="own_images",
+    )(*[x for listing in listings for x in listing], dirs, rock, *strains)
+
+
+def other_images(listing, dirs, rock, strain, init, tiles, half):
+    angles, qcount, comps = dirs.shape
+    rocks = rock.shape[0]
+
+    def kernel(count_ref, list_ref, dirs_ref, rock_ref, strain_ref, init_ref, sent_ref, kept_ref, acc, proj):
+        rock = prepared_rocks(rock_ref)
+        acc[...] = init_ref[...]
+        add_tiles(count_ref, list_ref, dirs_ref, rock, strain_ref, proj, acc)
+        factor = jnp.exp2(-(rock * rock))
+        for start, out in ((0, sent_ref), (half, kept_ref)):
+            for row in range(0, half, rocks):
+                out[pl.ds(row, rocks), :] = acc[pl.ds(start + row, rocks), :] * factor
+
+    smem = pl.BlockSpec(memory_space=pltpu.SMEM)
+    vmem = pl.BlockSpec(memory_space=pltpu.VMEM)
+    return pl.pallas_call(
+        kernel,
+        out_shape=[jax.ShapeDtypeStruct((half, LANES), jnp.float32)] * 2,
+        in_specs=[smem] * 4 + [vmem] * 2,
+        out_specs=[vmem] * 2,
+        scratch_shapes=[
+            pltpu.VMEM(init.shape, jnp.float32),
+            pltpu.VMEM((angles * qcount, tiles, LANES), jnp.float32),
+        ],
+        compiler_params=pltpu.CompilerParams(vmem_limit_bytes=VMEM_LIMIT // 4),
+        cost_estimate=pl.CostEstimate(flops=COST, bytes_accessed=COST, transcendentals=0),
+        name="other_images",
+    )(*listing, dirs, rock, strain, init)
 
 
 def resolve(norm, unit, total, blocks, parts):
@@ -223,32 +244,6 @@
         cost_estimate=pl.CostEstimate(flops=COST, bytes_accessed=COST, transcendentals=0),
         name="resolve",
     )(*blocks, *parts, *before)
-
-
-def cut(by_comp):
-    comps, tiles, pix = by_comp.shape
-    count = pix // LANES
-
-    def kernel(source, *rest):
-        outs, sems = rest[:count], rest[count]
-        copies = [
-            pltpu.make_async_copy(source.at[:, :, pl.ds(c * LANES, LANES)], outs[c], sems.at[c]) for c in range(count)
-        ]
-        for copy in copies:
-            copy.start()
-        for copy in copies:
-            copy.wait()
-
-    return pl.pallas_call(
-        kernel,
-        out_shape=[jax.ShapeDtypeStruct((comps, tiles, LANES), jnp.float32)] * count,
-        in_specs=[pl.BlockSpec(memory_space=pl.ANY)],
-        out_specs=[pl.BlockSpec(memory_space=pltpu.VMEM)] * count,
-        scratch_shapes=[pltpu.SemaphoreType.DMA((count,))],
-        compiler_params=pltpu.CompilerParams(vmem_limit_bytes=VMEM_LIMIT),
-        cost_estimate=pl.CostEstimate(flops=COST, bytes_accessed=COST, transcendentals=0),
-        name="cut",
-    )(by_comp)
 
 
 def bit(value, number):
@@ -288,14 +283,24 @@
     me = lax.axis_index("slab")
     chunks = pix // LANES
 
+    odd = lax.axis_index("rock") & 1
+
     def swap(value, number, axis="slab"):
-        size = lax.axis_size(axis)
-        return lax.ppermute(value, axis, [(i, i ^ (1 << number)) for i in range(size)])
-
-    plans = [(0, tuple(range(1, bits))), (1, tuple(range(2, bits)) + (0,))]
-    plan_of = [0] * (chunks - 1) + [1] if chunks > 1 else [0]
-    early = [c for c in range(chunks) if plan_of[c] == 0]
-    late = [c for c in range(chunks) if plan_of[c] == 1]
+        if axis == "slab" and number[0] != number[1]:
+            pairs = [
+                (i * rock_size + j, (i ^ (1 << number[j & 1])) * rock_size + j)
+                for i in range(slabs)
+                for j in range(rock_size)
+            ]
+            return lax.ppermute(value, ("slab", "rock"), pairs)
+        number = number[0] if axis == "slab" else number
+        return lax.ppermute(value, axis, [(i, i ^ (1 << number)) for i in range(lax.axis_size(axis))])
+
+    same = [(k, k) for k in range(bits)]
+    plans = [(same[0], tuple(same[1:])), ((1, 0), ((0, 1),) + tuple(same[2:]))]
+    plan_of = [1] * chunks
+    every = list(range(chunks))
+    launches = every
     last = []
 
     def tie(value):
@@ -305,38 +310,66 @@
         last[:] = [value]
         return value
 
-    own = cut(strain.transpose(1, 0, 2))
-    other = {c: swap(own[c], plans[plan_of[c]][0]) for c in early[:1] + late + early[1:]}
-    mark(own[0])
-    info = tie(dest[:, :, 0] * ROWS + det_row)
+    info = dest[:, :, 0] * ROWS + det_row
+    info_rows = angles * tiles // LANES
+    padded = jnp.pad(info.astype(jnp.float32).reshape(info_rows, LANES), ((0, -info_rows % GROUP), (0, 0)))
+    by_comp = strain.transpose(1, 0, 2).reshape(comps * tiles // GROUP, GROUP, pix)
+    padded = padded.reshape(-1, GROUP, LANES)
+    own = {}
+    other = {}
+    told = []
+    source = by_comp
+    for c in launches:
+        block = source[:, :, c * LANES : (c + 1) * LANES]
+        if plan_of[c] not in told:
+            told.append(plan_of[c])
+            block = jnp.concatenate([block, padded], axis=0)
+        own[c] = block
+        other[c] = swap(block, plans[plan_of[c]][0])
+        if c == launches[0]:
+            mark(block)
+            source = tie(by_comp)
+    mark(own[launches[-1]])
     used = sorted(set(plan_of))
-    other_info = {k: swap(info, plans[k][0]) for k in used}
-    own_list = {k: listing(info, me, *plans[k], angles, units) for k in used}
-    other_list = {k: listing(other_info[k], me, *plans[k], angles, units) for k in used}
-
+
+    def numbers(k):
+        raw, halves = plans[k]
+        pick = lambda pair: pair[0] if pair[0] == pair[1] else jnp.where(odd == 1, pair[1], pair[0])
+        return pick(raw), [pick(pair) for pair in halves]
+
+    own_list = {k: listing(tie(info), me, *numbers(k), angles, units) for k in used}
+    other_list = {}
+
+    def learn(c):
+        arrived = mark(tie(other[c]))
+        below = arrived[by_comp.shape[0] :].reshape(-1, LANES)[:info_rows]
+        below = below.reshape(angles, tiles).astype(jnp.int32)
+        other_list[plan_of[c]] = listing(below, me, *numbers(plan_of[c]), angles, units)
 
     partial = {}
     held = {}
     flying = {}
     half = image_rows // 2
 
-    def begin(c):
-        (partial[c],) = add_images(
-            "own_images",
-            own_list[plan_of[c]],
+    def begin(*group):
+        kinds = sorted({plan_of[c] for c in group})
+        found = own_images(
+            [kinds.index(plan_of[c]) for c in group],
+            [own_list[k] for k in kinds],
             dirs,
             rock_angles,
-            tie(own[c]),
-            None,
-            [image_rows + rocks],
-        )
-        mark(partial[c])
+            [tie(own[group[0]])] + [own[c] for c in group[1:]],
+            tiles,
+            image_rows + rocks,
+        )
+        partial.update(zip(group, found))
+        mark(found[0])
 
     def first(c):
         k = plan_of[c]
-        sent, held[c] = add_images(
-            "other_images", other_list[k], dirs, rock_angles, tie(other[c]), partial[c], [half, half]
-        )
+        if k not in other_list:
+            learn(c)
+        sent, held[c] = other_images(other_list[k], dirs, rock_angles, tie(other[c]), partial[c], tiles, half)
         mark(sent)
         flying[c] = swap(sent, plans[k][1][0])
 
@@ -394,11 +427,10 @@
         total = result[-1] if result else None
         result.append(mark(resolve(norm, unit, total, blocks[group], [tie(parts[0])] + parts[1:])))
 
-    if (len(early), len(late)) == (3, 1):
+    if plan_of == list(SCHEDULED):
         steps = SCHEDULE
     else:
-        every = early + late
-        steps = [(name, c) for name in ("begin", "first", "middle", "final") for c in every]
+        steps = [("begin", *every)] + [(name, c) for name in ("first", "middle", "final") for c in every]
         steps += [("rows", *every), ("near", *every), ("far", *every), ("multiply", *every)]
     doing = dict(begin=begin, first=first, middle=middle, final=final, arrive=arrive, near=near, far=far, rows=rows)
     doing["multiply"] = multiply
@@ -415,7 +447,7 @@
     slots = slabs * (2 * tiles // slabs)
     images_smaller = slabs * ROWS * rock_angles.shape[0] * pix <= slots * dirs.shape[1] * vox
     powers = all(size & (size - 1) == 0 for size in (slabs, rock_size, tiles))
-    regular = powers and slabs >= 4 and tiles % (4 * GROUP) == 0 and vox == pix and pix % LANES == 0
+    regular = powers and slabs >= 4 and tiles % LANES == 0 and vox == pix and pix % LANES == 0
     plan = by_images if images_smaller and regular else by_tiles
     return plan(strain, dest, det_row, dirs, rock_angles, resolution)
 

time: 65.6 us -> 62.1 us (0.947)
  Pallas kernels: 17.5 us -> 13.4 us
  local copies, waits for them, and re-layouts: 2.99 us -> 1.29 us
  other arithmetic: 2.15 us -> 3.63 us
  starting transfers between devices: 26 us -> 27.3 us
  waiting for transfers between devices: 16.3 us -> 15.4 us
    pallas_call x9 -> x6, Pallas kernels: 15.4 us -> 11.2 us  [the longest x4 6.08 us: other_images(): pl.pallas_call(kernel, out_shape=[jax.ShapeDtypeStruct((half, LANES), jnp...]
    unnamed x12 -> x8, local copies, waits for them, and re-layouts: 2.76 us -> 0.01 us
    ppermute x20, starting transfers between devices: 26 us -> 27.3 us  [the longest x12 17.1 us: swap(): lax.ppermute(value, axis, [(i, i ^ 1 << number) for i in range(lax.axis_s...]
    slice x0 -> x2, local copies, waits for them, and re-layouts: none -> 1.1 us  [by_images(): block = source[:, :, c * LANES:(c + 1) * LANES]]
    add x4, other arithmetic: 0.1 us -> 1 us  [final(): image[c] = mark(held[c] + tie(flying[c]))]
    add x4, other arithmetic: 0.07 us -> 0.97 us  [middle(): sent = mark(held[c][:rows] + arrived[:rows])]
    ppermute x20, waiting for transfers between devices: 16.3 us -> 15.4 us  [the longest x8 10.6 us: swap(): return lax.ppermute(value, ('slab', 'rock'), pairs)]
    convert_element_type x0 -> x1, other arithmetic: none -> 0.82 us  [by_images(): info.astype(jnp.float32).reshape(info_rows, LANES)]
  transfers between devices with their start and end apart: 20 -> 20, of which waited for: 7 -> 8; matrix products, arithmetic and copies ran while one was open for 3% -> 5% of each run, Pallas kernels for 23% -> 19%
where the time goes in v4:
time: 62.1 us; the launch traced here: 61.3 us
  starting transfers between devices  27.3 us (44%)
  waiting for transfers between devices  15.4 us (25%)
  Pallas kernels  13.4 us (22%)
  other arithmetic  3.63 us (6%)
  local copies, waits for them, and re-layouts  1.29 us (2%)
    ppermute x12, starting transfers between devices, swap(): lax.ppermute(value, axis, [(i, i ^ 1 << number) for i in range(lax.axis_s...  17.1 us
    ppermute x8, waiting for transfers between devices, swap(): return lax.ppermute(value, ('slab', 'rock'), pairs)  10.6 us
    ppermute x8, starting transfers between devices, swap(): return lax.ppermute(value, ('slab', 'rock'), pairs)  10.2 us
    pallas_call x4, Pallas kernels, other_images(): pl.pallas_call(kernel, out_shape=[jax.ShapeDtypeStruct((half, LANES), jnp...  6.08 us
    pallas_call x2, Pallas kernels, own_images(): pl.pallas_call(kernel, out_shape=[jax.ShapeDtypeStruct((rows, LANES), jnp...  5.08 us
    ppermute x12, waiting for transfers between devices, swap(): lax.ppermute(value, axis, [(i, i ^ 1 << number) for i in range(lax.axis_s...  4.81 us
    pallas_call x2, Pallas kernels, resolve(): pl.pallas_call(kernel, out_shape=jax.ShapeDtypeStruct((unit, cols), jnp.f...  2.22 us
  transfers between devices with their start and end apart: 20, of which 8 were waited for; matrix products, arithmetic and copies ran while one was open for 5% of the time, Pallas kernels for 19%

profile of v4, /device:TPU:0, one launch (start us, length us, event | category | flops | bytes accessed | tf_op | source)
XLA Modules:
  0.0 61.3 jit_solution(9539696260045404871)
XLA Ops:
  0.0 0.8 %fusion.8 = (f32[2,128]{1,0:T(2,128)S(1)}, s32[2,128]{1,0:T(2,128)S(1)}) fusion(s32[2,128]{1,0:T(2,128)} %param.8, s32[2,128,1]{1,0,2:T(2,128)} %bitcast.33), kind=kLoop, calls=%fused_computation.75 | loop fusion | flops 768 | bytes 4096 | tf_op jit(solution)/shard_map/convert_element_type | solution.py:315
  0.8 1.0 %slice.87 = f32[96,8,128]{2,1,0:T(8,128)S(1)} slice(f32[96,8,512]{2,1,0:T(8,128)} %bitcast.31), slice={[0:96], [0:8], [0:128]} | slice | bytes 786432 | tf_op jit(solution)/shard_map/slice | solution.py:323
  1.9 3.1 %collective-permute-start = (f32[97,8,128]{2,1,0:T(8,128)S(1)}, f32[97,8,128]{2,1,0:T(8,128)S(1)}, u32[]{:S(2)}, u32[]{:S(2)}) collective-permute-start(f32[97,8,128]{2,1,0:T(8,128)S(1)} %pad_maximum_fusion.refs_4_), channel_id=1, source_target_pairs={{0,8},{1,5},{2,10},{3,7},{4,12},{5,1},{6,14},{7,3},{8,0},{9,13},{1... | collective-permute-start | bytes 1191944 | tf_op jit(solution)/shard_map/ppermute | solution.py:295
  5.6 2.5 %own_images.2 = (f32[1040,128]{1,0:T(8,128)S(1)}, f32[1040,128]{1,0:T(8,128)S(1)}) custom-call(s32[2]{0:T(128)S(1)} %get-tuple-element.87.refs_0_, s32[2,128]{1,0:T(2,128)S(1)} %broadcast_add_fusion.1.refs_1_, f32[2,4,6]{2,1,0:T(4,128)S(1)} %copy-done, f32[16]{0:T(128)S(1)} %copy-done.1, f32[97,8,128]{2,1,0:T(8,128)S(1)} %pad_maximum_fusion.refs_4_, ...), custom_call_target="tpu_custom_call" | custom-call | flops 1024 | bytes 1024 | tf_op jit(solution)/shard_map/own_images/pallas_call | solution.py:177
  8.1 2.6 %collective-permute-done.strain_ref = f32[97,8,128]{2,1,0:T(8,128)S(1)} collective-permute-done((f32[97,8,128]{2,1,0:T(8,128)S(1)}, f32[97,8,128]{2,1,0:T(8,128)S(1)}, u32[]{:S(2)}, u32[]{:S(2)}) %collective-permute-start) | collective-permute-done | bytes 397344 | tf_op jit(solution)/shard_map/ppermute | solution.py:295
  11.2 1.5 %other_images.4 = (f32[512,128]{1,0:T(8,128)S(1)}, f32[512,128]{1,0:T(8,128)S(1)}) custom-call(s32[2]{0:T(128)S(1)} %get-tuple-element.83.count_ref, s32[2,128]{1,0:T(2,128)S(1)} %broadcast_add_fusion.list_ref, f32[2,4,6]{2,1,0:T(4,128)S(1)} %copy-done, f32[16]{0:T(128)S(1)} %copy-done.1, f32[97,8,128]{2,1,0:T(8,128)S(1)} %collective-permute-done.strain_ref, ...), custom_call_target="tpu_custom_call" | custom-call | flops 1024 | bytes 1024 | tf_op jit(solution)/shard_map/other_images/pallas_call | solution.py:204
  12.7 2.1 %collective-permute-start.2 = (f32[512,128]{1,0:T(8,128)S(1)}, f32[512,128]{1,0:T(8,128)}, u32[]{:S(2)}, u32[]{:S(2)}) collective-permute-start(f32[512,128]{1,0:T(8,128)S(1)} %get-tuple-element.50), channel_id=1, source_target_pairs={{0,4},{1,9},{2,6},{3,11},{4,0},{5,13},{6,2},{7,15},{8,12},{9,1},{1... | collective-permute-start | bytes 786440 | tf_op jit(solution)/shard_map/ppermute | solution.py:295
  14.8 2.0 %collective-permute-start.1 = (f32[96,8,128]{2,1,0:T(8,128)S(1)}, f32[96,8,128]{2,1,0:T(8,128)S(1)}, u32[]{:S(2)}, u32[]{:S(2)}) collective-permute-start(f32[96,8,128]{2,1,0:T(8,128)S(1)} %get-tuple-element.54.refs_4_), channel_id=1, source_target_pairs={{0,8},{1,5},{2,10},{3,7},{4,12},{5,1},{6,14},{7,3},{8,0},{9,13},{1... | collective-permute-start | bytes 1179656 | tf_op jit(solution)/shard_map/ppermute | solution.py:295
  16.9 1.5 %other_images.5 = (f32[512,128]{1,0:T(8,128)S(1)}, f32[512,128]{1,0:T(8,128)S(1)}) custom-call(s32[2]{0:T(128)S(1)} %get-tuple-element.83.count_ref, s32[2,128]{1,0:T(2,128)S(1)} %broadcast_add_fusion.list_ref, f32[2,4,6]{2,1,0:T(4,128)S(1)} %copy-done, f32[16]{0:T(128)S(1)} %copy-done.1, f32[96,8,128]{2,1,0:T(8,128)S(1)} %collective-permute-done.3.strain_ref, ...), custom_call_target="tpu_custom_call" | custom-call | flops 1024 | bytes 1024 | tf_op jit(solution)/shard_map/other_images/pallas_call | solution.py:204
  18.4 0.7 %collective-permute-start.7 = (f32[512,128]{1,0:T(8,128)S(1)}, f32[512,128]{1,0:T(8,128)S(1)}, u32[]{:S(2)}, u32[]{:S(2)}) collective-permute-start(f32[512,128]{1,0:T(8,128)S(1)} %get-tuple-element.53), channel_id=1, source_target_pairs={{0,4},{1,9},{2,6},{3,11},{4,0},{5,13},{6,2},{7,15},{8,12},{9,1},{1... | collective-permute-start | bytes 786440 | tf_op jit(solution)/shard_map/ppermute | solution.py:295
  19.1 2.5 %own_images.3 = (f32[1040,128]{1,0:T(8,128)S(1)}, f32[1040,128]{1,0:T(8,128)S(1)}) custom-call(s32[2]{0:T(128)S(1)} %get-tuple-element.87.refs_0_, s32[2,128]{1,0:T(2,128)S(1)} %broadcast_add_fusion.1.refs_1_, f32[2,4,6]{2,1,0:T(4,128)S(1)} %copy-done, f32[16]{0:T(128)S(1)} %copy-done.1, f32[96,8,128]{2,1,0:T(8,128)S(1)} %get-tuple-element.54.refs_4_, ...), custom_call_target="tpu_custom_call" | custom-call | flops 1024 | bytes 1024 | tf_op jit(solution)/shard_map/own_images/pallas_call | solution.py:177
  22.1 0.9 %slice_add_fusion.3 = f32[256,128]{1,0:T(8,128)S(1)} fusion(f32[512,128]{1,0:T(8,128)} %collective-permute-done.2, f32[512,128]{1,0:T(8,128)S(1)} %get-tuple-element.49), kind=kLoop, calls=%fused_computation.12 | loop fusion | flops 32768 | bytes 393216 | tf_op jit(solution)/shard_map/add | solution.py:380
  23.0 3.1 %collective-permute-start.5 = (f32[256,128]{1,0:T(8,128)S(1)}, f32[256,128]{1,0:T(8,128)S(1)}, u32[]{:S(2)}, u32[]{:S(2)}) collective-permute-start(f32[256,128]{1,0:T(8,128)S(1)} %slice_add_fusion.3), channel_id=1, source_target_pairs={{0,16},{4,20},{8,24},{12,28},{16,0},{20,4},{24,8},{28,12},{1,17},{... | collective-permute-start | bytes 393224 | tf_op jit(solution)/shard_map/ppermute | solution.py:297
  26.2 0.7 %collective-permute-done.1.strain_ref = f32[96,8,128]{2,1,0:T(8,128)S(1)} collective-permute-done((f32[96,8,128]{2,1,0:T(8,128)S(1)}, f32[96,8,128]{2,1,0:T(8,128)S(1)}, u32[]{:S(2)}, u32[]{:S(2)}) %collective-permute-start.1) | collective-permute-done | bytes 393248 | tf_op jit(solution)/shard_map/ppermute | solution.py:295
  26.8 1.5 %other_images.6 = (f32[512,128]{1,0:T(8,128)S(1)}, f32[512,128]{1,0:T(8,128)S(1)}) custom-call(s32[2]{0:T(128)S(1)} %get-tuple-element.83.count_ref, s32[2,128]{1,0:T(2,128)S(1)} %broadcast_add_fusion.list_ref, f32[2,4,6]{2,1,0:T(4,128)S(1)} %copy-done, f32[16]{0:T(128)S(1)} %copy-done.1, f32[96,8,128]{2,1,0:T(8,128)S(1)} %collective-permute-done.1.strain_ref, ...), custom_call_target="tpu_custom_call" | custom-call | flops 1024 | bytes 1024 | tf_op jit(solution)/shard_map/other_images/pallas_call | solution.py:204
  28.4 1.0 %collective-permute-start.4 = (f32[512,128]{1,0:T(8,128)S(1)}, f32[512,128]{1,0:T(8,128)S(1)}, u32[]{:S(2)}, u32[]{:S(2)}) collective-permute-start(f32[512,128]{1,0:T(8,128)S(1)} %get-tuple-element.58), channel_id=1, source_target_pairs={{0,4},{1,9},{2,6},{3,11},{4,0},{5,13},{6,2},{7,15},{8,12},{9,1},{1... | collective-permute-start | bytes 786440 | tf_op jit(solution)/shard_map/ppermute | solution.py:295
  29.6 1.5 %collective-permute-start.11 = (f32[256,128]{1,0:T(8,128)S(1)}, f32[256,128]{1,0:T(8,128)S(1)}, u32[]{:S(2)}, u32[]{:S(2)}) collective-permute-start(f32[256,128]{1,0:T(8,128)S(1)} %slice_add_fusion.2), channel_id=1, source_target_pairs={{0,16},{4,20},{8,24},{12,28},{16,0},{20,4},{24,8},{28,12},{1,17},{... | collective-permute-start | bytes 393224 | tf_op jit(solution)/shard_map/ppermute | solution.py:297
  31.1 6.8 %collective-permute-done.6.strain_ref = f32[96,8,128]{2,1,0:T(8,128)S(1)} collective-permute-done((f32[96,8,128]{2,1,0:T(8,128)S(1)}, f32[96,8,128]{2,1,0:T(8,128)S(1)}, u32[]{:S(2)}, u32[]{:S(2)}) %collective-permute-start.6) | collective-permute-done | bytes 393248 | tf_op jit(solution)/shard_map/ppermute | solution.py:295
  37.9 1.5 %other_images.7 = (f32[512,128]{1,0:T(8,128)S(1)}, f32[512,128]{1,0:T(8,128)S(1)}) custom-call(s32[2]{0:T(128)S(1)} %get-tuple-element.83.count_ref, s32[2,128]{1,0:T(2,128)S(1)} %broadcast_add_fusion.list_ref, f32[2,4,6]{2,1,0:T(4,128)S(1)} %copy-done, f32[16]{0:T(128)S(1)} %copy-done.1, f32[96,8,128]{2,1,0:T(8,128)S(1)} %collective-permute-done.6.strain_ref, ...), custom_call_target="tpu_custom_call" | custom-call | flops 1024 | bytes 1024 | tf_op jit(solution)/shard_map/other_images/pallas_call | solution.py:204
  39.4 1.1 %collective-permute-start.9 = (f32[512,128]{1,0:T(8,128)S(1)}, f32[512,128]{1,0:T(8,128)S(1)}, u32[]{:S(2)}, u32[]{:S(2)}) collective-permute-start(f32[512,128]{1,0:T(8,128)S(1)} %get-tuple-element.66), channel_id=1, source_target_pairs={{0,4},{1,9},{2,6},{3,11},{4,0},{5,13},{6,2},{7,15},{8,12},{9,1},{1... | collective-permute-start | bytes 786440 | tf_op jit(solution)/shard_map/ppermute | solution.py:295
  40.6 0.9 %add_add_fusion.3 = f32[256,128]{1,0:T(8,128)S(1)} fusion(f32[256,128]{1,0:T(8,128)S(1)} %collective-permute-done.5, f32[512,128]{1,0:T(8,128)} %collective-permute-done.2, f32[512,128]{1,0:T(8,128)S(1)} %get-tuple-element.49), kind=kLoop, calls=%fused_computation.11 | loop fusion | flops 65536 | bytes 524288 | tf_op jit(solution)/shard_map/add | solution.py:396
  41.5 1.6 %collective-permute-start.10 = (f32[256,128]{1,0:T(8,128)S(1)}, f32[256,128]{1,0:T(8,128)S(1)}, u32[]{:S(2)}, u32[]{:S(2)}) collective-permute-start(f32[256,128]{1,0:T(8,128)S(1)} %add_add_fusion.3), channel_id=1, source_target_pairs={{0,2},{1,3},{2,0},{3,1},{4,6},{5,7},{6,4},{7,5},{8,10},{9,11},{10,... | collective-permute-start | bytes 393224 | tf_op jit(solution)/shard_map/ppermute | solution.py:297
  43.1 2.5 %collective-permute-start.8 = (f32[256,128]{1,0:T(8,128)S(1)}, f32[256,128]{1,0:T(8,128)S(1)}, u32[]{:S(2)}, u32[]{:S(2)}) collective-permute-start(f32[256,128]{1,0:T(8,128)S(1)} %slice_add_fusion.1), channel_id=1, source_target_pairs={{0,16},{4,20},{8,24},{12,28},{16,0},{20,4},{24,8},{28,12},{1,17},{... | collective-permute-start | bytes 393224 | tf_op jit(solution)/shard_map/ppermute | solution.py:297
  45.6 0.6 collective-permute-start.13
  46.6 3.6 %collective-permute-start.12 = (f32[256,128]{1,0:T(8,128)S(1)}, f32[256,128]{1,0:T(8,128)S(1)}, u32[]{:S(2)}, u32[]{:S(2)}) collective-permute-start(f32[256,128]{1,0:T(8,128)S(1)} %slice_add_fusion), channel_id=1, source_target_pairs={{0,16},{4,20},{8,24},{12,28},{16,0},{20,4},{24,8},{28,12},{1,17},{... | collective-permute-start | bytes 393224 | tf_op jit(solution)/shard_map/ppermute | solution.py:297
  50.2 2.1 %collective-permute-start.14 = (f32[256,128]{1,0:T(8,128)S(1)}, f32[256,128]{1,0:T(8,128)S(1)}, u32[]{:S(2)}, u32[]{:S(2)}) collective-permute-start(f32[256,128]{1,0:T(8,128)S(1)} %add_add_fusion.2), channel_id=1, source_target_pairs={{0,2},{1,3},{2,0},{3,1},{4,6},{5,7},{6,4},{7,5},{8,10},{9,11},{10,... | collective-permute-start | bytes 393224 | tf_op jit(solution)/shard_map/ppermute | solution.py:297
  52.3 0.8 %collective-permute-done.12 = f32[256,128]{1,0:T(8,128)S(1)} collective-permute-done((f32[256,128]{1,0:T(8,128)S(1)}, f32[256,128]{1,0:T(8,128)S(1)}, u32[]{:S(2)}, u32[]{:S(2)}) %collective-permute-start.12) | collective-permute-done | bytes 131104 | tf_op jit(solution)/shard_map/ppermute | solution.py:297
  53.1 1.6 %collective-permute-start.15 = (f32[256,128]{1,0:T(8,128)S(1)}, f32[256,128]{1,0:T(8,128)S(1)}, u32[]{:S(2)}, u32[]{:S(2)}) collective-permute-start(f32[256,128]{1,0:T(8,128)S(1)} %add_add_fusion), channel_id=1, source_target_pairs={{0,2},{1,3},{2,0},{3,1},{4,6},{5,7},{6,4},{7,5},{8,10},{9,11},{10,... | collective-permute-start | bytes 393224 | tf_op jit(solution)/shard_map/ppermute | solution.py:297
  55.3 2.9 %collective-permute-done.15 = f32[256,128]{1,0:T(8,128)S(1)} collective-permute-done((f32[256,128]{1,0:T(8,128)S(1)}, f32[256,128]{1,0:T(8,128)S(1)}, u32[]{:S(2)}, u32[]{:S(2)}) %collective-permute-start.15) | collective-permute-done | bytes 131104 | tf_op jit(solution)/shard_map/ppermute | solution.py:297
  58.3 0.7 %resolve.2.refs_12_ = f32[256,512]{1,0:T(8,128)S(1)} custom-call(bf16[128,512]{1,0:T(8,128)(2,1)S(1)} %get-tuple-element.97.refs_0_, bf16[128,512]{1,0:T(8,128)(2,1)S(1)} %get-tuple-element.96.refs_1_, bf16[128,512]{1,0:T(8,128)(2,1)S(1)} %get-tuple-element.95.refs_2_, bf16[128,512]{1,0:T(8,128)(2,1)S(1)} %get-tuple-element.94.refs_3_, ...), custom_call_target="tpu_custom_call" | custom-call | flops 1024 | bytes 1024 | tf_op jit(solution)/shard_map/resolve/pallas_call | solution.py:238
  59.0 0.8 %collective-permute-done.17.refs_11_ = f32[512,128]{1,0:T(8,128)S(1)} collective-permute-done((f32[512,128]{1,0:T(8,128)S(1)}, f32[512,128]{1,0:T(8,128)S(1)}, u32[]{:S(2)}, u32[]{:S(2)}) %collective-permute-start.17) | collective-permute-done | bytes 262176 | tf_op jit(solution)/shard_map/ppermute | solution.py:297
  59.8 1.5 %resolve.3 = f32[256,512]{1,0:T(8,128)} custom-call(bf16[128,512]{1,0:T(8,128)(2,1)S(1)} %get-tuple-element.106.refs_0_, bf16[128,512]{1,0:T(8,128)(2,1)S(1)} %get-tuple-element.105.refs_1_, bf16[128,512]{1,0:T(8,128)(2,1)S(1)} %get-tuple-element.104.refs_2_, bf16[128,512]{1,0:T(8,128)(2,1)S(1)} %get-tuple-element.103.refs_3_, ...), custom_call_target="tpu_custom_call" | custom-call | flops 1024 | bytes 1024 | tf_op jit(solution)/shard_map/resolve/pallas_call | solution.py:238
  (56 shorter events, 2.9 us)
Async XLA Ops:
  0.0 5.0 %copy-start.3 = (f32[128,6,512]{2,0,1:T(8,128)S(1)}, f32[128,6,512]{2,0,1:T(8,128)}, u32[]{:S(2)}) copy-start(f32[128,6,512]{2,0,1:T(8,128)} %param.6) | copy-start | bytes 4718596
  0.0 5.6 %copy-start.1 = (f32[16]{0:T(128)S(1)}, f32[16]{0:T(128)}, u32[]{:S(2)}) copy-start(f32[16]{0:T(128)} %rock_ref.7) | copy-start | bytes 196
  0.0 5.6 %copy-start = (f32[2,4,6]{2,1,0:T(4,128)S(1)}, f32[2,4,6]{2,1,0:T(4,128)}, u32[]{:S(2)}) copy-start(f32[2,4,6]{2,1,0:T(4,128)} %dirs_ref.7) | copy-start | bytes 580
  1.9 8.9 %collective-permute-start = (f32[97,8,128]{2,1,0:T(8,128)S(1)}, f32[97,8,128]{2,1,0:T(8,128)S(1)}, u32[]{:S(2)}, u32[]{:S(2)}) collective-permute-start(f32[97,8,128]{2,1,0:T(8,128)S(1)} %pad_maximum_fusion.refs_4_), channel_id=1, source_target_pairs={{0,8},{1,5},{2,10},{3,7},{4,12},{5,1},{6,14},{7,3},{8,0},{9,13},{1... | collective-permute-start | bytes 1191944 | tf_op jit(solution)/shard_map/ppermute | solution.py:295
  5.1 11.8 %collective-permute-start.3 = (f32[96,8,128]{2,1,0:T(8,128)S(1)}, f32[96,8,128]{2,1,0:T(8,128)S(1)}, u32[]{:S(2)}, u32[]{:S(2)}) collective-permute-start(f32[96,8,128]{2,1,0:T(8,128)S(1)} %get-tuple-element.108.refs_5_), channel_id=1, source_target_pairs={{0,8},{1,5},{2,10},{3,7},{4,12},{5,1},{6,14},{7,3},{8,0},{9,13},{1... | collective-permute-start | bytes 1179656 | tf_op jit(solution)/shard_map/ppermute | solution.py:295
  12.7 9.4 %collective-permute-start.2 = (f32[512,128]{1,0:T(8,128)S(1)}, f32[512,128]{1,0:T(8,128)}, u32[]{:S(2)}, u32[]{:S(2)}) collective-permute-start(f32[512,128]{1,0:T(8,128)S(1)} %get-tuple-element.50), channel_id=1, source_target_pairs={{0,4},{1,9},{2,6},{3,11},{4,0},{5,13},{6,2},{7,15},{8,12},{9,1},{1... | collective-permute-start | bytes 786440 | tf_op jit(solution)/shard_map/ppermute | solution.py:295
  14.8 12.0 %collective-permute-start.1 = (f32[96,8,128]{2,1,0:T(8,128)S(1)}, f32[96,8,128]{2,1,0:T(8,128)S(1)}, u32[]{:S(2)}, u32[]{:S(2)}) collective-permute-start(f32[96,8,128]{2,1,0:T(8,128)S(1)} %get-tuple-element.54.refs_4_), channel_id=1, source_target_pairs={{0,8},{1,5},{2,10},{3,7},{4,12},{5,1},{6,14},{7,3},{8,0},{9,13},{1... | collective-permute-start | bytes 1179656 | tf_op jit(solution)/shard_map/ppermute | solution.py:295
  16.8 21.0 %collective-permute-start.6 = (f32[96,8,128]{2,1,0:T(8,128)S(1)}, f32[96,8,128]{2,1,0:T(8,128)S(1)}, u32[]{:S(2)}, u32[]{:S(2)}) collective-permute-start(f32[96,8,128]{2,1,0:T(8,128)S(1)} %get-tuple-element.109.refs_5_), channel_id=1, source_target_pairs={{0,8},{1,5},{2,10},{3,7},{4,12},{5,1},{6,14},{7,3},{8,0},{9,13},{1... | collective-permute-start | bytes 1179656 | tf_op jit(solution)/shard_map/ppermute | solution.py:295
  16.9 12.5 %copy-start.2 = (bf16[2048,512]{1,0:T(8,128)(2,1)S(1)}, bf16[2048,512]{1,0:T(8,128)(2,1)}, u32[]{:S(2)}) copy-start(bf16[2048,512]{1,0:T(8,128)(2,1)} %param.11) | copy-start | bytes 6291460
  18.4 11.2 %collective-permute-start.7 = (f32[512,128]{1,0:T(8,128)S(1)}, f32[512,128]{1,0:T(8,128)S(1)}, u32[]{:S(2)}, u32[]{:S(2)}) collective-permute-start(f32[512,128]{1,0:T(8,128)S(1)} %get-tuple-element.53), channel_id=1, source_target_pairs={{0,4},{1,9},{2,6},{3,11},{4,0},{5,13},{6,2},{7,15},{8,12},{9,1},{1... | collective-permute-start | bytes 786440 | tf_op jit(solution)/shard_map/ppermute | solution.py:295
  23.0 17.5 %collective-permute-start.5 = (f32[256,128]{1,0:T(8,128)S(1)}, f32[256,128]{1,0:T(8,128)S(1)}, u32[]{:S(2)}, u32[]{:S(2)}) collective-permute-start(f32[256,128]{1,0:T(8,128)S(1)} %slice_add_fusion.3), channel_id=1, source_target_pairs={{0,16},{4,20},{8,24},{12,28},{16,0},{20,4},{24,8},{28,12},{1,17},{... | collective-permute-start | bytes 393224 | tf_op jit(solution)/shard_map/ppermute | solution.py:297
  28.4 14.7 %collective-permute-start.4 = (f32[512,128]{1,0:T(8,128)S(1)}, f32[512,128]{1,0:T(8,128)S(1)}, u32[]{:S(2)}, u32[]{:S(2)}) collective-permute-start(f32[512,128]{1,0:T(8,128)S(1)} %get-tuple-element.58), channel_id=1, source_target_pairs={{0,4},{1,9},{2,6},{3,11},{4,0},{5,13},{6,2},{7,15},{8,12},{9,1},{1... | collective-permute-start | bytes 786440 | tf_op jit(solution)/shard_map/ppermute | solution.py:295
  29.6 15.9 %collective-permute-start.11 = (f32[256,128]{1,0:T(8,128)S(1)}, f32[256,128]{1,0:T(8,128)S(1)}, u32[]{:S(2)}, u32[]{:S(2)}) collective-permute-start(f32[256,128]{1,0:T(8,128)S(1)} %slice_add_fusion.2), channel_id=1, source_target_pairs={{0,16},{4,20},{8,24},{12,28},{16,0},{20,4},{24,8},{28,12},{1,17},{... | collective-permute-start | bytes 393224 | tf_op jit(solution)/shard_map/ppermute | solution.py:297
  39.4 7.1 %collective-permute-start.9 = (f32[512,128]{1,0:T(8,128)S(1)}, f32[512,128]{1,0:T(8,128)S(1)}, u32[]{:S(2)}, u32[]{:S(2)}) collective-permute-start(f32[512,128]{1,0:T(8,128)S(1)} %get-tuple-element.66), channel_id=1, source_target_pairs={{0,4},{1,9},{2,6},{3,11},{4,0},{5,13},{6,2},{7,15},{8,12},{9,1},{1... | collective-permute-start | bytes 786440 | tf_op jit(solution)/shard_map/ppermute | solution.py:295
  41.5 5.0 %collective-permute-start.10 = (f32[256,128]{1,0:T(8,128)S(1)}, f32[256,128]{1,0:T(8,128)S(1)}, u32[]{:S(2)}, u32[]{:S(2)}) collective-permute-start(f32[256,128]{1,0:T(8,128)S(1)} %add_add_fusion.3), channel_id=1, source_target_pairs={{0,2},{1,3},{2,0},{3,1},{4,6},{5,7},{6,4},{7,5},{8,10},{9,11},{10,... | collective-permute-start | bytes 393224 | tf_op jit(solution)/shard_map/ppermute | solution.py:297
  43.1 7.1 %collective-permute-start.8 = (f32[256,128]{1,0:T(8,128)S(1)}, f32[256,128]{1,0:T(8,128)S(1)}, u32[]{:S(2)}, u32[]{:S(2)}) collective-permute-start(f32[256,128]{1,0:T(8,128)S(1)} %slice_add_fusion.1), channel_id=1, source_target_pairs={{0,16},{4,20},{8,24},{12,28},{16,0},{20,4},{24,8},{28,12},{1,17},{... | collective-permute-start | bytes 393224 | tf_op jit(solution)/shard_map/ppermute | solution.py:297
  45.6 6.7 %collective-permute-start.13 = (f32[256,128]{1,0:T(8,128)S(1)}, f32[256,128]{1,0:T(8,128)S(1)}, u32[]{:S(2)}, u32[]{:S(2)}) collective-permute-start(f32[256,128]{1,0:T(8,128)S(1)} %add_add_fusion.1), channel_id=1, source_target_pairs={{0,2},{1,3},{2,0},{3,1},{4,6},{5,7},{6,4},{7,5},{8,10},{9,11},{10,... | collective-permute-start | bytes 393224 | tf_op jit(solution)/shard_map/ppermute | solution.py:297
  46.6 6.6 %collective-permute-start.12 = (f32[256,128]{1,0:T(8,128)S(1)}, f32[256,128]{1,0:T(8,128)S(1)}, u32[]{:S(2)}, u32[]{:S(2)}) collective-permute-start(f32[256,128]{1,0:T(8,128)S(1)} %slice_add_fusion), channel_id=1, source_target_pairs={{0,16},{4,20},{8,24},{12,28},{16,0},{20,4},{24,8},{28,12},{1,17},{... | collective-permute-start | bytes 393224 | tf_op jit(solution)/shard_map/ppermute | solution.py:297
  50.2 5.1 %collective-permute-start.14 = (f32[256,128]{1,0:T(8,128)S(1)}, f32[256,128]{1,0:T(8,128)S(1)}, u32[]{:S(2)}, u32[]{:S(2)}) collective-permute-start(f32[256,128]{1,0:T(8,128)S(1)} %add_add_fusion.2), channel_id=1, source_target_pairs={{0,2},{1,3},{2,0},{3,1},{4,6},{5,7},{6,4},{7,5},{8,10},{9,11},{10,... | collective-permute-start | bytes 393224 | tf_op jit(solution)/shard_map/ppermute | solution.py:297
  53.1 5.0 %collective-permute-start.15 = (f32[256,128]{1,0:T(8,128)S(1)}, f32[256,128]{1,0:T(8,128)S(1)}, u32[]{:S(2)}, u32[]{:S(2)}) collective-permute-start(f32[256,128]{1,0:T(8,128)S(1)} %add_add_fusion), channel_id=1, source_target_pairs={{0,2},{1,3},{2,0},{3,1},{4,6},{5,7},{6,4},{7,5},{8,10},{9,11},{10,... | collective-permute-start | bytes 393224 | tf_op jit(solution)/shard_map/ppermute | solution.py:297
  54.7 3.6 %collective-permute-start.18 = (f32[512,128]{1,0:T(8,128)S(1)}, f32[512,128]{1,0:T(8,128)S(1)}, u32[]{:S(2)}, u32[]{:S(2)}) collective-permute-start(f32[512,128]{1,0:T(8,128)S(1)} %pad_maximum_fusion.2.refs_8_), channel_id=1, source_target_pairs={{0,1},{1,0},{2,3},{3,2},{4,5},{5,4},{6,7},{7,6},{8,9},{9,8},{10,11... | collective-permute-start | bytes 786440 | tf_op jit(solution)/shard_map/ppermute | solution.py:297
  54.7 3.6 %collective-permute-start.19 = (f32[512,128]{1,0:T(8,128)S(1)}, f32[512,128]{1,0:T(8,128)S(1)}, u32[]{:S(2)}, u32[]{:S(2)}) collective-permute-start(f32[512,128]{1,0:T(8,128)S(1)} %pad_maximum_fusion.1.refs_10_), channel_id=1, source_target_pairs={{0,1},{1,0},{2,3},{3,2},{4,5},{5,4},{6,7},{7,6},{8,9},{9,8},{10,11... | collective-permute-start | bytes 786440 | tf_op jit(solution)/shard_map/ppermute | solution.py:297
  55.2 3.8 %collective-permute-start.16 = (f32[512,128]{1,0:T(8,128)S(1)}, f32[512,128]{1,0:T(8,128)S(1)}, u32[]{:S(2)}, u32[]{:S(2)}) collective-permute-start(f32[512,128]{1,0:T(8,128)S(1)} %pad_maximum_fusion.3.refs_8_), channel_id=1, source_target_pairs={{0,1},{1,0},{2,3},{3,2},{4,5},{5,4},{6,7},{7,6},{8,9},{9,8},{10,11... | collective-permute-start | bytes 786440 | tf_op jit(solution)/shard_map/ppermute | solution.py:297
  58.2 1.6 %collective-permute-start.17 = (f32[512,128]{1,0:T(8,128)S(1)}, f32[512,128]{1,0:T(8,128)S(1)}, u32[]{:S(2)}, u32[]{:S(2)}) collective-permute-start(f32[512,128]{1,0:T(8,128)S(1)} %pad_maximum_fusion.4.refs_10_), channel_id=1, source_target_pairs={{0,1},{1,0},{2,3},{3,2},{4,5},{5,4},{6,7},{7,6},{8,9},{9,8},{10,11... | collective-permute-start | bytes 786440 | tf_op jit(solution)/shard_map/ppermute | solution.py:297

commit v5 on v4

--- a/solution.py
+++ b/solution.py
@@ -17,8 +17,10 @@
 COST = 1024
 SCHEDULE = (
     ("begin", 0, 1),
+    ("launch", 2),
     ("first", 0),
     ("first", 1),
+    ("launch", 3),
     ("begin", 2, 3),
     ("middle", 0),
     ("first", 2),
@@ -26,8 +28,8 @@
     ("rows", 2, 3),
     ("middle", 1),
     ("first", 3),
+    ("middle", 2),
     ("final", 0),
-    ("middle", 2),
     ("final", 1),
     ("arrive", 0),
     ("middle", 3),
@@ -42,7 +44,7 @@
     ("far", 2, 3),
     ("multiply", 2, 3),
 )
-SCHEDULED = (1, 1, 1, 1)
+SCHEDULED = (1, 1, 1, 0)
 SCALE = math.sqrt(0.5 / math.log(2.0))
 
 
@@ -298,7 +300,7 @@
 
     same = [(k, k) for k in range(bits)]
     plans = [(same[0], tuple(same[1:])), ((1, 0), ((0, 1),) + tuple(same[2:]))]
-    plan_of = [1] * chunks
+    plan_of = [1] * (chunks - 1) + [0]
     every = list(range(chunks))
     launches = every
     last = []
@@ -317,19 +319,23 @@
     padded = padded.reshape(-1, GROUP, LANES)
     own = {}
     other = {}
-    told = []
-    source = by_comp
-    for c in launches:
+
+    def piece(source, c):
         block = source[:, :, c * LANES : (c + 1) * LANES]
-        if plan_of[c] not in told:
-            told.append(plan_of[c])
-            block = jnp.concatenate([block, padded], axis=0)
-        own[c] = block
-        other[c] = swap(block, plans[plan_of[c]][0])
-        if c == launches[0]:
-            mark(block)
-            source = tie(by_comp)
-    mark(own[launches[-1]])
+        if plan_of[c] in plan_of[:c]:
+            return block
+        return jnp.concatenate([block, padded], axis=0)
+
+    def launch(c):
+        own[c] = mark(tie(pieces[c]) if last else pieces[c])
+        other[c] = swap(own[c], plans[plan_of[c]][0])
+
+    pieces = {0: piece(by_comp, 0)}
+    launch(0)
+    source = tie(by_comp)
+    pieces.update({c: piece(source, c) for c in every[1:]})
+    if chunks > 1:
+        launch(1)
     used = sorted(set(plan_of))
 
     def numbers(k):
@@ -430,10 +436,12 @@
     if plan_of == list(SCHEDULED):
         steps = SCHEDULE
     else:
-        steps = [("begin", *every)] + [(name, c) for name in ("first", "middle", "final") for c in every]
+        steps = [("launch", c) for c in every[2:]] + [("begin", *every)] + [(name, c) for name in ("first", "middle", "final") for c in every]
         steps += [("rows", *every), ("near", *every), ("far", *every), ("multiply", *every)]
     doing = dict(begin=begin, first=first, middle=middle, final=final, arrive=arrive, near=near, far=far, rows=rows)
     doing["multiply"] = multiply
+    doing["launch"] = launch
+    doing["wait"] = lambda c: other.update({c: mark(tie(other[c]))})
     for name, *group in steps:
         doing[name](*group)
     return result[-1].reshape(angles, ROWS, rocks, pix)

time: 62.1 us -> 60.1 us (0.968)
  waiting for transfers between devices: 15.4 us -> 13 us
  Pallas kernels: 13.4 us -> 14.6 us
  starting transfers between devices: 27.3 us -> 26.5 us
  local copies, waits for them, and re-layouts: 1.29 us -> 2.02 us
    ppermute x8 -> x6, waiting for transfers between devices: 10.6 us -> 0.02 us  [swap(): return lax.ppermute(value, ('slab', 'rock'), pairs)]
    ppermute x12 -> x14, waiting for transfers between devices: 4.81 us -> 13 us  [swap(): lax.ppermute(value, axis, [(i, i ^ 1 << number) for i in range(lax.axis_s...]
    ppermute x8 -> x6, starting transfers between devices: 10.2 us -> 8.89 us  [swap(): return lax.ppermute(value, ('slab', 'rock'), pairs)]
    concatenate x1 -> x2, other arithmetic: 0.03 us -> 1.05 us  [piece(): return jnp.concatenate([block, padded], axis=0)]
    add x4, other arithmetic: 1 us -> 0.09 us  [final(): image[c] = mark(held[c] + tie(flying[c]))]
    pallas_call x4, Pallas kernels: 6.08 us -> 6.99 us  [other_images(): pl.pallas_call(kernel, out_shape=[jax.ShapeDtypeStruct((half, LANES), jnp...]
    add x4, other arithmetic: 0.97 us -> 0.06 us  [middle(): sent = mark(held[c][:rows] + arrived[:rows])]
    slice x2, local copies, waits for them, and re-layouts: 1.1 us -> 1.84 us  [piece(): block = source[:, :, c * LANES:(c + 1) * LANES]]
  transfers between devices with their start and end apart: 20 -> 20, of which waited for: 8 -> 6; matrix products, arithmetic and copies ran while one was open for 5% -> 6% of each run, Pallas kernels for 19% -> 22%
where the time goes in v5:
time: 60.1 us; the launch traced here: 59.9 us
  starting transfers between devices  26.5 us (44%)
  Pallas kernels  14.6 us (24%)
  waiting for transfers between devices  13 us (22%)
  other arithmetic  3.39 us (6%)
  local copies, waits for them, and re-layouts  2.02 us (3%)
    ppermute x14, starting transfers between devices, swap(): lax.ppermute(value, axis, [(i, i ^ 1 << number) for i in range(lax.axis_s...  17.6 us
    ppermute x14, waiting for transfers between devices, swap(): lax.ppermute(value, axis, [(i, i ^ 1 << number) for i in range(lax.axis_s...  13 us
    ppermute x6, starting transfers between devices, swap(): return lax.ppermute(value, ('slab', 'rock'), pairs)  8.89 us
    pallas_call x4, Pallas kernels, other_images(): pl.pallas_call(kernel, out_shape=[jax.ShapeDtypeStruct((half, LANES), jnp...  6.99 us
    pallas_call x2, Pallas kernels, own_images(): pl.pallas_call(kernel, out_shape=[jax.ShapeDtypeStruct((rows, LANES), jnp...  5.35 us
    pallas_call x2, Pallas kernels, resolve(): pl.pallas_call(kernel, out_shape=jax.ShapeDtypeStruct((unit, cols), jnp.f...  2.23 us
    slice x2, local copies, waits for them, and re-layouts, piece(): block = source[:, :, c * LANES:(c + 1) * LANES]  1.84 us
  transfers between devices with their start and end apart: 20, of which 6 were waited for; matrix products, arithmetic and copies ran while one was open for 6% of the time, Pallas kernels for 22%

profile of v5, /device:TPU:0, one launch (start us, length us, event | category | flops | bytes accessed | tf_op | source)
XLA Modules:
  0.0 59.9 jit_solution(15320343877966583745)
XLA Ops:
  0.0 0.8 %fusion.14 = (f32[2,128]{1,0:T(2,128)S(1)}, s32[2,128]{1,0:T(2,128)S(1)}) fusion(s32[2,128]{1,0:T(2,128)} %param.8, s32[2,128,1]{1,0,2:T(2,128)} %bitcast.54), kind=kLoop, calls=%fused_computation.109 | loop fusion | flops 768 | bytes 4096 | tf_op jit(solution)/shard_map/convert_element_type | solution.py:317
  0.8 1.0 %slice.94 = f32[96,8,128]{2,1,0:T(8,128)S(1)} slice(f32[96,8,512]{2,1,0:T(8,128)} %bitcast.52), slice={[0:96], [0:8], [0:128]} | slice | bytes 786432 | tf_op jit(solution)/shard_map/slice | solution.py:324
  1.9 3.1 %collective-permute-start = (f32[97,8,128]{2,1,0:T(8,128)S(1)}, f32[97,8,128]{2,1,0:T(8,128)S(1)}, u32[]{:S(2)}, u32[]{:S(2)}) collective-permute-start(f32[97,8,128]{2,1,0:T(8,128)S(1)} %pad_maximum_fusion.1.refs_4_), channel_id=1, source_target_pairs={{0,8},{1,5},{2,10},{3,7},{4,12},{5,1},{6,14},{7,3},{8,0},{9,13},{1... | collective-permute-start | bytes 1191944 | tf_op jit(solution)/shard_map/ppermute | solution.py:297
  5.0 0.8 %fusion.15 = (f32[96,8,128]{2,1,0:T(8,128)}, f32[96,8,128]{2,1,0:T(8,128)S(1)}, f32[96,8,128]{2,1,0:T(8,128)S(1)}) fusion(f32[96,8,512]{2,1,0:T(8,128)S(1)} %bitcast.53), kind=kLoop, calls=%fused_computation.110 | loop fusion | bytes 2359296 | tf_op jit(solution)/shard_map/slice | solution.py:324
  6.3 2.7 %own_images.2 = (f32[1040,128]{1,0:T(8,128)S(1)}, f32[1040,128]{1,0:T(8,128)S(1)}) custom-call(s32[2]{0:T(128)S(1)} %get-tuple-element.127.refs_0_.refs_2_, s32[2,128]{1,0:T(2,128)S(1)} %broadcast_add_fusion.3.refs_1_.refs_3_, f32[2,4,6]{2,1,0:T(4,128)S(1)} %copy-done, f32[16]{0:T(128)S(1)} %copy-done.1, f32[97,8,128]{2,1,0:T(8,128)S(1)} %pad_maximum_fusion.1.refs_4_, ...), custom_call_target="tpu_custom_call" | custom-call | flops 1024 | bytes 1024 | tf_op jit(solution)/shard_map/own_images/pallas_call | solution.py:179
  9.1 2.4 %collective-permute-start.1 = (f32[96,8,128]{2,1,0:T(8,128)S(1)}, f32[96,8,128]{2,1,0:T(8,128)S(1)}, u32[]{:S(2)}, u32[]{:S(2)}) collective-permute-start(f32[96,8,128]{2,1,0:T(8,128)S(1)} %get-tuple-element.61.refs_6_), channel_id=1, source_target_pairs={{0,8},{1,5},{2,10},{3,7},{4,12},{5,1},{6,14},{7,3},{8,0},{9,13},{1... | collective-permute-start | bytes 1179656 | tf_op jit(solution)/shard_map/ppermute | solution.py:297
  11.5 1.0 %pad_maximum_fusion.refs_7_ = f32[97,8,128]{2,1,0:T(8,128)S(1)} fusion(f32[1,8,128]{2,1,0:T(8,128)S(1)} %pad_bitcast_fusion, f32[96,8,128]{2,1,0:T(8,128)} %get-tuple-element.123), kind=kLoop, calls=%fused_computation | loop fusion | flops 99328 | bytes 794624 | tf_op jit(solution)/shard_map/concatenate | solution.py:327
  12.9 1.8 %other_images.4 = (f32[512,128]{1,0:T(8,128)S(1)}, f32[512,128]{1,0:T(8,128)S(1)}) custom-call(s32[2]{0:T(128)S(1)} %get-tuple-element.101.count_ref, s32[2,128]{1,0:T(2,128)S(1)} %broadcast_add_fusion.2.list_ref, f32[2,4,6]{2,1,0:T(4,128)S(1)} %copy-done, f32[16]{0:T(128)S(1)} %copy-done.1, f32[97,8,128]{2,1,0:T(8,128)S(1)} %collective-permute-done.strain_ref, ...), custom_call_target="tpu_custom_call" | custom-call | flops 1024 | bytes 1024 | tf_op jit(solution)/shard_map/other_images/pallas_call | solution.py:206
  14.7 1.6 %collective-permute-start.2 = (f32[512,128]{1,0:T(8,128)S(1)}, f32[512,128]{1,0:T(8,128)S(1)}, u32[]{:S(2)}, u32[]{:S(2)}) collective-permute-start(f32[512,128]{1,0:T(8,128)S(1)} %get-tuple-element.56), channel_id=1, source_target_pairs={{0,4},{1,9},{2,6},{3,11},{4,0},{5,13},{6,2},{7,15},{8,12},{9,1},{1... | collective-permute-start | bytes 786440 | tf_op jit(solution)/shard_map/ppermute | solution.py:297
  16.4 1.8 %other_images.5 = (f32[512,128]{1,0:T(8,128)S(1)}, f32[512,128]{1,0:T(8,128)S(1)}) custom-call(s32[2]{0:T(128)S(1)} %get-tuple-element.101.count_ref, s32[2,128]{1,0:T(2,128)S(1)} %broadcast_add_fusion.2.list_ref, f32[2,4,6]{2,1,0:T(4,128)S(1)} %copy-done, f32[16]{0:T(128)S(1)} %copy-done.1, f32[96,8,128]{2,1,0:T(8,128)S(1)} %collective-permute-done.3.strain_ref, ...), custom_call_target="tpu_custom_call" | custom-call | flops 1024 | bytes 1024 | tf_op jit(solution)/shard_map/other_images/pallas_call | solution.py:206
  18.2 0.6 %collective-permute-start.6 = (f32[512,128]{1,0:T(8,128)S(1)}, f32[512,128]{1,0:T(8,128)S(1)}, u32[]{:S(2)}, u32[]{:S(2)}) collective-permute-start(f32[512,128]{1,0:T(8,128)S(1)} %get-tuple-element.59), channel_id=1, source_target_pairs={{0,4},{1,9},{2,6},{3,11},{4,0},{5,13},{6,2},{7,15},{8,12},{9,1},{1... | collective-permute-start | bytes 786440 | tf_op jit(solution)/shard_map/ppermute | solution.py:297
  18.8 1.5 %collective-permute-start.5 = (f32[97,8,128]{2,1,0:T(8,128)S(1)}, f32[97,8,128]{2,1,0:T(8,128)S(1)}, u32[]{:S(2)}, u32[]{:S(2)}) collective-permute-start(f32[97,8,128]{2,1,0:T(8,128)S(1)} %pad_maximum_fusion.refs_7_), channel_id=1, source_target_pairs={{0,4},{4,0},{8,12},{12,8},{16,20},{20,16},{24,28},{28,24},{1,5},{5... | collective-permute-start | bytes 1191944 | tf_op jit(solution)/shard_map/ppermute | solution.py:299
  20.4 2.6 %own_images.3 = (f32[1040,128]{1,0:T(8,128)S(1)}, f32[1040,128]{1,0:T(8,128)S(1)}) custom-call(s32[2]{0:T(128)S(1)} %get-tuple-element.97.refs_0_, s32[2,128]{1,0:T(2,128)S(1)} %broadcast_add_fusion.1.refs_1_, s32[2]{0:T(128)S(1)} %get-tuple-element.127.refs_0_.refs_2_, s32[2,128]{1,0:T(2,128)S(1)} %broadcast_add_fusion.3.refs_1_.refs_3_, ...), custom_call_target="tpu_custom_call" | custom-call | flops 1024 | bytes 1024 | tf_op jit(solution)/shard_map/own_images/pallas_call | solution.py:179
  23.0 2.6 %collective-permute-start.9 = (f32[256,128]{1,0:T(8,128)S(1)}, f32[256,128]{1,0:T(8,128)S(1)}, u32[]{:S(2)}, u32[]{:S(2)}) collective-permute-start(f32[256,128]{1,0:T(8,128)S(1)} %slice_add_fusion.3), channel_id=1, source_target_pairs={{0,16},{4,20},{8,24},{12,28},{16,0},{20,4},{24,8},{28,12},{1,17},{... | collective-permute-start | bytes 393224 | tf_op jit(solution)/shard_map/ppermute | solution.py:299
  25.6 1.8 %other_images.6 = (f32[512,128]{1,0:T(8,128)S(1)}, f32[512,128]{1,0:T(8,128)S(1)}) custom-call(s32[2]{0:T(128)S(1)} %get-tuple-element.101.count_ref, s32[2,128]{1,0:T(2,128)S(1)} %broadcast_add_fusion.2.list_ref, f32[2,4,6]{2,1,0:T(4,128)S(1)} %copy-done, f32[16]{0:T(128)S(1)} %copy-done.1, f32[96,8,128]{2,1,0:T(8,128)S(1)} %collective-permute-done.1.strain_ref, ...), custom_call_target="tpu_custom_call" | custom-call | flops 1024 | bytes 1024 | tf_op jit(solution)/shard_map/other_images/pallas_call | solution.py:206
  27.4 1.1 %collective-permute-start.4 = (f32[512,128]{1,0:T(8,128)S(1)}, f32[512,128]{1,0:T(8,128)S(1)}, u32[]{:S(2)}, u32[]{:S(2)}) collective-permute-start(f32[512,128]{1,0:T(8,128)S(1)} %get-tuple-element.65), channel_id=1, source_target_pairs={{0,4},{1,9},{2,6},{3,11},{4,0},{5,13},{6,2},{7,15},{8,12},{9,1},{1... | collective-permute-start | bytes 786440 | tf_op jit(solution)/shard_map/ppermute | solution.py:297
  28.8 1.9 %collective-permute-start.11 = (f32[256,128]{1,0:T(8,128)S(1)}, f32[256,128]{1,0:T(8,128)S(1)}, u32[]{:S(2)}, u32[]{:S(2)}) collective-permute-start(f32[256,128]{1,0:T(8,128)S(1)} %slice_add_fusion.2), channel_id=1, source_target_pairs={{0,16},{4,20},{8,24},{12,28},{16,0},{20,4},{24,8},{28,12},{1,17},{... | collective-permute-start | bytes 393224 | tf_op jit(solution)/shard_map/ppermute | solution.py:299
  30.6 1.9 %collective-permute-done.5.strain_ref = f32[97,8,128]{2,1,0:T(8,128)S(1)} collective-permute-done((f32[97,8,128]{2,1,0:T(8,128)S(1)}, f32[97,8,128]{2,1,0:T(8,128)S(1)}, u32[]{:S(2)}, u32[]{:S(2)}) %collective-permute-start.5) | collective-permute-done | bytes 397344 | tf_op jit(solution)/shard_map/ppermute | solution.py:299
  32.9 1.6 %other_images.7 = (f32[512,128]{1,0:T(8,128)S(1)}, f32[512,128]{1,0:T(8,128)S(1)}) custom-call(s32[2]{0:T(128)S(1)} %get-tuple-element.93.count_ref, s32[2,128]{1,0:T(2,128)S(1)} %broadcast_add_fusion.list_ref, f32[2,4,6]{2,1,0:T(4,128)S(1)} %copy-done, f32[16]{0:T(128)S(1)} %copy-done.1, f32[97,8,128]{2,1,0:T(8,128)S(1)} %collective-permute-done.5.strain_ref, ...), custom_call_target="tpu_custom_call" | custom-call | flops 1024 | bytes 1024 | tf_op jit(solution)/shard_map/other_images/pallas_call | solution.py:206
  34.5 1.8 %collective-permute-start.8 = (f32[512,128]{1,0:T(8,128)S(1)}, f32[512,128]{1,0:T(8,128)S(1)}, u32[]{:S(2)}, u32[]{:S(2)}) collective-permute-start(f32[512,128]{1,0:T(8,128)S(1)} %get-tuple-element.74), channel_id=1, source_target_pairs={{0,8},{4,12},{8,0},{12,4},{16,24},{20,28},{24,16},{28,20},{1,9},{5... | collective-permute-start | bytes 786440 | tf_op jit(solution)/shard_map/ppermute | solution.py:299
  36.3 2.6 %collective-permute-start.7 = (f32[256,128]{1,0:T(8,128)S(1)}, f32[256,128]{1,0:T(8,128)S(1)}, u32[]{:S(2)}, u32[]{:S(2)}) collective-permute-start(f32[256,128]{1,0:T(8,128)S(1)} %slice_add_fusion.1), channel_id=1, source_target_pairs={{0,16},{4,20},{8,24},{12,28},{16,0},{20,4},{24,8},{28,12},{1,17},{... | collective-permute-start | bytes 393224 | tf_op jit(solution)/shard_map/ppermute | solution.py:299
  39.0 1.6 %collective-permute-start.10 = (f32[256,128]{1,0:T(8,128)S(1)}, f32[256,128]{1,0:T(8,128)S(1)}, u32[]{:S(2)}, u32[]{:S(2)}) collective-permute-start(f32[256,128]{1,0:T(8,128)S(1)} %add_add_fusion.2), channel_id=1, source_target_pairs={{0,2},{1,3},{2,0},{3,1},{4,6},{5,7},{6,4},{7,5},{8,10},{9,11},{10,... | collective-permute-start | bytes 393224 | tf_op jit(solution)/shard_map/ppermute | solution.py:299
  40.6 0.6 %collective-permute-start.13 = (f32[256,128]{1,0:T(8,128)S(1)}, f32[256,128]{1,0:T(8,128)S(1)}, u32[]{:S(2)}, u32[]{:S(2)}) collective-permute-start(f32[256,128]{1,0:T(8,128)S(1)} %add_add_fusion.1), channel_id=1, source_target_pairs={{0,2},{1,3},{2,0},{3,1},{4,6},{5,7},{6,4},{7,5},{8,10},{9,11},{10,... | collective-permute-start | bytes 393224 | tf_op jit(solution)/shard_map/ppermute | solution.py:299
  41.2 2.8 %collective-permute-done.10 = f32[256,128]{1,0:T(8,128)S(1)} collective-permute-done((f32[256,128]{1,0:T(8,128)S(1)}, f32[256,128]{1,0:T(8,128)S(1)}, u32[]{:S(2)}, u32[]{:S(2)}) %collective-permute-start.10) | collective-permute-done | bytes 131104 | tf_op jit(solution)/shard_map/ppermute | solution.py:299
  44.3 1.3 %collective-permute-start.12 = (f32[256,128]{1,0:T(8,128)S(1)}, f32[256,128]{1,0:T(8,128)S(1)}, u32[]{:S(2)}, u32[]{:S(2)}) collective-permute-start(f32[256,128]{1,0:T(8,128)S(1)} %slice_add_fusion), channel_id=1, source_target_pairs={{0,16},{4,20},{8,24},{12,28},{16,0},{20,4},{24,8},{28,12},{1,17},{... | collective-permute-start | bytes 393224 | tf_op jit(solution)/shard_map/ppermute | solution.py:299
  45.7 1.6 %collective-permute-start.14 = (f32[256,128]{1,0:T(8,128)S(1)}, f32[256,128]{1,0:T(8,128)S(1)}, u32[]{:S(2)}, u32[]{:S(2)}) collective-permute-start(f32[256,128]{1,0:T(8,128)S(1)} %add_add_fusion.3), channel_id=1, source_target_pairs={{0,2},{1,3},{2,0},{3,1},{4,6},{5,7},{6,4},{7,5},{8,10},{9,11},{10,... | collective-permute-start | bytes 393224 | tf_op jit(solution)/shard_map/ppermute | solution.py:299
  47.3 4.4 %collective-permute-done.12 = f32[256,128]{1,0:T(8,128)S(1)} collective-permute-done((f32[256,128]{1,0:T(8,128)S(1)}, f32[256,128]{1,0:T(8,128)S(1)}, u32[]{:S(2)}, u32[]{:S(2)}) %collective-permute-start.12) | collective-permute-done | bytes 131104 | tf_op jit(solution)/shard_map/ppermute | solution.py:299
  51.7 1.6 %collective-permute-start.15 = (f32[256,128]{1,0:T(8,128)S(1)}, f32[256,128]{1,0:T(8,128)S(1)}, u32[]{:S(2)}, u32[]{:S(2)}) collective-permute-start(f32[256,128]{1,0:T(8,128)S(1)} %add_add_fusion), channel_id=1, source_target_pairs={{0,2},{1,3},{2,0},{3,1},{4,6},{5,7},{6,4},{7,5},{8,10},{9,11},{10,... | collective-permute-start | bytes 393224 | tf_op jit(solution)/shard_map/ppermute | solution.py:299
  53.9 2.8 %collective-permute-done.15 = f32[256,128]{1,0:T(8,128)S(1)} collective-permute-done((f32[256,128]{1,0:T(8,128)S(1)}, f32[256,128]{1,0:T(8,128)S(1)}, u32[]{:S(2)}, u32[]{:S(2)}) %collective-permute-start.15) | collective-permute-done | bytes 131104 | tf_op jit(solution)/shard_map/ppermute | solution.py:299
  56.9 0.7 %resolve.2.refs_12_ = f32[256,512]{1,0:T(8,128)S(1)} custom-call(bf16[128,512]{1,0:T(8,128)(2,1)S(1)} %get-tuple-element.113.refs_0_, bf16[128,512]{1,0:T(8,128)(2,1)S(1)} %get-tuple-element.112.refs_1_, bf16[128,512]{1,0:T(8,128)(2,1)S(1)} %get-tuple-element.111.refs_2_, bf16[128,512]{1,0:T(8,128)(2,1)S(1)} %get-tuple-element.110.refs_3_, ...), custom_call_target="tpu_custom_call" | custom-call | flops 1024 | bytes 1024 | tf_op jit(solution)/shard_map/resolve/pallas_call | solution.py:240
  57.6 0.8 %collective-permute-done.17.refs_11_ = f32[512,128]{1,0:T(8,128)S(1)} collective-permute-done((f32[512,128]{1,0:T(8,128)S(1)}, f32[512,128]{1,0:T(8,128)S(1)}, u32[]{:S(2)}, u32[]{:S(2)}) %collective-permute-start.17) | collective-permute-done | bytes 262176 | tf_op jit(solution)/shard_map/ppermute | solution.py:299
  58.4 1.5 %resolve.3 = f32[256,512]{1,0:T(8,128)} custom-call(bf16[128,512]{1,0:T(8,128)(2,1)S(1)} %get-tuple-element.122.refs_0_, bf16[128,512]{1,0:T(8,128)(2,1)S(1)} %get-tuple-element.121.refs_1_, bf16[128,512]{1,0:T(8,128)(2,1)S(1)} %get-tuple-element.120.refs_2_, bf16[128,512]{1,0:T(8,128)(2,1)S(1)} %get-tuple-element.119.refs_3_, ...), custom_call_target="tpu_custom_call" | custom-call | flops 1024 | bytes 1024 | tf_op jit(solution)/shard_map/resolve/pallas_call | solution.py:240
  (65 shorter events, 2.7 us)
Async XLA Ops:
  0.0 5.0 %copy-start.3 = (f32[128,6,512]{2,0,1:T(8,128)S(1)}, f32[128,6,512]{2,0,1:T(8,128)}, u32[]{:S(2)}) copy-start(f32[128,6,512]{2,0,1:T(8,128)} %param.6) | copy-start | bytes 4718596
  0.0 6.3 %copy-start.1 = (f32[16]{0:T(128)S(1)}, f32[16]{0:T(128)}, u32[]{:S(2)}) copy-start(f32[16]{0:T(128)} %rock_ref.7) | copy-start | bytes 196
  0.0 6.3 %copy-start = (f32[2,4,6]{2,1,0:T(4,128)S(1)}, f32[2,4,6]{2,1,0:T(4,128)}, u32[]{:S(2)}) copy-start(f32[2,4,6]{2,1,0:T(4,128)} %dirs_ref.7) | copy-start | bytes 580
  1.9 10.6 %collective-permute-start = (f32[97,8,128]{2,1,0:T(8,128)S(1)}, f32[97,8,128]{2,1,0:T(8,128)S(1)}, u32[]{:S(2)}, u32[]{:S(2)}) collective-permute-start(f32[97,8,128]{2,1,0:T(8,128)S(1)} %pad_maximum_fusion.1.refs_4_), channel_id=1, source_target_pairs={{0,8},{1,5},{2,10},{3,7},{4,12},{5,1},{6,14},{7,3},{8,0},{9,13},{1... | collective-permute-start | bytes 1191944 | tf_op jit(solution)/shard_map/ppermute | solution.py:297
  5.8 10.6 %collective-permute-start.3 = (f32[96,8,128]{2,1,0:T(8,128)S(1)}, f32[96,8,128]{2,1,0:T(8,128)S(1)}, u32[]{:S(2)}, u32[]{:S(2)}) collective-permute-start(f32[96,8,128]{2,1,0:T(8,128)S(1)} %get-tuple-element.48.refs_5_), channel_id=1, source_target_pairs={{0,8},{1,5},{2,10},{3,7},{4,12},{5,1},{6,14},{7,3},{8,0},{9,13},{1... | collective-permute-start | bytes 1179656 | tf_op jit(solution)/shard_map/ppermute | solution.py:297
  9.1 16.6 %collective-permute-start.1 = (f32[96,8,128]{2,1,0:T(8,128)S(1)}, f32[96,8,128]{2,1,0:T(8,128)S(1)}, u32[]{:S(2)}, u32[]{:S(2)}) collective-permute-start(f32[96,8,128]{2,1,0:T(8,128)S(1)} %get-tuple-element.61.refs_6_), channel_id=1, source_target_pairs={{0,8},{1,5},{2,10},{3,7},{4,12},{5,1},{6,14},{7,3},{8,0},{9,13},{1... | collective-permute-start | bytes 1179656 | tf_op jit(solution)/shard_map/ppermute | solution.py:297
  12.5 16.1 %copy-start.2 = (bf16[2048,512]{1,0:T(8,128)(2,1)S(1)}, bf16[2048,512]{1,0:T(8,128)(2,1)}, u32[]{:S(2)}) copy-start(bf16[2048,512]{1,0:T(8,128)(2,1)} %param.11) | copy-start | bytes 6291460
  14.7 8.3 %collective-permute-start.2 = (f32[512,128]{1,0:T(8,128)S(1)}, f32[512,128]{1,0:T(8,128)S(1)}, u32[]{:S(2)}, u32[]{:S(2)}) collective-permute-start(f32[512,128]{1,0:T(8,128)S(1)} %get-tuple-element.56), channel_id=1, source_target_pairs={{0,4},{1,9},{2,6},{3,11},{4,0},{5,13},{6,2},{7,15},{8,12},{9,1},{1... | collective-permute-start | bytes 786440 | tf_op jit(solution)/shard_map/ppermute | solution.py:297
  18.2 10.6 %collective-permute-start.6 = (f32[512,128]{1,0:T(8,128)S(1)}, f32[512,128]{1,0:T(8,128)S(1)}, u32[]{:S(2)}, u32[]{:S(2)}) collective-permute-start(f32[512,128]{1,0:T(8,128)S(1)} %get-tuple-element.59), channel_id=1, source_target_pairs={{0,4},{1,9},{2,6},{3,11},{4,0},{5,13},{6,2},{7,15},{8,12},{9,1},{1... | collective-permute-start | bytes 786440 | tf_op jit(solution)/shard_map/ppermute | solution.py:297
  18.8 13.7 %collective-permute-start.5 = (f32[97,8,128]{2,1,0:T(8,128)S(1)}, f32[97,8,128]{2,1,0:T(8,128)S(1)}, u32[]{:S(2)}, u32[]{:S(2)}) collective-permute-start(f32[97,8,128]{2,1,0:T(8,128)S(1)} %pad_maximum_fusion.refs_7_), channel_id=1, source_target_pairs={{0,4},{4,0},{8,12},{12,8},{16,20},{20,16},{24,28},{28,24},{1,5},{5... | collective-permute-start | bytes 1191944 | tf_op jit(solution)/shard_map/ppermute | solution.py:299
  23.0 15.9 %collective-permute-start.9 = (f32[256,128]{1,0:T(8,128)S(1)}, f32[256,128]{1,0:T(8,128)S(1)}, u32[]{:S(2)}, u32[]{:S(2)}) collective-permute-start(f32[256,128]{1,0:T(8,128)S(1)} %slice_add_fusion.3), channel_id=1, source_target_pairs={{0,16},{4,20},{8,24},{12,28},{16,0},{20,4},{24,8},{28,12},{1,17},{... | collective-permute-start | bytes 393224 | tf_op jit(solution)/shard_map/ppermute | solution.py:299
  27.4 8.9 %collective-permute-start.4 = (f32[512,128]{1,0:T(8,128)S(1)}, f32[512,128]{1,0:T(8,128)S(1)}, u32[]{:S(2)}, u32[]{:S(2)}) collective-permute-start(f32[512,128]{1,0:T(8,128)S(1)} %get-tuple-element.65), channel_id=1, source_target_pairs={{0,4},{1,9},{2,6},{3,11},{4,0},{5,13},{6,2},{7,15},{8,12},{9,1},{1... | collective-permute-start | bytes 786440 | tf_op jit(solution)/shard_map/ppermute | solution.py:297
  28.8 11.8 %collective-permute-start.11 = (f32[256,128]{1,0:T(8,128)S(1)}, f32[256,128]{1,0:T(8,128)S(1)}, u32[]{:S(2)}, u32[]{:S(2)}) collective-permute-start(f32[256,128]{1,0:T(8,128)S(1)} %slice_add_fusion.2), channel_id=1, source_target_pairs={{0,16},{4,20},{8,24},{12,28},{16,0},{20,4},{24,8},{28,12},{1,17},{... | collective-permute-start | bytes 393224 | tf_op jit(solution)/shard_map/ppermute | solution.py:299
  34.5 9.8 %collective-permute-start.8 = (f32[512,128]{1,0:T(8,128)S(1)}, f32[512,128]{1,0:T(8,128)S(1)}, u32[]{:S(2)}, u32[]{:S(2)}) collective-permute-start(f32[512,128]{1,0:T(8,128)S(1)} %get-tuple-element.74), channel_id=1, source_target_pairs={{0,8},{4,12},{8,0},{12,4},{16,24},{20,28},{24,16},{28,20},{1,9},{5... | collective-permute-start | bytes 786440 | tf_op jit(solution)/shard_map/ppermute | solution.py:299
  36.3 9.3 %collective-permute-start.7 = (f32[256,128]{1,0:T(8,128)S(1)}, f32[256,128]{1,0:T(8,128)S(1)}, u32[]{:S(2)}, u32[]{:S(2)}) collective-permute-start(f32[256,128]{1,0:T(8,128)S(1)} %slice_add_fusion.1), channel_id=1, source_target_pairs={{0,16},{4,20},{8,24},{12,28},{16,0},{20,4},{24,8},{28,12},{1,17},{... | collective-permute-start | bytes 393224 | tf_op jit(solution)/shard_map/ppermute | solution.py:299
  39.0 5.0 %collective-permute-start.10 = (f32[256,128]{1,0:T(8,128)S(1)}, f32[256,128]{1,0:T(8,128)S(1)}, u32[]{:S(2)}, u32[]{:S(2)}) collective-permute-start(f32[256,128]{1,0:T(8,128)S(1)} %add_add_fusion.2), channel_id=1, source_target_pairs={{0,2},{1,3},{2,0},{3,1},{4,6},{5,7},{6,4},{7,5},{8,10},{9,11},{10,... | collective-permute-start | bytes 393224 | tf_op jit(solution)/shard_map/ppermute | solution.py:299
  40.6 6.7 %collective-permute-start.13 = (f32[256,128]{1,0:T(8,128)S(1)}, f32[256,128]{1,0:T(8,128)S(1)}, u32[]{:S(2)}, u32[]{:S(2)}) collective-permute-start(f32[256,128]{1,0:T(8,128)S(1)} %add_add_fusion.1), channel_id=1, source_target_pairs={{0,2},{1,3},{2,0},{3,1},{4,6},{5,7},{6,4},{7,5},{8,10},{9,11},{10,... | collective-permute-start | bytes 393224 | tf_op jit(solution)/shard_map/ppermute | solution.py:299
  44.3 7.3 %collective-permute-start.12 = (f32[256,128]{1,0:T(8,128)S(1)}, f32[256,128]{1,0:T(8,128)S(1)}, u32[]{:S(2)}, u32[]{:S(2)}) collective-permute-start(f32[256,128]{1,0:T(8,128)S(1)} %slice_add_fusion), channel_id=1, source_target_pairs={{0,16},{4,20},{8,24},{12,28},{16,0},{20,4},{24,8},{28,12},{1,17},{... | collective-permute-start | bytes 393224 | tf_op jit(solution)/shard_map/ppermute | solution.py:299
  45.7 8.2 %collective-permute-start.14 = (f32[256,128]{1,0:T(8,128)S(1)}, f32[256,128]{1,0:T(8,128)S(1)}, u32[]{:S(2)}, u32[]{:S(2)}) collective-permute-start(f32[256,128]{1,0:T(8,128)S(1)} %add_add_fusion.3), channel_id=1, source_target_pairs={{0,2},{1,3},{2,0},{3,1},{4,6},{5,7},{6,4},{7,5},{8,10},{9,11},{10,... | collective-permute-start | bytes 393224 | tf_op jit(solution)/shard_map/ppermute | solution.py:299
  51.7 5.0 %collective-permute-start.15 = (f32[256,128]{1,0:T(8,128)S(1)}, f32[256,128]{1,0:T(8,128)S(1)}, u32[]{:S(2)}, u32[]{:S(2)}) collective-permute-start(f32[256,128]{1,0:T(8,128)S(1)} %add_add_fusion), channel_id=1, source_target_pairs={{0,2},{1,3},{2,0},{3,1},{4,6},{5,7},{6,4},{7,5},{8,10},{9,11},{10,... | collective-permute-start | bytes 393224 | tf_op jit(solution)/shard_map/ppermute | solution.py:299
  53.3 3.6 %collective-permute-start.18 = (f32[512,128]{1,0:T(8,128)S(1)}, f32[512,128]{1,0:T(8,128)S(1)}, u32[]{:S(2)}, u32[]{:S(2)}) collective-permute-start(f32[512,128]{1,0:T(8,128)S(1)} %pad_maximum_fusion.3.refs_8_), channel_id=1, source_target_pairs={{0,1},{1,0},{2,3},{3,2},{4,5},{5,4},{6,7},{7,6},{8,9},{9,8},{10,11... | collective-permute-start | bytes 786440 | tf_op jit(solution)/shard_map/ppermute | solution.py:299
  53.3 3.6 %collective-permute-start.19 = (f32[512,128]{1,0:T(8,128)S(1)}, f32[512,128]{1,0:T(8,128)S(1)}, u32[]{:S(2)}, u32[]{:S(2)}) collective-permute-start(f32[512,128]{1,0:T(8,128)S(1)} %pad_maximum_fusion.2.refs_10_), channel_id=1, source_target_pairs={{0,1},{1,0},{2,3},{3,2},{4,5},{5,4},{6,7},{7,6},{8,9},{9,8},{10,11... | collective-permute-start | bytes 786440 | tf_op jit(solution)/shard_map/ppermute | solution.py:299
  53.8 3.8 %collective-permute-start.16 = (f32[512,128]{1,0:T(8,128)S(1)}, f32[512,128]{1,0:T(8,128)S(1)}, u32[]{:S(2)}, u32[]{:S(2)}) collective-permute-start(f32[512,128]{1,0:T(8,128)S(1)} %pad_maximum_fusion.4.refs_8_), channel_id=1, source_target_pairs={{0,1},{1,0},{2,3},{3,2},{4,5},{5,4},{6,7},{7,6},{8,9},{9,8},{10,11... | collective-permute-start | bytes 786440 | tf_op jit(solution)/shard_map/ppermute | solution.py:299
  56.8 1.6 %collective-permute-start.17 = (f32[512,128]{1,0:T(8,128)S(1)}, f32[512,128]{1,0:T(8,128)S(1)}, u32[]{:S(2)}, u32[]{:S(2)}) collective-permute-start(f32[512,128]{1,0:T(8,128)S(1)} %pad_maximum_fusion.5.refs_10_), channel_id=1, source_target_pairs={{0,1},{1,0},{2,3},{3,2},{4,5},{5,4},{6,7},{7,6},{8,9},{9,8},{10,11... | collective-permute-start | bytes 786440 | tf_op jit(solution)/shard_map/ppermute | solution.py:299

commit v6 on v5

--- a/solution.py
+++ b/solution.py
@@ -28,16 +28,16 @@
     ("rows", 2, 3),
     ("middle", 1),
     ("first", 3),
+    ("final", 0),
     ("middle", 2),
-    ("final", 0),
     ("final", 1),
     ("arrive", 0),
     ("middle", 3),
     ("final", 2),
     ("arrive", 1),
+    ("final", 3),
     ("near", 0, 1),
     ("far", 0, 1),
-    ("final", 3),
     ("multiply", 0, 1),
     ("near", 2, 3),
     ("arrive", 2),

time: 60.1 us -> 59.7 us (level)
  waiting for transfers between devices: 13 us -> 11.3 us
  starting transfers between devices: 26.5 us -> 27.4 us
    ppermute x14, waiting for transfers between devices: 13 us -> 11.3 us  [swap(): lax.ppermute(value, axis, [(i, i ^ 1 << number) for i in range(lax.axis_s...]
    ppermute x14, starting transfers between devices: 17.6 us -> 18.4 us  [swap(): lax.ppermute(value, axis, [(i, i ^ 1 << number) for i in range(lax.axis_s...]
where the time goes in v6:
time: 59.7 us; the launch traced here: 59.3 us
  starting transfers between devices  27.4 us (46%)
  Pallas kernels  14.8 us (25%)
  waiting for transfers between devices  11.3 us (19%)
  other arithmetic  3.4 us (6%)
  local copies, waits for them, and re-layouts  2.02 us (3%)
    ppermute x14, starting transfers between devices, swap(): lax.ppermute(value, axis, [(i, i ^ 1 << number) for i in range(lax.axis_s...  18.4 us
    ppermute x14, waiting for transfers between devices, swap(): lax.ppermute(value, axis, [(i, i ^ 1 << number) for i in range(lax.axis_s...  11.3 us
    ppermute x6, starting transfers between devices, swap(): return lax.ppermute(value, ('slab', 'rock'), pairs)  9.03 us
    pallas_call x4, Pallas kernels, other_images(): pl.pallas_call(kernel, out_shape=[jax.ShapeDtypeStruct((half, LANES), jnp...  6.93 us
    pallas_call x2, Pallas kernels, own_images(): pl.pallas_call(kernel, out_shape=[jax.ShapeDtypeStruct((rows, LANES), jnp...  5.66 us
    pallas_call x2, Pallas kernels, resolve(): pl.pallas_call(kernel, out_shape=jax.ShapeDtypeStruct((unit, cols), jnp.f...  2.23 us
    slice x2, local copies, waits for them, and re-layouts, piece(): block = source[:, :, c * LANES:(c + 1) * LANES]  1.84 us
  transfers between devices with their start and end apart: 20, of which 6 were waited for; matrix products, arithmetic and copies ran while one was open for 6% of the time, Pallas kernels for 22%

profile of v6, /device:TPU:0, one launch (start us, length us, event | category | flops | bytes accessed | tf_op | source)
XLA Modules:
  0.0 59.3 jit_solution(9489042006035265967)
XLA Ops:
  0.0 0.8 %fusion.14 = (f32[2,128]{1,0:T(2,128)S(1)}, s32[2,128]{1,0:T(2,128)S(1)}) fusion(s32[2,128]{1,0:T(2,128)} %param.8, s32[2,128,1]{1,0,2:T(2,128)} %bitcast.54), kind=kLoop, calls=%fused_computation.109 | loop fusion | flops 768 | bytes 4096 | tf_op jit(solution)/shard_map/convert_element_type | solution.py:317
  0.8 1.0 %slice.94 = f32[96,8,128]{2,1,0:T(8,128)S(1)} slice(f32[96,8,512]{2,1,0:T(8,128)} %bitcast.52), slice={[0:96], [0:8], [0:128]} | slice | bytes 786432 | tf_op jit(solution)/shard_map/slice | solution.py:324
  1.9 3.1 %collective-permute-start = (f32[97,8,128]{2,1,0:T(8,128)S(1)}, f32[97,8,128]{2,1,0:T(8,128)S(1)}, u32[]{:S(2)}, u32[]{:S(2)}) collective-permute-start(f32[97,8,128]{2,1,0:T(8,128)S(1)} %pad_maximum_fusion.1.refs_4_), channel_id=1, source_target_pairs={{0,8},{1,5},{2,10},{3,7},{4,12},{5,1},{6,14},{7,3},{8,0},{9,13},{1... | collective-permute-start | bytes 1191944 | tf_op jit(solution)/shard_map/ppermute | solution.py:297
  5.0 0.8 %fusion.15 = (f32[96,8,128]{2,1,0:T(8,128)}, f32[96,8,128]{2,1,0:T(8,128)S(1)}, f32[96,8,128]{2,1,0:T(8,128)S(1)}) fusion(f32[96,8,512]{2,1,0:T(8,128)S(1)} %bitcast.53), kind=kLoop, calls=%fused_computation.110 | loop fusion | bytes 2359296 | tf_op jit(solution)/shard_map/slice | solution.py:324
  6.3 2.8 %own_images.2 = (f32[1040,128]{1,0:T(8,128)S(1)}, f32[1040,128]{1,0:T(8,128)S(1)}) custom-call(s32[2]{0:T(128)S(1)} %get-tuple-element.127.refs_0_.refs_2_, s32[2,128]{1,0:T(2,128)S(1)} %broadcast_add_fusion.3.refs_1_.refs_3_, f32[2,4,6]{2,1,0:T(4,128)S(1)} %copy-done, f32[16]{0:T(128)S(1)} %copy-done.1, f32[97,8,128]{2,1,0:T(8,128)S(1)} %pad_maximum_fusion.1.refs_4_, ...), custom_call_target="tpu_custom_call" | custom-call | flops 1024 | bytes 1024 | tf_op jit(solution)/shard_map/own_images/pallas_call | solution.py:179
  9.2 2.3 %collective-permute-start.1 = (f32[96,8,128]{2,1,0:T(8,128)S(1)}, f32[96,8,128]{2,1,0:T(8,128)S(1)}, u32[]{:S(2)}, u32[]{:S(2)}) collective-permute-start(f32[96,8,128]{2,1,0:T(8,128)S(1)} %get-tuple-element.61.refs_6_), channel_id=1, source_target_pairs={{0,8},{1,5},{2,10},{3,7},{4,12},{5,1},{6,14},{7,3},{8,0},{9,13},{1... | collective-permute-start | bytes 1179656 | tf_op jit(solution)/shard_map/ppermute | solution.py:297
  11.4 1.0 %pad_maximum_fusion.refs_7_ = f32[97,8,128]{2,1,0:T(8,128)S(1)} fusion(f32[1,8,128]{2,1,0:T(8,128)S(1)} %pad_bitcast_fusion, f32[96,8,128]{2,1,0:T(8,128)} %get-tuple-element.123), kind=kLoop, calls=%fused_computation | loop fusion | flops 99328 | bytes 794624 | tf_op jit(solution)/shard_map/concatenate | solution.py:327
  12.9 1.7 %other_images.4 = (f32[512,128]{1,0:T(8,128)S(1)}, f32[512,128]{1,0:T(8,128)S(1)}) custom-call(s32[2]{0:T(128)S(1)} %get-tuple-element.101.count_ref, s32[2,128]{1,0:T(2,128)S(1)} %broadcast_add_fusion.2.list_ref, f32[2,4,6]{2,1,0:T(4,128)S(1)} %copy-done, f32[16]{0:T(128)S(1)} %copy-done.1, f32[97,8,128]{2,1,0:T(8,128)S(1)} %collective-permute-done.strain_ref, ...), custom_call_target="tpu_custom_call" | custom-call | flops 1024 | bytes 1024 | tf_op jit(solution)/shard_map/other_images/pallas_call | solution.py:206
  14.7 1.6 %collective-permute-start.2 = (f32[512,128]{1,0:T(8,128)S(1)}, f32[512,128]{1,0:T(8,128)S(1)}, u32[]{:S(2)}, u32[]{:S(2)}) collective-permute-start(f32[512,128]{1,0:T(8,128)S(1)} %get-tuple-element.56), channel_id=1, source_target_pairs={{0,4},{1,9},{2,6},{3,11},{4,0},{5,13},{6,2},{7,15},{8,12},{9,1},{1... | collective-permute-start | bytes 786440 | tf_op jit(solution)/shard_map/ppermute | solution.py:297
  16.3 1.7 %other_images.5 = (f32[512,128]{1,0:T(8,128)S(1)}, f32[512,128]{1,0:T(8,128)S(1)}) custom-call(s32[2]{0:T(128)S(1)} %get-tuple-element.101.count_ref, s32[2,128]{1,0:T(2,128)S(1)} %broadcast_add_fusion.2.list_ref, f32[2,4,6]{2,1,0:T(4,128)S(1)} %copy-done, f32[16]{0:T(128)S(1)} %copy-done.1, f32[96,8,128]{2,1,0:T(8,128)S(1)} %collective-permute-done.3.strain_ref, ...), custom_call_target="tpu_custom_call" | custom-call | flops 1024 | bytes 1024 | tf_op jit(solution)/shard_map/other_images/pallas_call | solution.py:206
  18.0 0.9 %collective-permute-start.7 = (f32[512,128]{1,0:T(8,128)S(1)}, f32[512,128]{1,0:T(8,128)S(1)}, u32[]{:S(2)}, u32[]{:S(2)}) collective-permute-start(f32[512,128]{1,0:T(8,128)S(1)} %get-tuple-element.59), channel_id=1, source_target_pairs={{0,4},{1,9},{2,6},{3,11},{4,0},{5,13},{6,2},{7,15},{8,12},{9,1},{1... | collective-permute-start | bytes 786440 | tf_op jit(solution)/shard_map/ppermute | solution.py:297
  18.9 1.2 %collective-permute-start.6 = (f32[97,8,128]{2,1,0:T(8,128)S(1)}, f32[97,8,128]{2,1,0:T(8,128)S(1)}, u32[]{:S(2)}, u32[]{:S(2)}) collective-permute-start(f32[97,8,128]{2,1,0:T(8,128)S(1)} %pad_maximum_fusion.refs_7_), channel_id=1, source_target_pairs={{0,4},{4,0},{8,12},{12,8},{16,20},{20,16},{24,28},{28,24},{1,5},{5... | collective-permute-start | bytes 1191944 | tf_op jit(solution)/shard_map/ppermute | solution.py:299
  20.2 2.8 %own_images.3 = (f32[1040,128]{1,0:T(8,128)S(1)}, f32[1040,128]{1,0:T(8,128)S(1)}) custom-call(s32[2]{0:T(128)S(1)} %get-tuple-element.97.refs_0_, s32[2,128]{1,0:T(2,128)S(1)} %broadcast_add_fusion.1.refs_1_, s32[2]{0:T(128)S(1)} %get-tuple-element.127.refs_0_.refs_2_, s32[2,128]{1,0:T(2,128)S(1)} %broadcast_add_fusion.3.refs_1_.refs_3_, ...), custom_call_target="tpu_custom_call" | custom-call | flops 1024 | bytes 1024 | tf_op jit(solution)/shard_map/own_images/pallas_call | solution.py:179
  23.1 2.7 %collective-permute-start.5 = (f32[256,128]{1,0:T(8,128)S(1)}, f32[256,128]{1,0:T(8,128)S(1)}, u32[]{:S(2)}, u32[]{:S(2)}) collective-permute-start(f32[256,128]{1,0:T(8,128)S(1)} %slice_add_fusion.3), channel_id=1, source_target_pairs={{0,16},{4,20},{8,24},{12,28},{16,0},{20,4},{24,8},{28,12},{1,17},{... | collective-permute-start | bytes 393224 | tf_op jit(solution)/shard_map/ppermute | solution.py:299
  25.8 1.7 %other_images.6 = (f32[512,128]{1,0:T(8,128)S(1)}, f32[512,128]{1,0:T(8,128)S(1)}) custom-call(s32[2]{0:T(128)S(1)} %get-tuple-element.101.count_ref, s32[2,128]{1,0:T(2,128)S(1)} %broadcast_add_fusion.2.list_ref, f32[2,4,6]{2,1,0:T(4,128)S(1)} %copy-done, f32[16]{0:T(128)S(1)} %copy-done.1, f32[96,8,128]{2,1,0:T(8,128)S(1)} %collective-permute-done.1.strain_ref, ...), custom_call_target="tpu_custom_call" | custom-call | flops 1024 | bytes 1024 | tf_op jit(solution)/shard_map/other_images/pallas_call | solution.py:206
  27.5 1.2 %collective-permute-start.4 = (f32[512,128]{1,0:T(8,128)S(1)}, f32[512,128]{1,0:T(8,128)S(1)}, u32[]{:S(2)}, u32[]{:S(2)}) collective-permute-start(f32[512,128]{1,0:T(8,128)S(1)} %get-tuple-element.65), channel_id=1, source_target_pairs={{0,4},{1,9},{2,6},{3,11},{4,0},{5,13},{6,2},{7,15},{8,12},{9,1},{1... | collective-permute-start | bytes 786440 | tf_op jit(solution)/shard_map/ppermute | solution.py:297
  28.9 1.8 %collective-permute-start.11 = (f32[256,128]{1,0:T(8,128)S(1)}, f32[256,128]{1,0:T(8,128)S(1)}, u32[]{:S(2)}, u32[]{:S(2)}) collective-permute-start(f32[256,128]{1,0:T(8,128)S(1)} %slice_add_fusion.2), channel_id=1, source_target_pairs={{0,16},{4,20},{8,24},{12,28},{16,0},{20,4},{24,8},{28,12},{1,17},{... | collective-permute-start | bytes 393224 | tf_op jit(solution)/shard_map/ppermute | solution.py:299
  30.7 1.7 %collective-permute-done.6.strain_ref = f32[97,8,128]{2,1,0:T(8,128)S(1)} collective-permute-done((f32[97,8,128]{2,1,0:T(8,128)S(1)}, f32[97,8,128]{2,1,0:T(8,128)S(1)}, u32[]{:S(2)}, u32[]{:S(2)}) %collective-permute-start.6) | collective-permute-done | bytes 397344 | tf_op jit(solution)/shard_map/ppermute | solution.py:299
  32.8 1.7 %other_images.7 = (f32[512,128]{1,0:T(8,128)S(1)}, f32[512,128]{1,0:T(8,128)S(1)}) custom-call(s32[2]{0:T(128)S(1)} %get-tuple-element.93.count_ref, s32[2,128]{1,0:T(2,128)S(1)} %broadcast_add_fusion.list_ref, f32[2,4,6]{2,1,0:T(4,128)S(1)} %copy-done, f32[16]{0:T(128)S(1)} %copy-done.1, f32[97,8,128]{2,1,0:T(8,128)S(1)} %collective-permute-done.6.strain_ref, ...), custom_call_target="tpu_custom_call" | custom-call | flops 1024 | bytes 1024 | tf_op jit(solution)/shard_map/other_images/pallas_call | solution.py:206
  34.6 1.8 %collective-permute-start.9 = (f32[512,128]{1,0:T(8,128)S(1)}, f32[512,128]{1,0:T(8,128)S(1)}, u32[]{:S(2)}, u32[]{:S(2)}) collective-permute-start(f32[512,128]{1,0:T(8,128)S(1)} %get-tuple-element.74), channel_id=1, source_target_pairs={{0,8},{4,12},{8,0},{12,4},{16,24},{20,28},{24,16},{28,20},{1,9},{5... | collective-permute-start | bytes 786440 | tf_op jit(solution)/shard_map/ppermute | solution.py:299
  36.4 1.6 %collective-permute-start.10 = (f32[256,128]{1,0:T(8,128)S(1)}, f32[256,128]{1,0:T(8,128)S(1)}, u32[]{:S(2)}, u32[]{:S(2)}) collective-permute-start(f32[256,128]{1,0:T(8,128)S(1)} %add_add_fusion.3), channel_id=1, source_target_pairs={{0,2},{1,3},{2,0},{3,1},{4,6},{5,7},{6,4},{7,5},{8,10},{9,11},{10,... | collective-permute-start | bytes 393224 | tf_op jit(solution)/shard_map/ppermute | solution.py:299
  38.0 2.7 %collective-permute-start.8 = (f32[256,128]{1,0:T(8,128)S(1)}, f32[256,128]{1,0:T(8,128)S(1)}, u32[]{:S(2)}, u32[]{:S(2)}) collective-permute-start(f32[256,128]{1,0:T(8,128)S(1)} %slice_add_fusion.1), channel_id=1, source_target_pairs={{0,16},{4,20},{8,24},{12,28},{16,0},{20,4},{24,8},{28,12},{1,17},{... | collective-permute-start | bytes 393224 | tf_op jit(solution)/shard_map/ppermute | solution.py:299
  40.7 0.6 %collective-permute-start.13 = (f32[256,128]{1,0:T(8,128)S(1)}, f32[256,128]{1,0:T(8,128)S(1)}, u32[]{:S(2)}, u32[]{:S(2)}) collective-permute-start(f32[256,128]{1,0:T(8,128)S(1)} %add_add_fusion.1), channel_id=1, source_target_pairs={{0,2},{1,3},{2,0},{3,1},{4,6},{5,7},{6,4},{7,5},{8,10},{9,11},{10,... | collective-permute-start | bytes 393224 | tf_op jit(solution)/shard_map/ppermute | solution.py:299
  41.4 2.3 %collective-permute-done.9 = f32[512,128]{1,0:T(8,128)S(1)} collective-permute-done((f32[512,128]{1,0:T(8,128)S(1)}, f32[512,128]{1,0:T(8,128)S(1)}, u32[]{:S(2)}, u32[]{:S(2)}) %collective-permute-start.9) | collective-permute-done | bytes 262176 | tf_op jit(solution)/shard_map/ppermute | solution.py:299
  43.8 1.5 %collective-permute-start.12 = (f32[256,128]{1,0:T(8,128)S(1)}, f32[256,128]{1,0:T(8,128)S(1)}, u32[]{:S(2)}, u32[]{:S(2)}) collective-permute-start(f32[256,128]{1,0:T(8,128)S(1)} %slice_add_fusion), channel_id=1, source_target_pairs={{0,16},{4,20},{8,24},{12,28},{16,0},{20,4},{24,8},{28,12},{1,17},{... | collective-permute-start | bytes 393224 | tf_op jit(solution)/shard_map/ppermute | solution.py:299
  45.3 1.6 %collective-permute-start.14 = (f32[256,128]{1,0:T(8,128)S(1)}, f32[256,128]{1,0:T(8,128)S(1)}, u32[]{:S(2)}, u32[]{:S(2)}) collective-permute-start(f32[256,128]{1,0:T(8,128)S(1)} %add_add_fusion.2), channel_id=1, source_target_pairs={{0,2},{1,3},{2,0},{3,1},{4,6},{5,7},{6,4},{7,5},{8,10},{9,11},{10,... | collective-permute-start | bytes 393224 | tf_op jit(solution)/shard_map/ppermute | solution.py:299
  47.0 4.1 %collective-permute-done.12 = f32[256,128]{1,0:T(8,128)S(1)} collective-permute-done((f32[256,128]{1,0:T(8,128)S(1)}, f32[256,128]{1,0:T(8,128)S(1)}, u32[]{:S(2)}, u32[]{:S(2)}) %collective-permute-start.12) | collective-permute-done | bytes 131104 | tf_op jit(solution)/shard_map/ppermute | solution.py:299
  51.1 2.1 %collective-permute-start.15 = (f32[256,128]{1,0:T(8,128)S(1)}, f32[256,128]{1,0:T(8,128)S(1)}, u32[]{:S(2)}, u32[]{:S(2)}) collective-permute-start(f32[256,128]{1,0:T(8,128)S(1)} %add_add_fusion), channel_id=1, source_target_pairs={{0,2},{1,3},{2,0},{3,1},{4,6},{5,7},{6,4},{7,5},{8,10},{9,11},{10,... | collective-permute-start | bytes 393224 | tf_op jit(solution)/shard_map/ppermute | solution.py:299
  53.9 2.3 %collective-permute-done.15 = f32[256,128]{1,0:T(8,128)S(1)} collective-permute-done((f32[256,128]{1,0:T(8,128)S(1)}, f32[256,128]{1,0:T(8,128)S(1)}, u32[]{:S(2)}, u32[]{:S(2)}) %collective-permute-start.15) | collective-permute-done | bytes 131104 | tf_op jit(solution)/shard_map/ppermute | solution.py:299
  56.3 0.7 %resolve.2.refs_12_ = f32[256,512]{1,0:T(8,128)S(1)} custom-call(bf16[128,512]{1,0:T(8,128)(2,1)S(1)} %get-tuple-element.113.refs_0_, bf16[128,512]{1,0:T(8,128)(2,1)S(1)} %get-tuple-element.112.refs_1_, bf16[128,512]{1,0:T(8,128)(2,1)S(1)} %get-tuple-element.111.refs_2_, bf16[128,512]{1,0:T(8,128)(2,1)S(1)} %get-tuple-element.110.refs_3_, ...), custom_call_target="tpu_custom_call" | custom-call | flops 1024 | bytes 1024 | tf_op jit(solution)/shard_map/resolve/pallas_call | solution.py:240
  57.1 0.8 %collective-permute-done.17.refs_11_ = f32[512,128]{1,0:T(8,128)S(1)} collective-permute-done((f32[512,128]{1,0:T(8,128)S(1)}, f32[512,128]{1,0:T(8,128)S(1)}, u32[]{:S(2)}, u32[]{:S(2)}) %collective-permute-start.17) | collective-permute-done | bytes 262176 | tf_op jit(solution)/shard_map/ppermute | solution.py:299
  57.8 1.5 %resolve.3 = f32[256,512]{1,0:T(8,128)} custom-call(bf16[128,512]{1,0:T(8,128)(2,1)S(1)} %get-tuple-element.122.refs_0_, bf16[128,512]{1,0:T(8,128)(2,1)S(1)} %get-tuple-element.121.refs_1_, bf16[128,512]{1,0:T(8,128)(2,1)S(1)} %get-tuple-element.120.refs_2_, bf16[128,512]{1,0:T(8,128)(2,1)S(1)} %get-tuple-element.119.refs_3_, ...), custom_call_target="tpu_custom_call" | custom-call | flops 1024 | bytes 1024 | tf_op jit(solution)/shard_map/resolve/pallas_call | solution.py:240
  (65 shorter events, 2.7 us)
Async XLA Ops:
  0.0 5.0 %copy-start.3 = (f32[128,6,512]{2,0,1:T(8,128)S(1)}, f32[128,6,512]{2,0,1:T(8,128)}, u32[]{:S(2)}) copy-start(f32[128,6,512]{2,0,1:T(8,128)} %param.6) | copy-start | bytes 4718596
  0.0 6.3 %copy-start.1 = (f32[16]{0:T(128)S(1)}, f32[16]{0:T(128)}, u32[]{:S(2)}) copy-start(f32[16]{0:T(128)} %rock_ref.7) | copy-start | bytes 196
  0.0 6.3 %copy-start = (f32[2,4,6]{2,1,0:T(4,128)S(1)}, f32[2,4,6]{2,1,0:T(4,128)}, u32[]{:S(2)}) copy-start(f32[2,4,6]{2,1,0:T(4,128)} %dirs_ref.7) | copy-start | bytes 580
  1.9 10.6 %collective-permute-start = (f32[97,8,128]{2,1,0:T(8,128)S(1)}, f32[97,8,128]{2,1,0:T(8,128)S(1)}, u32[]{:S(2)}, u32[]{:S(2)}) collective-permute-start(f32[97,8,128]{2,1,0:T(8,128)S(1)} %pad_maximum_fusion.1.refs_4_), channel_id=1, source_target_pairs={{0,8},{1,5},{2,10},{3,7},{4,12},{5,1},{6,14},{7,3},{8,0},{9,13},{1... | collective-permute-start | bytes 1191944 | tf_op jit(solution)/shard_map/ppermute | solution.py:297
  5.8 10.5 %collective-permute-start.3 = (f32[96,8,128]{2,1,0:T(8,128)S(1)}, f32[96,8,128]{2,1,0:T(8,128)S(1)}, u32[]{:S(2)}, u32[]{:S(2)}) collective-permute-start(f32[96,8,128]{2,1,0:T(8,128)S(1)} %get-tuple-element.48.refs_5_), channel_id=1, source_target_pairs={{0,8},{1,5},{2,10},{3,7},{4,12},{5,1},{6,14},{7,3},{8,0},{9,13},{1... | collective-permute-start | bytes 1179656 | tf_op jit(solution)/shard_map/ppermute | solution.py:297
  9.2 16.6 %collective-permute-start.1 = (f32[96,8,128]{2,1,0:T(8,128)S(1)}, f32[96,8,128]{2,1,0:T(8,128)S(1)}, u32[]{:S(2)}, u32[]{:S(2)}) collective-permute-start(f32[96,8,128]{2,1,0:T(8,128)S(1)} %get-tuple-element.61.refs_6_), channel_id=1, source_target_pairs={{0,8},{1,5},{2,10},{3,7},{4,12},{5,1},{6,14},{7,3},{8,0},{9,13},{1... | collective-permute-start | bytes 1179656 | tf_op jit(solution)/shard_map/ppermute | solution.py:297
  12.5 16.2 %copy-start.2 = (bf16[2048,512]{1,0:T(8,128)(2,1)S(1)}, bf16[2048,512]{1,0:T(8,128)(2,1)}, u32[]{:S(2)}) copy-start(bf16[2048,512]{1,0:T(8,128)(2,1)} %param.11) | copy-start | bytes 6291460
  14.7 8.4 %collective-permute-start.2 = (f32[512,128]{1,0:T(8,128)S(1)}, f32[512,128]{1,0:T(8,128)S(1)}, u32[]{:S(2)}, u32[]{:S(2)}) collective-permute-start(f32[512,128]{1,0:T(8,128)S(1)} %get-tuple-element.56), channel_id=1, source_target_pairs={{0,4},{1,9},{2,6},{3,11},{4,0},{5,13},{6,2},{7,15},{8,12},{9,1},{1... | collective-permute-start | bytes 786440 | tf_op jit(solution)/shard_map/ppermute | solution.py:297
  18.0 10.8 %collective-permute-start.7 = (f32[512,128]{1,0:T(8,128)S(1)}, f32[512,128]{1,0:T(8,128)S(1)}, u32[]{:S(2)}, u32[]{:S(2)}) collective-permute-start(f32[512,128]{1,0:T(8,128)S(1)} %get-tuple-element.59), channel_id=1, source_target_pairs={{0,4},{1,9},{2,6},{3,11},{4,0},{5,13},{6,2},{7,15},{8,12},{9,1},{1... | collective-permute-start | bytes 786440 | tf_op jit(solution)/shard_map/ppermute | solution.py:297
  18.9 13.6 %collective-permute-start.6 = (f32[97,8,128]{2,1,0:T(8,128)S(1)}, f32[97,8,128]{2,1,0:T(8,128)S(1)}, u32[]{:S(2)}, u32[]{:S(2)}) collective-permute-start(f32[97,8,128]{2,1,0:T(8,128)S(1)} %pad_maximum_fusion.refs_7_), channel_id=1, source_target_pairs={{0,4},{4,0},{8,12},{12,8},{16,20},{20,16},{24,28},{28,24},{1,5},{5... | collective-permute-start | bytes 1191944 | tf_op jit(solution)/shard_map/ppermute | solution.py:299
  23.1 13.3 %collective-permute-start.5 = (f32[256,128]{1,0:T(8,128)S(1)}, f32[256,128]{1,0:T(8,128)S(1)}, u32[]{:S(2)}, u32[]{:S(2)}) collective-permute-start(f32[256,128]{1,0:T(8,128)S(1)} %slice_add_fusion.3), channel_id=1, source_target_pairs={{0,16},{4,20},{8,24},{12,28},{16,0},{20,4},{24,8},{28,12},{1,17},{... | collective-permute-start | bytes 393224 | tf_op jit(solution)/shard_map/ppermute | solution.py:299
  27.5 10.5 %collective-permute-start.4 = (f32[512,128]{1,0:T(8,128)S(1)}, f32[512,128]{1,0:T(8,128)S(1)}, u32[]{:S(2)}, u32[]{:S(2)}) collective-permute-start(f32[512,128]{1,0:T(8,128)S(1)} %get-tuple-element.65), channel_id=1, source_target_pairs={{0,4},{1,9},{2,6},{3,11},{4,0},{5,13},{6,2},{7,15},{8,12},{9,1},{1... | collective-permute-start | bytes 786440 | tf_op jit(solution)/shard_map/ppermute | solution.py:297
  28.9 11.8 %collective-permute-start.11 = (f32[256,128]{1,0:T(8,128)S(1)}, f32[256,128]{1,0:T(8,128)S(1)}, u32[]{:S(2)}, u32[]{:S(2)}) collective-permute-start(f32[256,128]{1,0:T(8,128)S(1)} %slice_add_fusion.2), channel_id=1, source_target_pairs={{0,16},{4,20},{8,24},{12,28},{16,0},{20,4},{24,8},{28,12},{1,17},{... | collective-permute-start | bytes 393224 | tf_op jit(solution)/shard_map/ppermute | solution.py:299
  34.6 9.2 %collective-permute-start.9 = (f32[512,128]{1,0:T(8,128)S(1)}, f32[512,128]{1,0:T(8,128)S(1)}, u32[]{:S(2)}, u32[]{:S(2)}) collective-permute-start(f32[512,128]{1,0:T(8,128)S(1)} %get-tuple-element.74), channel_id=1, source_target_pairs={{0,8},{4,12},{8,0},{12,4},{16,24},{20,28},{24,16},{28,20},{1,9},{5... | collective-permute-start | bytes 786440 | tf_op jit(solution)/shard_map/ppermute | solution.py:299
  36.4 5.0 %collective-permute-start.10 = (f32[256,128]{1,0:T(8,128)S(1)}, f32[256,128]{1,0:T(8,128)S(1)}, u32[]{:S(2)}, u32[]{:S(2)}) collective-permute-start(f32[256,128]{1,0:T(8,128)S(1)} %add_add_fusion.3), channel_id=1, source_target_pairs={{0,2},{1,3},{2,0},{3,1},{4,6},{5,7},{6,4},{7,5},{8,10},{9,11},{10,... | collective-permute-start | bytes 393224 | tf_op jit(solution)/shard_map/ppermute | solution.py:299
  38.0 7.3 %collective-permute-start.8 = (f32[256,128]{1,0:T(8,128)S(1)}, f32[256,128]{1,0:T(8,128)S(1)}, u32[]{:S(2)}, u32[]{:S(2)}) collective-permute-start(f32[256,128]{1,0:T(8,128)S(1)} %slice_add_fusion.1), channel_id=1, source_target_pairs={{0,16},{4,20},{8,24},{12,28},{16,0},{20,4},{24,8},{28,12},{1,17},{... | collective-permute-start | bytes 393224 | tf_op jit(solution)/shard_map/ppermute | solution.py:299
  40.7 6.3 %collective-permute-start.13 = (f32[256,128]{1,0:T(8,128)S(1)}, f32[256,128]{1,0:T(8,128)S(1)}, u32[]{:S(2)}, u32[]{:S(2)}) collective-permute-start(f32[256,128]{1,0:T(8,128)S(1)} %add_add_fusion.1), channel_id=1, source_target_pairs={{0,2},{1,3},{2,0},{3,1},{4,6},{5,7},{6,4},{7,5},{8,10},{9,11},{10,... | collective-permute-start | bytes 393224 | tf_op jit(solution)/shard_map/ppermute | solution.py:299
  41.3 15.0 %collective-permute-start.18 = (f32[512,128]{1,0:T(8,128)S(1)}, f32[512,128]{1,0:T(8,128)S(1)}, u32[]{:S(2)}, u32[]{:S(2)}) collective-permute-start(f32[512,128]{1,0:T(8,128)S(1)} %pad_maximum_fusion.4.refs_8_), channel_id=1, source_target_pairs={{0,1},{1,0},{2,3},{3,2},{4,5},{5,4},{6,7},{7,6},{8,9},{9,8},{10,11... | collective-permute-start | bytes 786440 | tf_op jit(solution)/shard_map/ppermute | solution.py:299
  43.8 7.3 %collective-permute-start.12 = (f32[256,128]{1,0:T(8,128)S(1)}, f32[256,128]{1,0:T(8,128)S(1)}, u32[]{:S(2)}, u32[]{:S(2)}) collective-permute-start(f32[256,128]{1,0:T(8,128)S(1)} %slice_add_fusion), channel_id=1, source_target_pairs={{0,16},{4,20},{8,24},{12,28},{16,0},{20,4},{24,8},{28,12},{1,17},{... | collective-permute-start | bytes 393224 | tf_op jit(solution)/shard_map/ppermute | solution.py:299
  45.3 8.6 %collective-permute-start.14 = (f32[256,128]{1,0:T(8,128)S(1)}, f32[256,128]{1,0:T(8,128)S(1)}, u32[]{:S(2)}, u32[]{:S(2)}) collective-permute-start(f32[256,128]{1,0:T(8,128)S(1)} %add_add_fusion.2), channel_id=1, source_target_pairs={{0,2},{1,3},{2,0},{3,1},{4,6},{5,7},{6,4},{7,5},{8,10},{9,11},{10,... | collective-permute-start | bytes 393224 | tf_op jit(solution)/shard_map/ppermute | solution.py:299
  51.1 5.1 %collective-permute-start.15 = (f32[256,128]{1,0:T(8,128)S(1)}, f32[256,128]{1,0:T(8,128)S(1)}, u32[]{:S(2)}, u32[]{:S(2)}) collective-permute-start(f32[256,128]{1,0:T(8,128)S(1)} %add_add_fusion), channel_id=1, source_target_pairs={{0,2},{1,3},{2,0},{3,1},{4,6},{5,7},{6,4},{7,5},{8,10},{9,11},{10,... | collective-permute-start | bytes 393224 | tf_op jit(solution)/shard_map/ppermute | solution.py:299
  53.3 3.0 %collective-permute-start.19 = (f32[512,128]{1,0:T(8,128)S(1)}, f32[512,128]{1,0:T(8,128)S(1)}, u32[]{:S(2)}, u32[]{:S(2)}) collective-permute-start(f32[512,128]{1,0:T(8,128)S(1)} %pad_maximum_fusion.5.refs_10_), channel_id=1, source_target_pairs={{0,1},{1,0},{2,3},{3,2},{4,5},{5,4},{6,7},{7,6},{8,9},{9,8},{10,11... | collective-permute-start | bytes 786440 | tf_op jit(solution)/shard_map/ppermute | solution.py:299
  53.4 3.7 %collective-permute-start.16 = (f32[512,128]{1,0:T(8,128)S(1)}, f32[512,128]{1,0:T(8,128)S(1)}, u32[]{:S(2)}, u32[]{:S(2)}) collective-permute-start(f32[512,128]{1,0:T(8,128)S(1)} %pad_maximum_fusion.2.refs_8_), channel_id=1, source_target_pairs={{0,1},{1,0},{2,3},{3,2},{4,5},{5,4},{6,7},{7,6},{8,9},{9,8},{10,11... | collective-permute-start | bytes 786440 | tf_op jit(solution)/shard_map/ppermute | solution.py:299
  56.2 1.6 %collective-permute-start.17 = (f32[512,128]{1,0:T(8,128)S(1)}, f32[512,128]{1,0:T(8,128)S(1)}, u32[]{:S(2)}, u32[]{:S(2)}) collective-permute-start(f32[512,128]{1,0:T(8,128)S(1)} %pad_maximum_fusion.3.refs_10_), channel_id=1, source_target_pairs={{0,1},{1,0},{2,3},{3,2},{4,5},{5,4},{6,7},{7,6},{8,9},{9,8},{10,11... | collective-permute-start | bytes 786440 | tf_op jit(solution)/shard_map/ppermute | solution.py:299

commit v7 on v6

--- a/solution.py
+++ b/solution.py
@@ -188,7 +188,7 @@
     )(*[x for listing in listings for x in listing], dirs, rock, *strains)
 
 
-def other_images(listing, dirs, rock, strain, init, tiles, half):
+def other_images(listing, dirs, rock, strain, init, tiles, half, norm):
     angles, qcount, comps = dirs.shape
     rocks = rock.shape[0]
 
@@ -196,7 +196,7 @@
         rock = prepared_rocks(rock_ref)
         acc[...] = init_ref[...]
         add_tiles(count_ref, list_ref, dirs_ref, rock, strain_ref, proj, acc)
-        factor = jnp.exp2(-(rock * rock))
+        factor = jnp.exp2(-(rock * rock)) * norm
         for start, out in ((0, sent_ref), (half, kept_ref)):
             for row in range(0, half, rocks):
                 out[pl.ds(row, rocks), :] = acc[pl.ds(start + row, rocks), :] * factor
@@ -218,7 +218,7 @@
     )(*listing, dirs, rock, strain, init)
 
 
-def resolve(norm, unit, total, blocks, parts):
+def resolve(unit, total, blocks, parts):
     cols = blocks[0].shape[1]
     vmem = pl.BlockSpec(memory_space=pltpu.VMEM)
     before = () if total is None else (total,)
@@ -226,7 +226,7 @@
     def kernel(*refs):
         block_refs, part_refs, out_ref = refs[: len(blocks)], refs[len(blocks) : len(blocks) + len(parts)], refs[-1]
         values = [
-            part[pl.ds(start, unit), :] * norm for part in part_refs for start in range(0, part.shape[0], unit)
+            part[pl.ds(start, unit), :] for part in part_refs for start in range(0, part.shape[0], unit)
         ]
         value = jnp.concatenate(values, axis=1)
         block = jnp.concatenate([ref[...] for ref in block_refs], axis=0)
@@ -375,7 +375,7 @@
         k = plan_of[c]
         if k not in other_list:
             learn(c)
-        sent, held[c] = other_images(other_list[k], dirs, rock_angles, tie(other[c]), partial[c], tiles, half)
+        sent, held[c] = other_images(other_list[k], dirs, rock_angles, tie(other[c]), partial[c], tiles, half, norm)
         mark(sent)
         flying[c] = swap(sent, plans[k][1][0])
 
@@ -431,7 +431,7 @@
     def multiply(*group):
         parts = found[group]
         total = result[-1] if result else None
-        result.append(mark(resolve(norm, unit, total, blocks[group], [tie(parts[0])] + parts[1:])))
+        result.append(mark(resolve(unit, total, blocks[group], [tie(parts[0])] + parts[1:])))
 
     if plan_of == list(SCHEDULED):
         steps = SCHEDULE

time: 59.7 us -> 59.7 us (level)
  starting transfers between devices: 27.4 us -> 23.7 us
  Pallas kernels: 14.8 us -> 17.8 us
  waiting for transfers between devices: 11.3 us -> 12.5 us
    ppermute x14, starting transfers between devices: 18.4 us -> 16.6 us  [swap(): lax.ppermute(value, axis, [(i, i ^ 1 << number) for i in range(lax.axis_s...]
    ppermute x6, starting transfers between devices: 9.03 us -> 7.19 us  [swap(): return lax.ppermute(value, ('slab', 'rock'), pairs)]
    pallas_call x4, Pallas kernels: 6.93 us -> 8.54 us  [other_images(): pl.pallas_call(kernel, out_shape=[jax.ShapeDtypeStruct((half, LANES), jnp...]
    pallas_call x2, Pallas kernels: 5.66 us -> 7.02 us  [own_images(): pl.pallas_call(kernel, out_shape=[jax.ShapeDtypeStruct((rows, LANES), jnp...]
    ppermute x14, waiting for transfers between devices: 11.3 us -> 12.5 us  [swap(): lax.ppermute(value, axis, [(i, i ^ 1 << number) for i in range(lax.axis_s...]
  transfers between devices with their start and end apart: 20 -> 20, of which waited for: 6 -> 6; matrix products, arithmetic and copies ran while one was open for 6% -> 6% of each run, Pallas kernels for 22% -> 27%
where the time goes in v7:
time: 59.7 us; the launch traced here: 59.8 us
  starting transfers between devices  23.7 us (40%)
  Pallas kernels  17.8 us (30%)
  waiting for transfers between devices  12.5 us (21%)
  other arithmetic  3.4 us (6%)
  local copies, waits for them, and re-layouts  2.02 us (3%)
    ppermute x14, starting transfers between devices, swap(): lax.ppermute(value, axis, [(i, i ^ 1 << number) for i in range(lax.axis_s...  16.6 us
    ppermute x14, waiting for transfers between devices, swap(): lax.ppermute(value, axis, [(i, i ^ 1 << number) for i in range(lax.axis_s...  12.5 us
    pallas_call x4, Pallas kernels, other_images(): pl.pallas_call(kernel, out_shape=[jax.ShapeDtypeStruct((half, LANES), jnp...  8.54 us
    ppermute x6, starting transfers between devices, swap(): return lax.ppermute(value, ('slab', 'rock'), pairs)  7.19 us
    pallas_call x2, Pallas kernels, own_images(): pl.pallas_call(kernel, out_shape=[jax.ShapeDtypeStruct((rows, LANES), jnp...  7.02 us
    pallas_call x2, Pallas kernels, resolve(): pl.pallas_call(kernel, out_shape=jax.ShapeDtypeStruct((unit, cols), jnp.f...  2.22 us
    slice x2, local copies, waits for them, and re-layouts, piece(): block = source[:, :, c * LANES:(c + 1) * LANES]  1.84 us
  transfers between devices with their start and end apart: 20, of which 6 were waited for; matrix products, arithmetic and copies ran while one was open for 6% of the time, Pallas kernels for 27%

profile of v7, /device:TPU:0, one launch (start us, length us, event | category | flops | bytes accessed | tf_op | source)
XLA Modules:
  0.0 59.8 jit_solution(7918554702839323147)
XLA Ops:
  0.0 0.8 %fusion.14 = (f32[2,128]{1,0:T(2,128)S(1)}, s32[2,128]{1,0:T(2,128)S(1)}) fusion(s32[2,128]{1,0:T(2,128)} %param.8, s32[2,128,1]{1,0,2:T(2,128)} %bitcast.54), kind=kLoop, calls=%fused_computation.109 | loop fusion | flops 768 | bytes 4096 | tf_op jit(solution)/shard_map/convert_element_type | solution.py:317
  0.8 1.0 %slice.94 = f32[96,8,128]{2,1,0:T(8,128)S(1)} slice(f32[96,8,512]{2,1,0:T(8,128)} %bitcast.52), slice={[0:96], [0:8], [0:128]} | slice | bytes 786432 | tf_op jit(solution)/shard_map/slice | solution.py:324
  1.9 3.1 %collective-permute-start = (f32[97,8,128]{2,1,0:T(8,128)S(1)}, f32[97,8,128]{2,1,0:T(8,128)S(1)}, u32[]{:S(2)}, u32[]{:S(2)}) collective-permute-start(f32[97,8,128]{2,1,0:T(8,128)S(1)} %pad_maximum_fusion.1.refs_4_), channel_id=1, source_target_pairs={{0,8},{1,5},{2,10},{3,7},{4,12},{5,1},{6,14},{7,3},{8,0},{9,13},{1... | collective-permute-start | bytes 1191944 | tf_op jit(solution)/shard_map/ppermute | solution.py:297
  5.0 0.8 %fusion.15 = (f32[96,8,128]{2,1,0:T(8,128)}, f32[96,8,128]{2,1,0:T(8,128)S(1)}, f32[96,8,128]{2,1,0:T(8,128)S(1)}) fusion(f32[96,8,512]{2,1,0:T(8,128)S(1)} %bitcast.53), kind=kLoop, calls=%fused_computation.110 | loop fusion | bytes 2359296 | tf_op jit(solution)/shard_map/slice | solution.py:324
  6.3 3.4 %own_images.2 = (f32[1040,128]{1,0:T(8,128)S(1)}, f32[1040,128]{1,0:T(8,128)S(1)}) custom-call(s32[2]{0:T(128)S(1)} %get-tuple-element.127.refs_0_.refs_2_, s32[2,128]{1,0:T(2,128)S(1)} %broadcast_add_fusion.3.refs_1_.refs_3_, f32[2,4,6]{2,1,0:T(4,128)S(1)} %copy-done, f32[16]{0:T(128)S(1)} %copy-done.1, f32[97,8,128]{2,1,0:T(8,128)S(1)} %pad_maximum_fusion.1.refs_4_, ...), custom_call_target="tpu_custom_call" | custom-call | flops 1024 | bytes 1024 | tf_op jit(solution)/shard_map/own_images/pallas_call | solution.py:179
  9.7 1.1 %collective-permute-start.1 = (f32[96,8,128]{2,1,0:T(8,128)S(1)}, f32[96,8,128]{2,1,0:T(8,128)S(1)}, u32[]{:S(2)}, u32[]{:S(2)}) collective-permute-start(f32[96,8,128]{2,1,0:T(8,128)S(1)} %get-tuple-element.61.refs_6_), channel_id=1, source_target_pairs={{0,8},{1,5},{2,10},{3,7},{4,12},{5,1},{6,14},{7,3},{8,0},{9,13},{1... | collective-permute-start | bytes 1179656 | tf_op jit(solution)/shard_map/ppermute | solution.py:297
  10.8 1.0 %pad_maximum_fusion.refs_7_ = f32[97,8,128]{2,1,0:T(8,128)S(1)} fusion(f32[1,8,128]{2,1,0:T(8,128)S(1)} %pad_bitcast_fusion, f32[96,8,128]{2,1,0:T(8,128)} %get-tuple-element.123), kind=kLoop, calls=%fused_computation | loop fusion | flops 99328 | bytes 794624 | tf_op jit(solution)/shard_map/concatenate | solution.py:327
  12.3 2.1 %other_images.4 = (f32[512,128]{1,0:T(8,128)S(1)}, f32[512,128]{1,0:T(8,128)S(1)}) custom-call(s32[2]{0:T(128)S(1)} %get-tuple-element.101.count_ref, s32[2,128]{1,0:T(2,128)S(1)} %broadcast_add_fusion.2.list_ref, f32[2,4,6]{2,1,0:T(4,128)S(1)} %copy-done, f32[16]{0:T(128)S(1)} %copy-done.1, f32[97,8,128]{2,1,0:T(8,128)S(1)} %collective-permute-done.strain_ref, ...), custom_call_target="tpu_custom_call" | custom-call | flops 1024 | bytes 1024 | tf_op jit(solution)/shard_map/other_images/pallas_call | solution.py:206
  14.4 1.6 %collective-permute-start.2 = (f32[512,128]{1,0:T(8,128)S(1)}, f32[512,128]{1,0:T(8,128)S(1)}, u32[]{:S(2)}, u32[]{:S(2)}) collective-permute-start(f32[512,128]{1,0:T(8,128)S(1)} %get-tuple-element.56), channel_id=1, source_target_pairs={{0,4},{1,9},{2,6},{3,11},{4,0},{5,13},{6,2},{7,15},{8,12},{9,1},{1... | collective-permute-start | bytes 786440 | tf_op jit(solution)/shard_map/ppermute | solution.py:297
  16.0 2.1 %other_images.5 = (f32[512,128]{1,0:T(8,128)S(1)}, f32[512,128]{1,0:T(8,128)S(1)}) custom-call(s32[2]{0:T(128)S(1)} %get-tuple-element.101.count_ref, s32[2,128]{1,0:T(2,128)S(1)} %broadcast_add_fusion.2.list_ref, f32[2,4,6]{2,1,0:T(4,128)S(1)} %copy-done, f32[16]{0:T(128)S(1)} %copy-done.1, f32[96,8,128]{2,1,0:T(8,128)S(1)} %collective-permute-done.3.strain_ref, ...), custom_call_target="tpu_custom_call" | custom-call | flops 1024 | bytes 1024 | tf_op jit(solution)/shard_map/other_images/pallas_call | solution.py:206
  18.2 0.9 %collective-permute-start.7 = (f32[512,128]{1,0:T(8,128)S(1)}, f32[512,128]{1,0:T(8,128)S(1)}, u32[]{:S(2)}, u32[]{:S(2)}) collective-permute-start(f32[512,128]{1,0:T(8,128)S(1)} %get-tuple-element.59), channel_id=1, source_target_pairs={{0,4},{1,9},{2,6},{3,11},{4,0},{5,13},{6,2},{7,15},{8,12},{9,1},{1... | collective-permute-start | bytes 786440 | tf_op jit(solution)/shard_map/ppermute | solution.py:297
  19.1 1.2 %collective-permute-start.6 = (f32[97,8,128]{2,1,0:T(8,128)S(1)}, f32[97,8,128]{2,1,0:T(8,128)S(1)}, u32[]{:S(2)}, u32[]{:S(2)}) collective-permute-start(f32[97,8,128]{2,1,0:T(8,128)S(1)} %pad_maximum_fusion.refs_7_), channel_id=1, source_target_pairs={{0,4},{4,0},{8,12},{12,8},{16,20},{20,16},{24,28},{28,24},{1,5},{5... | collective-permute-start | bytes 1191944 | tf_op jit(solution)/shard_map/ppermute | solution.py:299
  20.4 3.6 %own_images.3 = (f32[1040,128]{1,0:T(8,128)S(1)}, f32[1040,128]{1,0:T(8,128)S(1)}) custom-call(s32[2]{0:T(128)S(1)} %get-tuple-element.97.refs_0_, s32[2,128]{1,0:T(2,128)S(1)} %broadcast_add_fusion.1.refs_1_, s32[2]{0:T(128)S(1)} %get-tuple-element.127.refs_0_.refs_2_, s32[2,128]{1,0:T(2,128)S(1)} %broadcast_add_fusion.3.refs_1_.refs_3_, ...), custom_call_target="tpu_custom_call" | custom-call | flops 1024 | bytes 1024 | tf_op jit(solution)/shard_map/own_images/pallas_call | solution.py:179
  24.0 2.5 %collective-permute-start.5 = (f32[256,128]{1,0:T(8,128)S(1)}, f32[256,128]{1,0:T(8,128)S(1)}, u32[]{:S(2)}, u32[]{:S(2)}) collective-permute-start(f32[256,128]{1,0:T(8,128)S(1)} %slice_add_fusion.3), channel_id=1, source_target_pairs={{0,16},{4,20},{8,24},{12,28},{16,0},{20,4},{24,8},{28,12},{1,17},{... | collective-permute-start | bytes 393224 | tf_op jit(solution)/shard_map/ppermute | solution.py:299
  26.5 2.1 %other_images.6 = (f32[512,128]{1,0:T(8,128)S(1)}, f32[512,128]{1,0:T(8,128)S(1)}) custom-call(s32[2]{0:T(128)S(1)} %get-tuple-element.101.count_ref, s32[2,128]{1,0:T(2,128)S(1)} %broadcast_add_fusion.2.list_ref, f32[2,4,6]{2,1,0:T(4,128)S(1)} %copy-done, f32[16]{0:T(128)S(1)} %copy-done.1, f32[96,8,128]{2,1,0:T(8,128)S(1)} %collective-permute-done.1.strain_ref, ...), custom_call_target="tpu_custom_call" | custom-call | flops 1024 | bytes 1024 | tf_op jit(solution)/shard_map/other_images/pallas_call | solution.py:206
  29.3 1.0 %collective-permute-start.11 = (f32[256,128]{1,0:T(8,128)S(1)}, f32[256,128]{1,0:T(8,128)S(1)}, u32[]{:S(2)}, u32[]{:S(2)}) collective-permute-start(f32[256,128]{1,0:T(8,128)S(1)} %slice_add_fusion.2), channel_id=1, source_target_pairs={{0,16},{4,20},{8,24},{12,28},{16,0},{20,4},{24,8},{28,12},{1,17},{... | collective-permute-start | bytes 393224 | tf_op jit(solution)/shard_map/ppermute | solution.py:299
  30.3 2.1 %collective-permute-done.6.strain_ref = f32[97,8,128]{2,1,0:T(8,128)S(1)} collective-permute-done((f32[97,8,128]{2,1,0:T(8,128)S(1)}, f32[97,8,128]{2,1,0:T(8,128)S(1)}, u32[]{:S(2)}, u32[]{:S(2)}) %collective-permute-start.6) | collective-permute-done | bytes 397344 | tf_op jit(solution)/shard_map/ppermute | solution.py:299
  32.8 2.2 %other_images.7 = (f32[512,128]{1,0:T(8,128)S(1)}, f32[512,128]{1,0:T(8,128)S(1)}) custom-call(s32[2]{0:T(128)S(1)} %get-tuple-element.93.count_ref, s32[2,128]{1,0:T(2,128)S(1)} %broadcast_add_fusion.list_ref, f32[2,4,6]{2,1,0:T(4,128)S(1)} %copy-done, f32[16]{0:T(128)S(1)} %copy-done.1, f32[97,8,128]{2,1,0:T(8,128)S(1)} %collective-permute-done.6.strain_ref, ...), custom_call_target="tpu_custom_call" | custom-call | flops 1024 | bytes 1024 | tf_op jit(solution)/shard_map/other_images/pallas_call | solution.py:206
  35.0 1.8 %collective-permute-start.9 = (f32[512,128]{1,0:T(8,128)S(1)}, f32[512,128]{1,0:T(8,128)S(1)}, u32[]{:S(2)}, u32[]{:S(2)}) collective-permute-start(f32[512,128]{1,0:T(8,128)S(1)} %get-tuple-element.74), channel_id=1, source_target_pairs={{0,8},{4,12},{8,0},{12,4},{16,24},{20,28},{24,16},{28,20},{1,9},{5... | collective-permute-start | bytes 786440 | tf_op jit(solution)/shard_map/ppermute | solution.py:299
  36.9 1.6 %collective-permute-start.10 = (f32[256,128]{1,0:T(8,128)S(1)}, f32[256,128]{1,0:T(8,128)S(1)}, u32[]{:S(2)}, u32[]{:S(2)}) collective-permute-start(f32[256,128]{1,0:T(8,128)S(1)} %add_add_fusion.3), channel_id=1, source_target_pairs={{0,2},{1,3},{2,0},{3,1},{4,6},{5,7},{6,4},{7,5},{8,10},{9,11},{10,... | collective-permute-start | bytes 393224 | tf_op jit(solution)/shard_map/ppermute | solution.py:299
  38.5 2.7 %collective-permute-start.8 = (f32[256,128]{1,0:T(8,128)S(1)}, f32[256,128]{1,0:T(8,128)S(1)}, u32[]{:S(2)}, u32[]{:S(2)}) collective-permute-start(f32[256,128]{1,0:T(8,128)S(1)} %slice_add_fusion.1), channel_id=1, source_target_pairs={{0,16},{4,20},{8,24},{12,28},{16,0},{20,4},{24,8},{28,12},{1,17},{... | collective-permute-start | bytes 393224 | tf_op jit(solution)/shard_map/ppermute | solution.py:299
  41.2 0.6 %collective-permute-start.13 = (f32[256,128]{1,0:T(8,128)S(1)}, f32[256,128]{1,0:T(8,128)S(1)}, u32[]{:S(2)}, u32[]{:S(2)}) collective-permute-start(f32[256,128]{1,0:T(8,128)S(1)} %add_add_fusion.1), channel_id=1, source_target_pairs={{0,2},{1,3},{2,0},{3,1},{4,6},{5,7},{6,4},{7,5},{8,10},{9,11},{10,... | collective-permute-start | bytes 393224 | tf_op jit(solution)/shard_map/ppermute | solution.py:299
  41.9 2.5 %collective-permute-done.9 = f32[512,128]{1,0:T(8,128)S(1)} collective-permute-done((f32[512,128]{1,0:T(8,128)S(1)}, f32[512,128]{1,0:T(8,128)S(1)}, u32[]{:S(2)}, u32[]{:S(2)}) %collective-permute-start.9) | collective-permute-done | bytes 262176 | tf_op jit(solution)/shard_map/ppermute | solution.py:299
  44.4 0.9 %collective-permute-start.12 = (f32[256,128]{1,0:T(8,128)S(1)}, f32[256,128]{1,0:T(8,128)S(1)}, u32[]{:S(2)}, u32[]{:S(2)}) collective-permute-start(f32[256,128]{1,0:T(8,128)S(1)} %slice_add_fusion), channel_id=1, source_target_pairs={{0,16},{4,20},{8,24},{12,28},{16,0},{20,4},{24,8},{28,12},{1,17},{... | collective-permute-start | bytes 393224 | tf_op jit(solution)/shard_map/ppermute | solution.py:299
  45.8 1.5 %collective-permute-start.14 = (f32[256,128]{1,0:T(8,128)S(1)}, f32[256,128]{1,0:T(8,128)S(1)}, u32[]{:S(2)}, u32[]{:S(2)}) collective-permute-start(f32[256,128]{1,0:T(8,128)S(1)} %add_add_fusion.2), channel_id=1, source_target_pairs={{0,2},{1,3},{2,0},{3,1},{4,6},{5,7},{6,4},{7,5},{8,10},{9,11},{10,... | collective-permute-start | bytes 393224 | tf_op jit(solution)/shard_map/ppermute | solution.py:299
  47.4 4.3 %collective-permute-done.12 = f32[256,128]{1,0:T(8,128)S(1)} collective-permute-done((f32[256,128]{1,0:T(8,128)S(1)}, f32[256,128]{1,0:T(8,128)S(1)}, u32[]{:S(2)}, u32[]{:S(2)}) %collective-permute-start.12) | collective-permute-done | bytes 131104 | tf_op jit(solution)/shard_map/ppermute | solution.py:299
  51.6 2.0 %collective-permute-start.15 = (f32[256,128]{1,0:T(8,128)S(1)}, f32[256,128]{1,0:T(8,128)S(1)}, u32[]{:S(2)}, u32[]{:S(2)}) collective-permute-start(f32[256,128]{1,0:T(8,128)S(1)} %add_add_fusion), channel_id=1, source_target_pairs={{0,2},{1,3},{2,0},{3,1},{4,6},{5,7},{6,4},{7,5},{8,10},{9,11},{10,... | collective-permute-start | bytes 393224 | tf_op jit(solution)/shard_map/ppermute | solution.py:299
  53.7 0.6 collective-permute-start.16
  54.3 2.4 %collective-permute-done.15 = f32[256,128]{1,0:T(8,128)S(1)} collective-permute-done((f32[256,128]{1,0:T(8,128)S(1)}, f32[256,128]{1,0:T(8,128)S(1)}, u32[]{:S(2)}, u32[]{:S(2)}) %collective-permute-start.15) | collective-permute-done | bytes 131104 | tf_op jit(solution)/shard_map/ppermute | solution.py:299
  56.8 0.7 %resolve.2.refs_12_ = f32[256,512]{1,0:T(8,128)S(1)} custom-call(bf16[128,512]{1,0:T(8,128)(2,1)S(1)} %get-tuple-element.113.refs_0_, bf16[128,512]{1,0:T(8,128)(2,1)S(1)} %get-tuple-element.112.refs_1_, bf16[128,512]{1,0:T(8,128)(2,1)S(1)} %get-tuple-element.111.refs_2_, bf16[128,512]{1,0:T(8,128)(2,1)S(1)} %get-tuple-element.110.refs_3_, ...), custom_call_target="tpu_custom_call" | custom-call | flops 1024 | bytes 1024 | tf_op jit(solution)/shard_map/resolve/pallas_call | solution.py:240
  57.5 0.8 %collective-permute-done.17.refs_11_ = f32[512,128]{1,0:T(8,128)S(1)} collective-permute-done((f32[512,128]{1,0:T(8,128)S(1)}, f32[512,128]{1,0:T(8,128)S(1)}, u32[]{:S(2)}, u32[]{:S(2)}) %collective-permute-start.17) | collective-permute-done | bytes 262176 | tf_op jit(solution)/shard_map/ppermute | solution.py:299
  58.3 1.5 %resolve.3 = f32[256,512]{1,0:T(8,128)} custom-call(bf16[128,512]{1,0:T(8,128)(2,1)S(1)} %get-tuple-element.122.refs_0_, bf16[128,512]{1,0:T(8,128)(2,1)S(1)} %get-tuple-element.121.refs_1_, bf16[128,512]{1,0:T(8,128)(2,1)S(1)} %get-tuple-element.120.refs_2_, bf16[128,512]{1,0:T(8,128)(2,1)S(1)} %get-tuple-element.119.refs_3_, ...), custom_call_target="tpu_custom_call" | custom-call | flops 1024 | bytes 1024 | tf_op jit(solution)/shard_map/resolve/pallas_call | solution.py:240
  (65 shorter events, 2.9 us)
Async XLA Ops:
  0.0 5.0 %copy-start.3 = (f32[128,6,512]{2,0,1:T(8,128)S(1)}, f32[128,6,512]{2,0,1:T(8,128)}, u32[]{:S(2)}) copy-start(f32[128,6,512]{2,0,1:T(8,128)} %param.6) | copy-start | bytes 4718596
  0.0 6.3 %copy-start.1 = (f32[16]{0:T(128)S(1)}, f32[16]{0:T(128)}, u32[]{:S(2)}) copy-start(f32[16]{0:T(128)} %rock_ref.7) | copy-start | bytes 196
  0.0 6.3 %copy-start = (f32[2,4,6]{2,1,0:T(4,128)S(1)}, f32[2,4,6]{2,1,0:T(4,128)}, u32[]{:S(2)}) copy-start(f32[2,4,6]{2,1,0:T(4,128)} %dirs_ref.7) | copy-start | bytes 580
  1.9 10.0 %collective-permute-start = (f32[97,8,128]{2,1,0:T(8,128)S(1)}, f32[97,8,128]{2,1,0:T(8,128)S(1)}, u32[]{:S(2)}, u32[]{:S(2)}) collective-permute-start(f32[97,8,128]{2,1,0:T(8,128)S(1)} %pad_maximum_fusion.1.refs_4_), channel_id=1, source_target_pairs={{0,8},{1,5},{2,10},{3,7},{4,12},{5,1},{6,14},{7,3},{8,0},{9,13},{1... | collective-permute-start | bytes 1191944 | tf_op jit(solution)/shard_map/ppermute | solution.py:297
  5.8 10.2 %collective-permute-start.3 = (f32[96,8,128]{2,1,0:T(8,128)S(1)}, f32[96,8,128]{2,1,0:T(8,128)S(1)}, u32[]{:S(2)}, u32[]{:S(2)}) collective-permute-start(f32[96,8,128]{2,1,0:T(8,128)S(1)} %get-tuple-element.48.refs_5_), channel_id=1, source_target_pairs={{0,8},{1,5},{2,10},{3,7},{4,12},{5,1},{6,14},{7,3},{8,0},{9,13},{1... | collective-permute-start | bytes 1179656 | tf_op jit(solution)/shard_map/ppermute | solution.py:297
  9.7 16.8 %collective-permute-start.1 = (f32[96,8,128]{2,1,0:T(8,128)S(1)}, f32[96,8,128]{2,1,0:T(8,128)S(1)}, u32[]{:S(2)}, u32[]{:S(2)}) collective-permute-start(f32[96,8,128]{2,1,0:T(8,128)S(1)} %get-tuple-element.61.refs_6_), channel_id=1, source_target_pairs={{0,8},{1,5},{2,10},{3,7},{4,12},{5,1},{6,14},{7,3},{8,0},{9,13},{1... | collective-permute-start | bytes 1179656 | tf_op jit(solution)/shard_map/ppermute | solution.py:297
  11.8 17.2 %copy-start.2 = (bf16[2048,512]{1,0:T(8,128)(2,1)S(1)}, bf16[2048,512]{1,0:T(8,128)(2,1)}, u32[]{:S(2)}) copy-start(bf16[2048,512]{1,0:T(8,128)(2,1)} %param.11) | copy-start | bytes 6291460
  14.4 9.6 %collective-permute-start.2 = (f32[512,128]{1,0:T(8,128)S(1)}, f32[512,128]{1,0:T(8,128)S(1)}, u32[]{:S(2)}, u32[]{:S(2)}) collective-permute-start(f32[512,128]{1,0:T(8,128)S(1)} %get-tuple-element.56), channel_id=1, source_target_pairs={{0,4},{1,9},{2,6},{3,11},{4,0},{5,13},{6,2},{7,15},{8,12},{9,1},{1... | collective-permute-start | bytes 786440 | tf_op jit(solution)/shard_map/ppermute | solution.py:297
  18.2 11.1 %collective-permute-start.7 = (f32[512,128]{1,0:T(8,128)S(1)}, f32[512,128]{1,0:T(8,128)S(1)}, u32[]{:S(2)}, u32[]{:S(2)}) collective-permute-start(f32[512,128]{1,0:T(8,128)S(1)} %get-tuple-element.59), channel_id=1, source_target_pairs={{0,4},{1,9},{2,6},{3,11},{4,0},{5,13},{6,2},{7,15},{8,12},{9,1},{1... | collective-permute-start | bytes 786440 | tf_op jit(solution)/shard_map/ppermute | solution.py:297
  19.1 13.3 %collective-permute-start.6 = (f32[97,8,128]{2,1,0:T(8,128)S(1)}, f32[97,8,128]{2,1,0:T(8,128)S(1)}, u32[]{:S(2)}, u32[]{:S(2)}) collective-permute-start(f32[97,8,128]{2,1,0:T(8,128)S(1)} %pad_maximum_fusion.refs_7_), channel_id=1, source_target_pairs={{0,4},{4,0},{8,12},{12,8},{16,20},{20,16},{24,28},{28,24},{1,5},{5... | collective-permute-start | bytes 1191944 | tf_op jit(solution)/shard_map/ppermute | solution.py:299
  24.0 12.8 %collective-permute-start.5 = (f32[256,128]{1,0:T(8,128)S(1)}, f32[256,128]{1,0:T(8,128)S(1)}, u32[]{:S(2)}, u32[]{:S(2)}) collective-permute-start(f32[256,128]{1,0:T(8,128)S(1)} %slice_add_fusion.3), channel_id=1, source_target_pairs={{0,16},{4,20},{8,24},{12,28},{16,0},{20,4},{24,8},{28,12},{1,17},{... | collective-permute-start | bytes 393224 | tf_op jit(solution)/shard_map/ppermute | solution.py:299
  28.6 9.8 %collective-permute-start.4 = (f32[512,128]{1,0:T(8,128)S(1)}, f32[512,128]{1,0:T(8,128)S(1)}, u32[]{:S(2)}, u32[]{:S(2)}) collective-permute-start(f32[512,128]{1,0:T(8,128)S(1)} %get-tuple-element.65), channel_id=1, source_target_pairs={{0,4},{1,9},{2,6},{3,11},{4,0},{5,13},{6,2},{7,15},{8,12},{9,1},{1... | collective-permute-start | bytes 786440 | tf_op jit(solution)/shard_map/ppermute | solution.py:297
  29.3 11.9 %collective-permute-start.11 = (f32[256,128]{1,0:T(8,128)S(1)}, f32[256,128]{1,0:T(8,128)S(1)}, u32[]{:S(2)}, u32[]{:S(2)}) collective-permute-start(f32[256,128]{1,0:T(8,128)S(1)} %slice_add_fusion.2), channel_id=1, source_target_pairs={{0,16},{4,20},{8,24},{12,28},{16,0},{20,4},{24,8},{28,12},{1,17},{... | collective-permute-start | bytes 393224 | tf_op jit(solution)/shard_map/ppermute | solution.py:299
  35.0 9.4 %collective-permute-start.9 = (f32[512,128]{1,0:T(8,128)S(1)}, f32[512,128]{1,0:T(8,128)S(1)}, u32[]{:S(2)}, u32[]{:S(2)}) collective-permute-start(f32[512,128]{1,0:T(8,128)S(1)} %get-tuple-element.74), channel_id=1, source_target_pairs={{0,8},{4,12},{8,0},{12,4},{16,24},{20,28},{24,16},{28,20},{1,9},{5... | collective-permute-start | bytes 786440 | tf_op jit(solution)/shard_map/ppermute | solution.py:299
  36.9 5.0 %collective-permute-start.10 = (f32[256,128]{1,0:T(8,128)S(1)}, f32[256,128]{1,0:T(8,128)S(1)}, u32[]{:S(2)}, u32[]{:S(2)}) collective-permute-start(f32[256,128]{1,0:T(8,128)S(1)} %add_add_fusion.3), channel_id=1, source_target_pairs={{0,2},{1,3},{2,0},{3,1},{4,6},{5,7},{6,4},{7,5},{8,10},{9,11},{10,... | collective-permute-start | bytes 393224 | tf_op jit(solution)/shard_map/ppermute | solution.py:299
  38.5 7.3 %collective-permute-start.8 = (f32[256,128]{1,0:T(8,128)S(1)}, f32[256,128]{1,0:T(8,128)S(1)}, u32[]{:S(2)}, u32[]{:S(2)}) collective-permute-start(f32[256,128]{1,0:T(8,128)S(1)} %slice_add_fusion.1), channel_id=1, source_target_pairs={{0,16},{4,20},{8,24},{12,28},{16,0},{20,4},{24,8},{28,12},{1,17},{... | collective-permute-start | bytes 393224 | tf_op jit(solution)/shard_map/ppermute | solution.py:299
  41.2 6.2 %collective-permute-start.13 = (f32[256,128]{1,0:T(8,128)S(1)}, f32[256,128]{1,0:T(8,128)S(1)}, u32[]{:S(2)}, u32[]{:S(2)}) collective-permute-start(f32[256,128]{1,0:T(8,128)S(1)} %add_add_fusion.1), channel_id=1, source_target_pairs={{0,2},{1,3},{2,0},{3,1},{4,6},{5,7},{6,4},{7,5},{8,10},{9,11},{10,... | collective-permute-start | bytes 393224 | tf_op jit(solution)/shard_map/ppermute | solution.py:299
  41.8 14.9 %collective-permute-start.18 = (f32[512,128]{1,0:T(8,128)S(1)}, f32[512,128]{1,0:T(8,128)S(1)}, u32[]{:S(2)}, u32[]{:S(2)}) collective-permute-start(f32[512,128]{1,0:T(8,128)S(1)} %pad_maximum_fusion.4.refs_8_), channel_id=1, source_target_pairs={{0,1},{1,0},{2,3},{3,2},{4,5},{5,4},{6,7},{7,6},{8,9},{9,8},{10,11... | collective-permute-start | bytes 786440 | tf_op jit(solution)/shard_map/ppermute | solution.py:299
  44.4 7.2 %collective-permute-start.12 = (f32[256,128]{1,0:T(8,128)S(1)}, f32[256,128]{1,0:T(8,128)S(1)}, u32[]{:S(2)}, u32[]{:S(2)}) collective-permute-start(f32[256,128]{1,0:T(8,128)S(1)} %slice_add_fusion), channel_id=1, source_target_pairs={{0,16},{4,20},{8,24},{12,28},{16,0},{20,4},{24,8},{28,12},{1,17},{... | collective-permute-start | bytes 393224 | tf_op jit(solution)/shard_map/ppermute | solution.py:299
  45.8 8.4 %collective-permute-start.14 = (f32[256,128]{1,0:T(8,128)S(1)}, f32[256,128]{1,0:T(8,128)S(1)}, u32[]{:S(2)}, u32[]{:S(2)}) collective-permute-start(f32[256,128]{1,0:T(8,128)S(1)} %add_add_fusion.2), channel_id=1, source_target_pairs={{0,2},{1,3},{2,0},{3,1},{4,6},{5,7},{6,4},{7,5},{8,10},{9,11},{10,... | collective-permute-start | bytes 393224 | tf_op jit(solution)/shard_map/ppermute | solution.py:299
  51.6 5.0 %collective-permute-start.15 = (f32[256,128]{1,0:T(8,128)S(1)}, f32[256,128]{1,0:T(8,128)S(1)}, u32[]{:S(2)}, u32[]{:S(2)}) collective-permute-start(f32[256,128]{1,0:T(8,128)S(1)} %add_add_fusion), channel_id=1, source_target_pairs={{0,2},{1,3},{2,0},{3,1},{4,6},{5,7},{6,4},{7,5},{8,10},{9,11},{10,... | collective-permute-start | bytes 393224 | tf_op jit(solution)/shard_map/ppermute | solution.py:299
  53.6 3.2 %collective-permute-start.19 = (f32[512,128]{1,0:T(8,128)S(1)}, f32[512,128]{1,0:T(8,128)S(1)}, u32[]{:S(2)}, u32[]{:S(2)}) collective-permute-start(f32[512,128]{1,0:T(8,128)S(1)} %pad_maximum_fusion.5.refs_10_), channel_id=1, source_target_pairs={{0,1},{1,0},{2,3},{3,2},{4,5},{5,4},{6,7},{7,6},{8,9},{9,8},{10,11... | collective-permute-start | bytes 786440 | tf_op jit(solution)/shard_map/ppermute | solution.py:299
  53.7 3.8 %collective-permute-start.16 = (f32[512,128]{1,0:T(8,128)S(1)}, f32[512,128]{1,0:T(8,128)S(1)}, u32[]{:S(2)}, u32[]{:S(2)}) collective-permute-start(f32[512,128]{1,0:T(8,128)S(1)} %pad_maximum_fusion.2.refs_8_), channel_id=1, source_target_pairs={{0,1},{1,0},{2,3},{3,2},{4,5},{5,4},{6,7},{7,6},{8,9},{9,8},{10,11... | collective-permute-start | bytes 786440 | tf_op jit(solution)/shard_map/ppermute | solution.py:299
  56.7 1.6 %collective-permute-start.17 = (f32[512,128]{1,0:T(8,128)S(1)}, f32[512,128]{1,0:T(8,128)S(1)}, u32[]{:S(2)}, u32[]{:S(2)}) collective-permute-start(f32[512,128]{1,0:T(8,128)S(1)} %pad_maximum_fusion.3.refs_10_), channel_id=1, source_target_pairs={{0,1},{1,0},{2,3},{3,2},{4,5},{5,4},{6,7},{7,6},{8,9},{9,8},{10,11... | collective-permute-start | bytes 786440 | tf_op jit(solution)/shard_map/ppermute | solution.py:299

commit v8 on v7

--- a/solution.py
+++ b/solution.py
@@ -30,14 +30,14 @@
     ("first", 3),
     ("final", 0),
     ("middle", 2),
+    ("arrive", 0),
     ("final", 1),
-    ("arrive", 0),
     ("middle", 3),
     ("final", 2),
     ("arrive", 1),
-    ("final", 3),
     ("near", 0, 1),
     ("far", 0, 1),
+    ("final", 3),
     ("multiply", 0, 1),
     ("near", 2, 3),
     ("arrive", 2),

time: 59.7 us -> 59.7 us (level)
  starting transfers between devices: 23.7 us -> 27 us
  Pallas kernels: 17.8 us -> 14.6 us
    ppermute x14, starting transfers between devices: 16.6 us -> 18.2 us  [swap(): lax.ppermute(value, axis, [(i, i ^ 1 << number) for i in range(lax.axis_s...]
    ppermute x6, starting transfers between devices: 7.19 us -> 8.83 us  [swap(): return lax.ppermute(value, ('slab', 'rock'), pairs)]
    pallas_call x4, Pallas kernels: 8.54 us -> 6.92 us  [other_images(): pl.pallas_call(kernel, out_shape=[jax.ShapeDtypeStruct((half, LANES), jnp...]
    pallas_call x2, Pallas kernels: 7.02 us -> 5.46 us  [own_images(): pl.pallas_call(kernel, out_shape=[jax.ShapeDtypeStruct((rows, LANES), jnp...]
  transfers between devices with their start and end apart: 20 -> 20, of which waited for: 6 -> 8; matrix products, arithmetic and copies ran while one was open for 6% -> 6% of each run, Pallas kernels for 27% -> 22%
where the time goes in v8:
time: 59.7 us; the launch traced here: 59.4 us
  starting transfers between devices  27 us (45%)
  Pallas kernels  14.6 us (24%)
  waiting for transfers between devices  12 us (20%)
  other arithmetic  3.39 us (6%)
  local copies, waits for them, and re-layouts  2.02 us (3%)
    ppermute x14, starting transfers between devices, swap(): lax.ppermute(value, axis, [(i, i ^ 1 << number) for i in range(lax.axis_s...  18.2 us
    ppermute x14, waiting for transfers between devices, swap(): lax.ppermute(value, axis, [(i, i ^ 1 << number) for i in range(lax.axis_s...  12 us
    ppermute x6, starting transfers between devices, swap(): return lax.ppermute(value, ('slab', 'rock'), pairs)  8.83 us
    pallas_call x4, Pallas kernels, other_images(): pl.pallas_call(kernel, out_shape=[jax.ShapeDtypeStruct((half, LANES), jnp...  6.92 us
    pallas_call x2, Pallas kernels, own_images(): pl.pallas_call(kernel, out_shape=[jax.ShapeDtypeStruct((rows, LANES), jnp...  5.46 us
    pallas_call x2, Pallas kernels, resolve(): pl.pallas_call(kernel, out_shape=jax.ShapeDtypeStruct((unit, cols), jnp.f...  2.23 us
    slice x2, local copies, waits for them, and re-layouts, piece(): block = source[:, :, c * LANES:(c + 1) * LANES]  1.84 us
  transfers between devices with their start and end apart: 20, of which 8 were waited for; matrix products, arithmetic and copies ran while one was open for 6% of the time, Pallas kernels for 22%

profile of v8, /device:TPU:0, one launch (start us, length us, event | category | flops | bytes accessed | tf_op | source)
XLA Modules:
  0.0 59.4 jit_solution(8047895475311798389)
XLA Ops:
  0.0 0.8 %fusion.14 = (f32[2,128]{1,0:T(2,128)S(1)}, s32[2,128]{1,0:T(2,128)S(1)}) fusion(s32[2,128]{1,0:T(2,128)} %param.8, s32[2,128,1]{1,0,2:T(2,128)} %bitcast.54), kind=kLoop, calls=%fused_computation.109 | loop fusion | flops 768 | bytes 4096 | tf_op jit(solution)/shard_map/convert_element_type | solution.py:317
  0.8 1.0 %slice.94 = f32[96,8,128]{2,1,0:T(8,128)S(1)} slice(f32[96,8,512]{2,1,0:T(8,128)} %bitcast.52), slice={[0:96], [0:8], [0:128]} | slice | bytes 786432 | tf_op jit(solution)/shard_map/slice | solution.py:324
  1.9 3.1 %collective-permute-start = (f32[97,8,128]{2,1,0:T(8,128)S(1)}, f32[97,8,128]{2,1,0:T(8,128)S(1)}, u32[]{:S(2)}, u32[]{:S(2)}) collective-permute-start(f32[97,8,128]{2,1,0:T(8,128)S(1)} %pad_maximum_fusion.1.refs_4_), channel_id=1, source_target_pairs={{0,8},{1,5},{2,10},{3,7},{4,12},{5,1},{6,14},{7,3},{8,0},{9,13},{1... | collective-permute-start | bytes 1191944 | tf_op jit(solution)/shard_map/ppermute | solution.py:297
  5.0 0.8 %fusion.15 = (f32[96,8,128]{2,1,0:T(8,128)}, f32[96,8,128]{2,1,0:T(8,128)S(1)}, f32[96,8,128]{2,1,0:T(8,128)S(1)}) fusion(f32[96,8,512]{2,1,0:T(8,128)S(1)} %bitcast.53), kind=kLoop, calls=%fused_computation.110 | loop fusion | bytes 2359296 | tf_op jit(solution)/shard_map/slice | solution.py:324
  6.3 2.6 %own_images.2 = (f32[1040,128]{1,0:T(8,128)S(1)}, f32[1040,128]{1,0:T(8,128)S(1)}) custom-call(s32[2]{0:T(128)S(1)} %get-tuple-element.127.refs_0_.refs_2_, s32[2,128]{1,0:T(2,128)S(1)} %broadcast_add_fusion.3.refs_1_.refs_3_, f32[2,4,6]{2,1,0:T(4,128)S(1)} %copy-done, f32[16]{0:T(128)S(1)} %copy-done.1, f32[97,8,128]{2,1,0:T(8,128)S(1)} %pad_maximum_fusion.1.refs_4_, ...), custom_call_target="tpu_custom_call" | custom-call | flops 1024 | bytes 1024 | tf_op jit(solution)/shard_map/own_images/pallas_call | solution.py:179
  9.0 2.7 %collective-permute-start.1 = (f32[96,8,128]{2,1,0:T(8,128)S(1)}, f32[96,8,128]{2,1,0:T(8,128)S(1)}, u32[]{:S(2)}, u32[]{:S(2)}) collective-permute-start(f32[96,8,128]{2,1,0:T(8,128)S(1)} %get-tuple-element.61.refs_6_), channel_id=1, source_target_pairs={{0,8},{1,5},{2,10},{3,7},{4,12},{5,1},{6,14},{7,3},{8,0},{9,13},{1... | collective-permute-start | bytes 1179656 | tf_op jit(solution)/shard_map/ppermute | solution.py:297
  11.7 1.0 %pad_maximum_fusion.refs_7_ = f32[97,8,128]{2,1,0:T(8,128)S(1)} fusion(f32[1,8,128]{2,1,0:T(8,128)S(1)} %pad_bitcast_fusion, f32[96,8,128]{2,1,0:T(8,128)} %get-tuple-element.123), kind=kLoop, calls=%fused_computation | loop fusion | flops 99328 | bytes 794624 | tf_op jit(solution)/shard_map/concatenate | solution.py:327
  13.1 1.7 %other_images.4 = (f32[512,128]{1,0:T(8,128)S(1)}, f32[512,128]{1,0:T(8,128)S(1)}) custom-call(s32[2]{0:T(128)S(1)} %get-tuple-element.101.count_ref, s32[2,128]{1,0:T(2,128)S(1)} %broadcast_add_fusion.2.list_ref, f32[2,4,6]{2,1,0:T(4,128)S(1)} %copy-done, f32[16]{0:T(128)S(1)} %copy-done.1, f32[97,8,128]{2,1,0:T(8,128)S(1)} %collective-permute-done.strain_ref, ...), custom_call_target="tpu_custom_call" | custom-call | flops 1024 | bytes 1024 | tf_op jit(solution)/shard_map/other_images/pallas_call | solution.py:206
  14.8 1.5 %collective-permute-start.2 = (f32[512,128]{1,0:T(8,128)S(1)}, f32[512,128]{1,0:T(8,128)S(1)}, u32[]{:S(2)}, u32[]{:S(2)}) collective-permute-start(f32[512,128]{1,0:T(8,128)S(1)} %get-tuple-element.56), channel_id=1, source_target_pairs={{0,4},{1,9},{2,6},{3,11},{4,0},{5,13},{6,2},{7,15},{8,12},{9,1},{1... | collective-permute-start | bytes 786440 | tf_op jit(solution)/shard_map/ppermute | solution.py:297
  16.4 1.7 %other_images.5 = (f32[512,128]{1,0:T(8,128)S(1)}, f32[512,128]{1,0:T(8,128)S(1)}) custom-call(s32[2]{0:T(128)S(1)} %get-tuple-element.101.count_ref, s32[2,128]{1,0:T(2,128)S(1)} %broadcast_add_fusion.2.list_ref, f32[2,4,6]{2,1,0:T(4,128)S(1)} %copy-done, f32[16]{0:T(128)S(1)} %copy-done.1, f32[96,8,128]{2,1,0:T(8,128)S(1)} %collective-permute-done.3.strain_ref, ...), custom_call_target="tpu_custom_call" | custom-call | flops 1024 | bytes 1024 | tf_op jit(solution)/shard_map/other_images/pallas_call | solution.py:206
  18.1 0.8 %collective-permute-start.7 = (f32[512,128]{1,0:T(8,128)S(1)}, f32[512,128]{1,0:T(8,128)S(1)}, u32[]{:S(2)}, u32[]{:S(2)}) collective-permute-start(f32[512,128]{1,0:T(8,128)S(1)} %get-tuple-element.59), channel_id=1, source_target_pairs={{0,4},{1,9},{2,6},{3,11},{4,0},{5,13},{6,2},{7,15},{8,12},{9,1},{1... | collective-permute-start | bytes 786440 | tf_op jit(solution)/shard_map/ppermute | solution.py:297
  18.9 1.3 %collective-permute-start.6 = (f32[97,8,128]{2,1,0:T(8,128)S(1)}, f32[97,8,128]{2,1,0:T(8,128)S(1)}, u32[]{:S(2)}, u32[]{:S(2)}) collective-permute-start(f32[97,8,128]{2,1,0:T(8,128)S(1)} %pad_maximum_fusion.refs_7_), channel_id=1, source_target_pairs={{0,4},{4,0},{8,12},{12,8},{16,20},{20,16},{24,28},{28,24},{1,5},{5... | collective-permute-start | bytes 1191944 | tf_op jit(solution)/shard_map/ppermute | solution.py:299
  20.3 2.8 %own_images.3 = (f32[1040,128]{1,0:T(8,128)S(1)}, f32[1040,128]{1,0:T(8,128)S(1)}) custom-call(s32[2]{0:T(128)S(1)} %get-tuple-element.97.refs_0_, s32[2,128]{1,0:T(2,128)S(1)} %broadcast_add_fusion.1.refs_1_, s32[2]{0:T(128)S(1)} %get-tuple-element.127.refs_0_.refs_2_, s32[2,128]{1,0:T(2,128)S(1)} %broadcast_add_fusion.3.refs_1_.refs_3_, ...), custom_call_target="tpu_custom_call" | custom-call | flops 1024 | bytes 1024 | tf_op jit(solution)/shard_map/own_images/pallas_call | solution.py:179
  23.1 2.8 %collective-permute-start.5 = (f32[256,128]{1,0:T(8,128)S(1)}, f32[256,128]{1,0:T(8,128)S(1)}, u32[]{:S(2)}, u32[]{:S(2)}) collective-permute-start(f32[256,128]{1,0:T(8,128)S(1)} %slice_add_fusion.3), channel_id=1, source_target_pairs={{0,16},{4,20},{8,24},{12,28},{16,0},{20,4},{24,8},{28,12},{1,17},{... | collective-permute-start | bytes 393224 | tf_op jit(solution)/shard_map/ppermute | solution.py:299
  26.0 1.7 %other_images.6 = (f32[512,128]{1,0:T(8,128)S(1)}, f32[512,128]{1,0:T(8,128)S(1)}) custom-call(s32[2]{0:T(128)S(1)} %get-tuple-element.101.count_ref, s32[2,128]{1,0:T(2,128)S(1)} %broadcast_add_fusion.2.list_ref, f32[2,4,6]{2,1,0:T(4,128)S(1)} %copy-done, f32[16]{0:T(128)S(1)} %copy-done.1, f32[96,8,128]{2,1,0:T(8,128)S(1)} %collective-permute-done.1.strain_ref, ...), custom_call_target="tpu_custom_call" | custom-call | flops 1024 | bytes 1024 | tf_op jit(solution)/shard_map/other_images/pallas_call | solution.py:206
  28.5 2.1 %collective-permute-start.10 = (f32[256,128]{1,0:T(8,128)S(1)}, f32[256,128]{1,0:T(8,128)S(1)}, u32[]{:S(2)}, u32[]{:S(2)}) collective-permute-start(f32[256,128]{1,0:T(8,128)S(1)} %slice_add_fusion.2), channel_id=1, source_target_pairs={{0,16},{4,20},{8,24},{12,28},{16,0},{20,4},{24,8},{28,12},{1,17},{... | collective-permute-start | bytes 393224 | tf_op jit(solution)/shard_map/ppermute | solution.py:299
  30.6 2.0 %collective-permute-done.6.strain_ref = f32[97,8,128]{2,1,0:T(8,128)S(1)} collective-permute-done((f32[97,8,128]{2,1,0:T(8,128)S(1)}, f32[97,8,128]{2,1,0:T(8,128)S(1)}, u32[]{:S(2)}, u32[]{:S(2)}) %collective-permute-start.6) | collective-permute-done | bytes 397344 | tf_op jit(solution)/shard_map/ppermute | solution.py:299
  33.0 1.9 %other_images.7 = (f32[512,128]{1,0:T(8,128)S(1)}, f32[512,128]{1,0:T(8,128)S(1)}) custom-call(s32[2]{0:T(128)S(1)} %get-tuple-element.93.count_ref, s32[2,128]{1,0:T(2,128)S(1)} %broadcast_add_fusion.list_ref, f32[2,4,6]{2,1,0:T(4,128)S(1)} %copy-done, f32[16]{0:T(128)S(1)} %copy-done.1, f32[97,8,128]{2,1,0:T(8,128)S(1)} %collective-permute-done.6.strain_ref, ...), custom_call_target="tpu_custom_call" | custom-call | flops 1024 | bytes 1024 | tf_op jit(solution)/shard_map/other_images/pallas_call | solution.py:206
  34.8 1.8 %collective-permute-start.9 = (f32[512,128]{1,0:T(8,128)S(1)}, f32[512,128]{1,0:T(8,128)S(1)}, u32[]{:S(2)}, u32[]{:S(2)}) collective-permute-start(f32[512,128]{1,0:T(8,128)S(1)} %get-tuple-element.74), channel_id=1, source_target_pairs={{0,8},{4,12},{8,0},{12,4},{16,24},{20,28},{24,16},{28,20},{1,9},{5... | collective-permute-start | bytes 786440 | tf_op jit(solution)/shard_map/ppermute | solution.py:299
  36.6 1.6 %collective-permute-start.11 = (f32[256,128]{1,0:T(8,128)S(1)}, f32[256,128]{1,0:T(8,128)S(1)}, u32[]{:S(2)}, u32[]{:S(2)}) collective-permute-start(f32[256,128]{1,0:T(8,128)S(1)} %add_add_fusion.3), channel_id=1, source_target_pairs={{0,2},{1,3},{2,0},{3,1},{4,6},{5,7},{6,4},{7,5},{8,10},{9,11},{10,... | collective-permute-start | bytes 393224 | tf_op jit(solution)/shard_map/ppermute | solution.py:299
  38.2 2.6 %collective-permute-start.8 = (f32[256,128]{1,0:T(8,128)S(1)}, f32[256,128]{1,0:T(8,128)S(1)}, u32[]{:S(2)}, u32[]{:S(2)}) collective-permute-start(f32[256,128]{1,0:T(8,128)S(1)} %slice_add_fusion.1), channel_id=1, source_target_pairs={{0,16},{4,20},{8,24},{12,28},{16,0},{20,4},{24,8},{28,12},{1,17},{... | collective-permute-start | bytes 393224 | tf_op jit(solution)/shard_map/ppermute | solution.py:299
  40.8 0.8 %collective-permute-done.11 = f32[256,128]{1,0:T(8,128)S(1)} collective-permute-done((f32[256,128]{1,0:T(8,128)S(1)}, f32[256,128]{1,0:T(8,128)S(1)}, u32[]{:S(2)}, u32[]{:S(2)}) %collective-permute-start.11) | collective-permute-done | bytes 131104 | tf_op jit(solution)/shard_map/ppermute | solution.py:299
  41.7 1.6 %collective-permute-start.13 = (f32[256,128]{1,0:T(8,128)S(1)}, f32[256,128]{1,0:T(8,128)S(1)}, u32[]{:S(2)}, u32[]{:S(2)}) collective-permute-start(f32[256,128]{1,0:T(8,128)S(1)} %add_add_fusion.1), channel_id=1, source_target_pairs={{0,2},{1,3},{2,0},{3,1},{4,6},{5,7},{6,4},{7,5},{8,10},{9,11},{10,... | collective-permute-start | bytes 393224 | tf_op jit(solution)/shard_map/ppermute | solution.py:299
  43.3 0.7 %collective-permute-done.9 = f32[512,128]{1,0:T(8,128)S(1)} collective-permute-done((f32[512,128]{1,0:T(8,128)S(1)}, f32[512,128]{1,0:T(8,128)S(1)}, u32[]{:S(2)}, u32[]{:S(2)}) %collective-permute-start.9) | collective-permute-done | bytes 262176 | tf_op jit(solution)/shard_map/ppermute | solution.py:299
  44.0 2.0 %collective-permute-start.12 = (f32[256,128]{1,0:T(8,128)S(1)}, f32[256,128]{1,0:T(8,128)S(1)}, u32[]{:S(2)}, u32[]{:S(2)}) collective-permute-start(f32[256,128]{1,0:T(8,128)S(1)} %slice_add_fusion), channel_id=1, source_target_pairs={{0,16},{4,20},{8,24},{12,28},{16,0},{20,4},{24,8},{28,12},{1,17},{... | collective-permute-start | bytes 393224 | tf_op jit(solution)/shard_map/ppermute | solution.py:299
  45.9 2.0 %collective-permute-done.8 = f32[256,128]{1,0:T(8,128)S(1)} collective-permute-done((f32[256,128]{1,0:T(8,128)S(1)}, f32[256,128]{1,0:T(8,128)S(1)}, u32[]{:S(2)}, u32[]{:S(2)}) %collective-permute-start.8) | collective-permute-done | bytes 131104 | tf_op jit(solution)/shard_map/ppermute | solution.py:299
  48.1 3.1 %collective-permute-done.12 = f32[256,128]{1,0:T(8,128)S(1)} collective-permute-done((f32[256,128]{1,0:T(8,128)S(1)}, f32[256,128]{1,0:T(8,128)S(1)}, u32[]{:S(2)}, u32[]{:S(2)}) %collective-permute-start.12) | collective-permute-done | bytes 131104 | tf_op jit(solution)/shard_map/ppermute | solution.py:299
  51.2 1.8 %collective-permute-start.15 = (f32[256,128]{1,0:T(8,128)S(1)}, f32[256,128]{1,0:T(8,128)S(1)}, u32[]{:S(2)}, u32[]{:S(2)}) collective-permute-start(f32[256,128]{1,0:T(8,128)S(1)} %add_add_fusion), channel_id=1, source_target_pairs={{0,2},{1,3},{2,0},{3,1},{4,6},{5,7},{6,4},{7,5},{8,10},{9,11},{10,... | collective-permute-start | bytes 393224 | tf_op jit(solution)/shard_map/ppermute | solution.py:299
  53.7 2.6 %collective-permute-done.15 = f32[256,128]{1,0:T(8,128)S(1)} collective-permute-done((f32[256,128]{1,0:T(8,128)S(1)}, f32[256,128]{1,0:T(8,128)S(1)}, u32[]{:S(2)}, u32[]{:S(2)}) %collective-permute-start.15) | collective-permute-done | bytes 131104 | tf_op jit(solution)/shard_map/ppermute | solution.py:299
  56.3 0.7 %resolve.2.refs_12_ = f32[256,512]{1,0:T(8,128)S(1)} custom-call(bf16[128,512]{1,0:T(8,128)(2,1)S(1)} %get-tuple-element.113.refs_0_, bf16[128,512]{1,0:T(8,128)(2,1)S(1)} %get-tuple-element.112.refs_1_, bf16[128,512]{1,0:T(8,128)(2,1)S(1)} %get-tuple-element.111.refs_2_, bf16[128,512]{1,0:T(8,128)(2,1)S(1)} %get-tuple-element.110.refs_3_, ...), custom_call_target="tpu_custom_call" | custom-call | flops 1024 | bytes 1024 | tf_op jit(solution)/shard_map/resolve/pallas_call | solution.py:240
  57.1 0.8 %collective-permute-done.17.refs_11_ = f32[512,128]{1,0:T(8,128)S(1)} collective-permute-done((f32[512,128]{1,0:T(8,128)S(1)}, f32[512,128]{1,0:T(8,128)S(1)}, u32[]{:S(2)}, u32[]{:S(2)}) %collective-permute-start.17) | collective-permute-done | bytes 262176 | tf_op jit(solution)/shard_map/ppermute | solution.py:299
  57.8 1.5 %resolve.3 = f32[256,512]{1,0:T(8,128)} custom-call(bf16[128,512]{1,0:T(8,128)(2,1)S(1)} %get-tuple-element.122.refs_0_, bf16[128,512]{1,0:T(8,128)(2,1)S(1)} %get-tuple-element.121.refs_1_, bf16[128,512]{1,0:T(8,128)(2,1)S(1)} %get-tuple-element.120.refs_2_, bf16[128,512]{1,0:T(8,128)(2,1)S(1)} %get-tuple-element.119.refs_3_, ...), custom_call_target="tpu_custom_call" | custom-call | flops 1024 | bytes 1024 | tf_op jit(solution)/shard_map/resolve/pallas_call | solution.py:240
  (65 shorter events, 3.2 us)
Async XLA Ops:
  0.0 5.0 %copy-start.3 = (f32[128,6,512]{2,0,1:T(8,128)S(1)}, f32[128,6,512]{2,0,1:T(8,128)}, u32[]{:S(2)}) copy-start(f32[128,6,512]{2,0,1:T(8,128)} %param.6) | copy-start | bytes 4718596
  0.0 6.3 %copy-start.1 = (f32[16]{0:T(128)S(1)}, f32[16]{0:T(128)}, u32[]{:S(2)}) copy-start(f32[16]{0:T(128)} %rock_ref.7) | copy-start | bytes 196
  0.0 6.3 %copy-start = (f32[2,4,6]{2,1,0:T(4,128)S(1)}, f32[2,4,6]{2,1,0:T(4,128)}, u32[]{:S(2)}) copy-start(f32[2,4,6]{2,1,0:T(4,128)} %dirs_ref.7) | copy-start | bytes 580
  1.9 10.8 %collective-permute-start = (f32[97,8,128]{2,1,0:T(8,128)S(1)}, f32[97,8,128]{2,1,0:T(8,128)S(1)}, u32[]{:S(2)}, u32[]{:S(2)}) collective-permute-start(f32[97,8,128]{2,1,0:T(8,128)S(1)} %pad_maximum_fusion.1.refs_4_), channel_id=1, source_target_pairs={{0,8},{1,5},{2,10},{3,7},{4,12},{5,1},{6,14},{7,3},{8,0},{9,13},{1... | collective-permute-start | bytes 1191944 | tf_op jit(solution)/shard_map/ppermute | solution.py:297
  5.8 10.6 %collective-permute-start.3 = (f32[96,8,128]{2,1,0:T(8,128)S(1)}, f32[96,8,128]{2,1,0:T(8,128)S(1)}, u32[]{:S(2)}, u32[]{:S(2)}) collective-permute-start(f32[96,8,128]{2,1,0:T(8,128)S(1)} %get-tuple-element.48.refs_5_), channel_id=1, source_target_pairs={{0,8},{1,5},{2,10},{3,7},{4,12},{5,1},{6,14},{7,3},{8,0},{9,13},{1... | collective-permute-start | bytes 1179656 | tf_op jit(solution)/shard_map/ppermute | solution.py:297
  9.0 17.0 %collective-permute-start.1 = (f32[96,8,128]{2,1,0:T(8,128)S(1)}, f32[96,8,128]{2,1,0:T(8,128)S(1)}, u32[]{:S(2)}, u32[]{:S(2)}) collective-permute-start(f32[96,8,128]{2,1,0:T(8,128)S(1)} %get-tuple-element.61.refs_6_), channel_id=1, source_target_pairs={{0,8},{1,5},{2,10},{3,7},{4,12},{5,1},{6,14},{7,3},{8,0},{9,13},{1... | collective-permute-start | bytes 1179656 | tf_op jit(solution)/shard_map/ppermute | solution.py:297
  12.7 15.6 %copy-start.2 = (bf16[2048,512]{1,0:T(8,128)(2,1)S(1)}, bf16[2048,512]{1,0:T(8,128)(2,1)}, u32[]{:S(2)}) copy-start(bf16[2048,512]{1,0:T(8,128)(2,1)} %param.11) | copy-start | bytes 6291460
  14.8 8.3 %collective-permute-start.2 = (f32[512,128]{1,0:T(8,128)S(1)}, f32[512,128]{1,0:T(8,128)S(1)}, u32[]{:S(2)}, u32[]{:S(2)}) collective-permute-start(f32[512,128]{1,0:T(8,128)S(1)} %get-tuple-element.56), channel_id=1, source_target_pairs={{0,4},{1,9},{2,6},{3,11},{4,0},{5,13},{6,2},{7,15},{8,12},{9,1},{1... | collective-permute-start | bytes 786440 | tf_op jit(solution)/shard_map/ppermute | solution.py:297
  18.1 10.4 %collective-permute-start.7 = (f32[512,128]{1,0:T(8,128)S(1)}, f32[512,128]{1,0:T(8,128)S(1)}, u32[]{:S(2)}, u32[]{:S(2)}) collective-permute-start(f32[512,128]{1,0:T(8,128)S(1)} %get-tuple-element.59), channel_id=1, source_target_pairs={{0,4},{1,9},{2,6},{3,11},{4,0},{5,13},{6,2},{7,15},{8,12},{9,1},{1... | collective-permute-start | bytes 786440 | tf_op jit(solution)/shard_map/ppermute | solution.py:297
  18.9 13.7 %collective-permute-start.6 = (f32[97,8,128]{2,1,0:T(8,128)S(1)}, f32[97,8,128]{2,1,0:T(8,128)S(1)}, u32[]{:S(2)}, u32[]{:S(2)}) collective-permute-start(f32[97,8,128]{2,1,0:T(8,128)S(1)} %pad_maximum_fusion.refs_7_), channel_id=1, source_target_pairs={{0,4},{4,0},{8,12},{12,8},{16,20},{20,16},{24,28},{28,24},{1,5},{5... | collective-permute-start | bytes 1191944 | tf_op jit(solution)/shard_map/ppermute | solution.py:299
  23.1 13.5 %collective-permute-start.5 = (f32[256,128]{1,0:T(8,128)S(1)}, f32[256,128]{1,0:T(8,128)S(1)}, u32[]{:S(2)}, u32[]{:S(2)}) collective-permute-start(f32[256,128]{1,0:T(8,128)S(1)} %slice_add_fusion.3), channel_id=1, source_target_pairs={{0,16},{4,20},{8,24},{12,28},{16,0},{20,4},{24,8},{28,12},{1,17},{... | collective-permute-start | bytes 393224 | tf_op jit(solution)/shard_map/ppermute | solution.py:299
  27.6 10.5 %collective-permute-start.4 = (f32[512,128]{1,0:T(8,128)S(1)}, f32[512,128]{1,0:T(8,128)S(1)}, u32[]{:S(2)}, u32[]{:S(2)}) collective-permute-start(f32[512,128]{1,0:T(8,128)S(1)} %get-tuple-element.65), channel_id=1, source_target_pairs={{0,4},{1,9},{2,6},{3,11},{4,0},{5,13},{6,2},{7,15},{8,12},{9,1},{1... | collective-permute-start | bytes 786440 | tf_op jit(solution)/shard_map/ppermute | solution.py:297
  28.5 13.2 %collective-permute-start.10 = (f32[256,128]{1,0:T(8,128)S(1)}, f32[256,128]{1,0:T(8,128)S(1)}, u32[]{:S(2)}, u32[]{:S(2)}) collective-permute-start(f32[256,128]{1,0:T(8,128)S(1)} %slice_add_fusion.2), channel_id=1, source_target_pairs={{0,16},{4,20},{8,24},{12,28},{16,0},{20,4},{24,8},{28,12},{1,17},{... | collective-permute-start | bytes 393224 | tf_op jit(solution)/shard_map/ppermute | solution.py:299
  34.8 9.1 %collective-permute-start.9 = (f32[512,128]{1,0:T(8,128)S(1)}, f32[512,128]{1,0:T(8,128)S(1)}, u32[]{:S(2)}, u32[]{:S(2)}) collective-permute-start(f32[512,128]{1,0:T(8,128)S(1)} %get-tuple-element.74), channel_id=1, source_target_pairs={{0,8},{4,12},{8,0},{12,4},{16,24},{20,28},{24,16},{28,20},{1,9},{5... | collective-permute-start | bytes 786440 | tf_op jit(solution)/shard_map/ppermute | solution.py:299
  36.6 5.1 %collective-permute-start.11 = (f32[256,128]{1,0:T(8,128)S(1)}, f32[256,128]{1,0:T(8,128)S(1)}, u32[]{:S(2)}, u32[]{:S(2)}) collective-permute-start(f32[256,128]{1,0:T(8,128)S(1)} %add_add_fusion.3), channel_id=1, source_target_pairs={{0,2},{1,3},{2,0},{3,1},{4,6},{5,7},{6,4},{7,5},{8,10},{9,11},{10,... | collective-permute-start | bytes 393224 | tf_op jit(solution)/shard_map/ppermute | solution.py:299
  38.2 9.8 %collective-permute-start.8 = (f32[256,128]{1,0:T(8,128)S(1)}, f32[256,128]{1,0:T(8,128)S(1)}, u32[]{:S(2)}, u32[]{:S(2)}) collective-permute-start(f32[256,128]{1,0:T(8,128)S(1)} %slice_add_fusion.1), channel_id=1, source_target_pairs={{0,16},{4,20},{8,24},{12,28},{16,0},{20,4},{24,8},{28,12},{1,17},{... | collective-permute-start | bytes 393224 | tf_op jit(solution)/shard_map/ppermute | solution.py:299
  41.7 6.4 %collective-permute-start.13 = (f32[256,128]{1,0:T(8,128)S(1)}, f32[256,128]{1,0:T(8,128)S(1)}, u32[]{:S(2)}, u32[]{:S(2)}) collective-permute-start(f32[256,128]{1,0:T(8,128)S(1)} %add_add_fusion.1), channel_id=1, source_target_pairs={{0,2},{1,3},{2,0},{3,1},{4,6},{5,7},{6,4},{7,5},{8,10},{9,11},{10,... | collective-permute-start | bytes 393224 | tf_op jit(solution)/shard_map/ppermute | solution.py:299
  44.0 7.2 %collective-permute-start.12 = (f32[256,128]{1,0:T(8,128)S(1)}, f32[256,128]{1,0:T(8,128)S(1)}, u32[]{:S(2)}, u32[]{:S(2)}) collective-permute-start(f32[256,128]{1,0:T(8,128)S(1)} %slice_add_fusion), channel_id=1, source_target_pairs={{0,16},{4,20},{8,24},{12,28},{16,0},{20,4},{24,8},{28,12},{1,17},{... | collective-permute-start | bytes 393224 | tf_op jit(solution)/shard_map/ppermute | solution.py:299
  48.0 5.7 %collective-permute-start.14 = (f32[256,128]{1,0:T(8,128)S(1)}, f32[256,128]{1,0:T(8,128)S(1)}, u32[]{:S(2)}, u32[]{:S(2)}) collective-permute-start(f32[256,128]{1,0:T(8,128)S(1)} %add_add_fusion.2), channel_id=1, source_target_pairs={{0,2},{1,3},{2,0},{3,1},{4,6},{5,7},{6,4},{7,5},{8,10},{9,11},{10,... | collective-permute-start | bytes 393224 | tf_op jit(solution)/shard_map/ppermute | solution.py:299
  51.2 5.0 %collective-permute-start.15 = (f32[256,128]{1,0:T(8,128)S(1)}, f32[256,128]{1,0:T(8,128)S(1)}, u32[]{:S(2)}, u32[]{:S(2)}) collective-permute-start(f32[256,128]{1,0:T(8,128)S(1)} %add_add_fusion), channel_id=1, source_target_pairs={{0,2},{1,3},{2,0},{3,1},{4,6},{5,7},{6,4},{7,5},{8,10},{9,11},{10,... | collective-permute-start | bytes 393224 | tf_op jit(solution)/shard_map/ppermute | solution.py:299
  53.0 3.3 %collective-permute-start.18 = (f32[512,128]{1,0:T(8,128)S(1)}, f32[512,128]{1,0:T(8,128)S(1)}, u32[]{:S(2)}, u32[]{:S(2)}) collective-permute-start(f32[512,128]{1,0:T(8,128)S(1)} %pad_maximum_fusion.3.refs_8_), channel_id=1, source_target_pairs={{0,1},{1,0},{2,3},{3,2},{4,5},{5,4},{6,7},{7,6},{8,9},{9,8},{10,11... | collective-permute-start | bytes 786440 | tf_op jit(solution)/shard_map/ppermute | solution.py:299
  53.0 3.3 %collective-permute-start.19 = (f32[512,128]{1,0:T(8,128)S(1)}, f32[512,128]{1,0:T(8,128)S(1)}, u32[]{:S(2)}, u32[]{:S(2)}) collective-permute-start(f32[512,128]{1,0:T(8,128)S(1)} %pad_maximum_fusion.2.refs_10_), channel_id=1, source_target_pairs={{0,1},{1,0},{2,3},{3,2},{4,5},{5,4},{6,7},{7,6},{8,9},{9,8},{10,11... | collective-permute-start | bytes 786440 | tf_op jit(solution)/shard_map/ppermute | solution.py:299
  53.5 3.5 %collective-permute-start.16 = (f32[512,128]{1,0:T(8,128)S(1)}, f32[512,128]{1,0:T(8,128)S(1)}, u32[]{:S(2)}, u32[]{:S(2)}) collective-permute-start(f32[512,128]{1,0:T(8,128)S(1)} %pad_maximum_fusion.4.refs_8_), channel_id=1, source_target_pairs={{0,1},{1,0},{2,3},{3,2},{4,5},{5,4},{6,7},{7,6},{8,9},{9,8},{10,11... | collective-permute-start | bytes 786440 | tf_op jit(solution)/shard_map/ppermute | solution.py:299
  56.2 1.6 %collective-permute-start.17 = (f32[512,128]{1,0:T(8,128)S(1)}, f32[512,128]{1,0:T(8,128)S(1)}, u32[]{:S(2)}, u32[]{:S(2)}) collective-permute-start(f32[512,128]{1,0:T(8,128)S(1)} %pad_maximum_fusion.5.refs_10_), channel_id=1, source_target_pairs={{0,1},{1,0},{2,3},{3,2},{4,5},{5,4},{6,7},{7,6},{8,9},{9,8},{10,11... | collective-permute-start | bytes 786440 | tf_op jit(solution)/shard_map/ppermute | solution.py:299
